TPU v7x, 32 devices: a whole 2x2x4 slice. The times are simulated.
32 devices in a mesh: cal: 8 (over z, y), gr: 4 (over x, core).
Axes of the slice: x: 2, y: 2, z: 4, core: 2. Of those that a mesh axis runs over, the one named last changes fastest.
Arguments:
- features: bfloat16 [16384, 4096], P('cal', 'gr'), may hold values from -6 to 6
- coef: bfloat16 [4096], P('gr'), may hold values from -0.09375 to 0.09375
- log_exposure: float32 [16384], P('cal'), may hold values from -0.7 to 0.7
- claims: float32 [16384], P('cal'), may hold values from 0 to 4
- cluster_id: int32 [16384], P('cal'), may hold values from 0 to 127
- period: int32 [16384], P('cal'), may hold values from 0 to 15, as said below
- period_effect: float32 [16], replicated, may hold values from -0.5 to 0.5
Outputs:
- meat: float32 [4096, 4096], P('cal', 'gr')
Inputs may be any that keep to these rules, and one draw needn't show every extreme that they name: `period`: rows of index d of cal lie in periods d * 2 to (d + 1) * 2 - 1.
All inputs are finite; a program needn't handle non-finite values.
Results may differ from a plain program's by a relative error of at most 0.0044.
Values sent between devices are 32-bit elements; how exact they have to be, the bound alone decides.
No kernel may reach another device: no remote copies, remote signals or barrier semaphores. Data moves between devices by JAX's collectives and lax.ppermute only.
A program may use at most 64 MiB of HBM per device.

v0:
```python
import jax
import jax.numpy as jnp
from jax import lax
from jax.sharding import PartitionSpec as P

CL_DEV = 16


def per_device(features, coef, log_exposure, claims, cluster_id, period, period_effect):
    rows_here = features.shape[0]
    width = features.shape[1]
    n_cal = lax.axis_size("cal")
    clusters = CL_DEV * n_cal
    local_lin = jnp.dot(features, coef, preferred_element_type=jnp.float32)
    linear = lax.psum(local_lin, "gr")
    periods = period_effect.shape[0]
    table = jnp.where(
        period[:, None] == jnp.arange(periods, dtype=jnp.int32)[None, :],
        period_effect[None, :],
        jnp.float32(0.0),
    )
    shift = jnp.sum(table, axis=1)
    resid = (claims - jnp.exp(linear + log_exposure + shift)).astype(jnp.bfloat16)
    block = min(512, rows_here)
    count = rows_here // block
    feats = features.reshape(count, block, width)
    res_b = resid.reshape(count, block)
    ids_b = cluster_id.reshape(count, block)
    cluster_range = jnp.arange(clusters, dtype=jnp.int32)

    def step(carry, item):
        feat_blk, res_blk, id_blk = item
        picks = jnp.where(
            id_blk[:, None] == cluster_range[None, :], res_blk[:, None], jnp.bfloat16(0.0)
        )
        term = lax.dot_general(
            picks, feat_blk, (((0,), (0,)), ((), ())), preferred_element_type=jnp.float32
        )
        return (carry + term, None)

    partial_scores, _ = lax.scan(
        step, jnp.zeros((clusters, width), jnp.float32), (feats, res_b, ids_b)
    )
    owned = lax.psum_scatter(partial_scores, "cal", scatter_dimension=0, tiled=True)
    full_scores = lax.all_gather(owned, "gr", axis=1, tiled=True)
    scale = jnp.float32(1.0) / jnp.float32(rows_here * n_cal)
    my_rows = lax.all_to_all(full_scores, "cal", split_axis=1, concat_axis=0, tiled=True)
    meat_block = lax.dot_general(
        my_rows,
        lax.all_gather(owned, "cal", axis=0, tiled=True),
        (((0,), (0,)), ((), ())),
        precision=lax.Precision.HIGHEST,
        preferred_element_type=jnp.float32,
    )
    return meat_block * scale


def solution(mesh):
    placed = (P("cal", "gr"), P("gr"), P("cal"), P("cal"), P("cal"), P("cal"), P())
    return jax.shard_map(
        per_device, mesh=mesh, in_specs=placed, out_specs=P("cal", "gr"), check_vma=False
    )
```

profile of v0, /device:TPU:0, one launch (start us, length us, event | category | flops | bytes accessed | tf_op | source)
XLA Modules:
  0.0 145.5 jit_solution(7464718148224890148)
XLA Ops:
  6.5 0.0 copy-start.1
  6.5 0.0 copy-start.5
  6.5 0.0 copy-start.2
  6.5 0.0 copy-start.3
  6.5 0.0 copy-start.4
  6.5 0.0 reduce-scatter.2.cloned.1.call-start
  6.6 0.7 reshape.22
  7.3 3.4 %fusion.11 = f32[1,2048]{1,0:T(1,128)S(1)} fusion(bf16[2048,1024]{1,0:T(8,128)(2,1)} %param.9, bf16[1024,1]{0,1:T(2,128)(2,1)S(1)} %reshape.22), kind=kOutput, calls=%fused_computation.18 | convolution fusion | flops 4194304 | bytes 4204544 | tf_op jit(solution)/shard_map/dot_general | solution.py:14
  10.7 8.5 %psum.7 = f32[2048]{0:T(1024)S(1)} all-reduce(f32[2048]{0:T(1024)S(1)} %bitcast.25), channel_id=1, replica_groups=mesh['cal'=8,'gr'=4] {'gr'}, use_global_device_ids=true, to_apply=%region_0.0 | all-reduce | flops 2048 | bytes 16384 | tf_op jit(solution)/shard_map/psum | solution.py:15
  19.2 0.0 copy-done.1
  19.2 0.0 copy-done.5
  19.2 0.0 copy-done.2
  19.2 0.1 select_reduce_fusion
  19.3 0.0 copy-done.3
  19.3 0.0 copy-done.4
  19.3 7.7 %while.11 = (s32[]{:T(128)}, f32[128,1024]{1,0:T(8,128)S(1)}, s32[4,512]{1,0:T(4,128)S(1)}, bf16[4,512]{1,0:T(4,128)(2,1)S(1)}, bf16[4,512,1024]{2,1,0:T(8,128)(2,1)}, /*index=5*/s32[]{:T(128)}, s32[]{:T(128)}) while((s32[]{:T(128)}, f32[128,1024]{1,0:T(8,128)S(1)}, s32[4,512]{1,0:T(4,128)S(1)}, bf16[4,512]{1,0:T(4,128)(2,1)S(1)}, ...), condition=%wide.region_3.4_spmd.clone, body=%wide.region_2.3_spmd.clone.sunk | while | flops 134610944 | bytes 2106475 | solution.py:41
  19.4 1.9 %convolution_add_fusion.2 = f32[128,1024]{1,0:T(8,128)S(1)} fusion(bf16[4,512,1024]{2,1,0:T(8,128)(2,1)} %get-tuple-element.117, s32[]{:T(128)S(6)} %copy.16, f32[128,1024]{1,0:T(8,128)S(1)} %get-tuple-element.107, pred[]{:T(512)S(6)} %compare.3, s32[512]{0:T(512)S(1)} %bitcast.24, bf16[512]{0:T(512)(128)(2,1)S(1)} %dynamic-slice_reduce_fusion.2), kind=kOutput, calls=%fused_computation.1.clone.1 | convolution fusion | flops 134610944 | bytes 2100229 | tf_op jit(solution)/shard_map/while/body/eval_jaxpr/dot_general | solution.py:36
  21.3 1.9 %convolution_add_fusion.2 = f32[128,1024]{1,0:T(8,128)S(1)} fusion(bf16[4,512,1024]{2,1,0:T(8,128)(2,1)} %get-tuple-element.117, s32[]{:T(128)S(6)} %copy.16, f32[128,1024]{1,0:T(8,128)S(1)} %get-tuple-element.107, pred[]{:T(512)S(6)} %compare.3, s32[512]{0:T(512)S(1)} %bitcast.24, bf16[512]{0:T(512)(128)(2,1)S(1)} %dynamic-slice_reduce_fusion.2), kind=kOutput, calls=%fused_computation.1.clone.1 | convolution fusion | flops 134610944 | bytes 2100229 | tf_op jit(solution)/shard_map/while/body/eval_jaxpr/dot_general | solution.py:36
  23.3 1.9 %convolution_add_fusion.2 = f32[128,1024]{1,0:T(8,128)S(1)} fusion(bf16[4,512,1024]{2,1,0:T(8,128)(2,1)} %get-tuple-element.117, s32[]{:T(128)S(6)} %copy.16, f32[128,1024]{1,0:T(8,128)S(1)} %get-tuple-element.107, pred[]{:T(512)S(6)} %compare.3, s32[512]{0:T(512)S(1)} %bitcast.24, bf16[512]{0:T(512)(128)(2,1)S(1)} %dynamic-slice_reduce_fusion.2), kind=kOutput, calls=%fused_computation.1.clone.1 | convolution fusion | flops 134610944 | bytes 2100229 | tf_op jit(solution)/shard_map/while/body/eval_jaxpr/dot_general | solution.py:36
  25.2 1.9 %convolution_add_fusion.2 = f32[128,1024]{1,0:T(8,128)S(1)} fusion(bf16[4,512,1024]{2,1,0:T(8,128)(2,1)} %get-tuple-element.117, s32[]{:T(128)S(6)} %copy.16, f32[128,1024]{1,0:T(8,128)S(1)} %get-tuple-element.107, pred[]{:T(512)S(6)} %compare.3, s32[512]{0:T(512)S(1)} %bitcast.24, bf16[512]{0:T(512)(128)(2,1)S(1)} %dynamic-slice_reduce_fusion.2), kind=kOutput, calls=%fused_computation.1.clone.1 | convolution fusion | flops 134610944 | bytes 2100229 | tf_op jit(solution)/shard_map/while/body/eval_jaxpr/dot_general | solution.py:36
  27.1 0.0 copy-start
  27.1 0.8 copy-done
  27.9 0.0 reduce-scatter.2.cloned.1.call-update
  27.9 62.8 %reduce-scatter.2.cloned.1.call-done = f32[16,1024]{1,0:T(8,128)} async-done(((f32[128,1024]{1,0:T(8,128)}), f32[16,1024]{1,0:T(8,128)}) %reduce-scatter.2.cloned.1.call-update) | async-done | bytes 65552 | tf_op jit(solution)/shard_map/reduce_scatter | solution.py:44
  90.7 6.0 %all_gather.6 = f32[16,4096]{1,0:T(8,128)S(1)} all-gather(f32[16,1024]{1,0:T(8,128)} %reduce-scatter.2.cloned.1.call-done), channel_id=1, replica_groups=mesh['cal'=8,'gr'=4] {'gr'}, dimensions={1}, use_global_device_ids=true | all-gather | bytes 327680 | tf_op jit(solution)/shard_map/all_gather | solution.py:45
  96.7 0.7 copy.13
  97.4 3.6 %all-to-all-start = ((f32[16,8,512]{2,0,1:T(8,128)}), f32[16,8,512]{2,0,1:T(8,128)S(1)}, u32[]{:S(2)}, u32[]{:S(2)}) async-start(f32[16,8,512]{2,0,1:T(8,128)} %bitcast.16), calls=%async_computation.1 | async-start | bytes 524288 | tf_op jit(solution)/shard_map/all_to_all | solution.py:47
  101.0 34.5 %all_gather.7 = f32[128,1024]{1,0:T(8,128)S(1)} all-gather(f32[16,1024]{1,0:T(8,128)} %reduce-scatter.2.cloned.1.call-done), channel_id=1, replica_groups=mesh['cal'=8,'gr'=4] {'cal'}, dimensions={0}, use_global_device_ids=true | all-gather | bytes 589824 | tf_op jit(solution)/shard_map/all_gather | solution.py:50
  135.5 0.0 all-to-all-done
  135.5 3.2 %convolution_multiply_fusion = f32[512,1024]{1,0:T(8,128)} fusion(f32[128,512]{1,0:T(8,128)S(1)} %bitcast.23, f32[128,1024]{1,0:T(8,128)S(1)} %all_gather.7), kind=kOutput, calls=%fused_computation.13 | convolution fusion | flops 805830656 | bytes 2883584 | tf_op jit(solution)/shard_map/dot_general | solution.py:48
  (12 shorter events, 0.2 us)
Async XLA Ops:
  6.5 12.6 %copy-start.1 = (s32[2048]{0:T(1024)S(1)}, s32[2048]{0:T(1024)}, u32[]{:S(2)}) copy-start(s32[2048]{0:T(1024)} %param.13) | copy-start | bytes 24580
  6.5 12.6 %copy-start.5 = (f32[16]{0:T(128)S(1)}, f32[16]{0:T(128)}, u32[]{:S(2)}) copy-start(f32[16]{0:T(128)} %param.15) | copy-start | bytes 196
  6.5 12.6 %copy-start.2 = (s32[2048]{0:T(1024)S(1)}, s32[2048]{0:T(1024)}, u32[]{:S(2)}) copy-start(s32[2048]{0:T(1024)} %param.14) | copy-start | bytes 24580
  6.5 12.8 %copy-start.3 = (f32[2048]{0:T(1024)S(1)}, f32[2048]{0:T(1024)}, u32[]{:S(2)}) copy-start(f32[2048]{0:T(1024)} %param.12) | copy-start | bytes 24580
  6.5 12.8 %copy-start.4 = (f32[2048]{0:T(1024)S(1)}, f32[2048]{0:T(1024)}, u32[]{:S(2)}) copy-start(f32[2048]{0:T(1024)} %param.11) | copy-start | bytes 24580
  6.5 84.1 %reduce-scatter.2.cloned.1.call-start = ((), (), s32[]{:S(2)}) async-start(), calls=%async_computation.2 | async-start | bytes 589824 | tf_op jit(solution)/shard_map/reduce_scatter | solution.py:44
  27.1 0.8 copy-start
  97.4 38.1 %all-to-all-start = ((f32[16,8,512]{2,0,1:T(8,128)}), f32[16,8,512]{2,0,1:T(8,128)S(1)}, u32[]{:S(2)}, u32[]{:S(2)}) async-start(f32[16,8,512]{2,0,1:T(8,128)} %bitcast.16), calls=%async_computation.1 | async-start | bytes 524288 | tf_op jit(solution)/shard_map/all_to_all | solution.py:47
Sparse Core Ops, SparseCore 0:
  28.0 62.6 reduce-scatter.1
where the time goes:
time: 146 us
  waiting for transfers between devices  62.8 us (43%)
  blocking collectives  49 us (34%)
  matrix products  14 us (10%)
  between operations  13.5 us (9%)
  starting transfers between devices  3.65 us (2%)
  local copies, waits for them, and re-layouts  2.37 us (2%)
    reduce_scatter x1, waiting for transfers between devices, per_device(): lax.psum_scatter(partial_scores, 'cal', scatter_dimension=0, tiled=True)  62.8 us
    all_gather x1, blocking collectives, per_device(): lax.all_gather(owned, 'cal', axis=0, tiled=True)  34.5 us
    psum x1, blocking collectives, per_device(): linear = lax.psum(local_lin, 'gr')  8.48 us
    dot_general x4, matrix products, step(): lax.dot_general(picks, feat_blk, (((0,), (0,)), ((), ())), preferred_elem...  7.46 us
    all_gather x1, blocking collectives, per_device(): full_scores = lax.all_gather(owned, 'gr', axis=1, tiled=True)  5.98 us
    all_to_all x1, starting transfers between devices, per_device(): lax.all_to_all(full_scores, 'cal', split_axis=1, concat_axis=0, tiled=True)  3.61 us
    dot_general x1, matrix products, per_device(): local_lin = jnp.dot(features, coef, preferred_element_type=jnp.float32)  3.37 us
    dot_general x1, matrix products, per_device(): lax.dot_general(my_rows, lax.all_gather(owned, 'cal', axis=0, tiled=True)...  3.16 us
  transfers between devices with their start and end apart: 2, of which 1 were waited for; matrix products, arithmetic and copies ran while one was open for 0% of the time, Pallas kernels for 0%

commit v1 on v0

v1 whole, which is shorter than its diff:
```python
import functools

import jax
import jax.numpy as jnp
from jax import lax
from jax.experimental import pallas as pl
from jax.experimental.pallas import tpu as pltpu
from jax.sharding import PartitionSpec as P

CL_DEV = 16
AXES = ("cal", "gr")
VMEM = pl.BlockSpec(memory_space=pltpu.VMEM)
SMEM = pl.BlockSpec(memory_space=pltpu.SMEM)
ANY = pl.BlockSpec(memory_space=pl.ANY)
LIMIT = 40 * 1024 * 1024


def split_two(value):
    high = value.astype(jnp.bfloat16)
    low = (value - high.astype(jnp.float32)).astype(jnp.bfloat16)
    return high, low


def linear_kernel(pieces, feats, coef, lin, held, sems):
    rows = held.shape[0] // pieces
    copies = []
    for i in range(pieces):
        part = pl.ds(i * rows, rows)
        copies.append(pltpu.make_async_copy(feats.at[part], held.at[part], sems.at[i]))
        copies[-1].start()
    weights = jnp.broadcast_to(coef[...], (16, coef.shape[1]))
    for i in range(pieces):
        copies[i].wait()
        out = lax.dot_general(
            weights,
            held[i * rows : (i + 1) * rows, :],
            (((1,), (1,)), ((), ())),
            preferred_element_type=jnp.float32,
        )
        lin[:, i * rows : (i + 1) * rows] = out[0:1]


def linear_call(features, coef):
    rows, width = features.shape
    pieces = 8
    return pl.pallas_call(
        functools.partial(linear_kernel, pieces),
        out_shape=(
            jax.ShapeDtypeStruct((1, rows), jnp.float32),
            jax.ShapeDtypeStruct((rows, width), features.dtype),
        ),
        in_specs=[ANY, VMEM],
        out_specs=(VMEM, VMEM),
        scratch_shapes=[pltpu.SemaphoreType.DMA((pieces,))],
        compiler_params=pltpu.CompilerParams(vmem_limit_bytes=LIMIT),
        cost_estimate=pl.CostEstimate(
            flops=2 * rows * width, bytes_accessed=2 * rows * width, transcendentals=0
        ),
        name="linear",
    )(features, coef)


def picks_kernel(first, where, effect, lin_a, lin_b, exposure, claims, ids, period, held, out, picks):
    base = where[0]
    shift = jnp.zeros(lin_a.shape, jnp.float32)
    for k in range(first):
        shift = jnp.where(period[...] == base + k, effect[base + k], shift)
    linear = lin_a[...] + lin_b[...]
    resid = claims[...] - jnp.exp(linear + exposure[...] + shift)
    clusters, rows = picks.shape
    resid = resid.astype(jnp.bfloat16).astype(jnp.float32)
    cluster = lax.broadcasted_iota(jnp.int32, (clusters, rows), 0)
    picks[...] = jnp.where(cluster == ids[...], resid, 0.0).astype(jnp.bfloat16)
    half = out.shape[1]
    columns = pl.ds(pl.multiple_of(where[1] * half, half), half)
    out[...] = jnp.dot(picks[...], held[:, columns], preferred_element_type=jnp.float32)


def keep_kernel(where, picks, held, out):
    half = out.shape[1]
    columns = pl.ds(pl.multiple_of(where[0] * half, half), half)
    out[...] = jnp.dot(picks[...], held[:, columns], preferred_element_type=jnp.float32)


def meat_kernel(scale, where, own_rows, near_rows, far_rows, own, other, out):
    mode = where[0]
    rows = jnp.where(mode == 0, own_rows[...], jnp.where(mode == 1, near_rows[...], far_rows[...]))
    left_high, left_low = split_two(rows)
    left = jnp.concatenate([left_high, left_low], axis=0)
    half = own.shape[1]
    for k, part in enumerate((own, other)):
        high, low = split_two(part[...])
        dims = (((0,), (0,)), ((), ()))
        total = lax.dot_general(
            left, jnp.concatenate([high, high], axis=0), dims, preferred_element_type=jnp.float32
        ) + lax.dot_general(left_high, low, dims, preferred_element_type=jnp.float32)
        spot = where[1] if k == 0 else 1 - where[1]
        out[:, pl.ds(pl.multiple_of(spot * half, half), half)] = total * scale


def exchange(value, cal_bits, gr_bits, n_cal, n_gr):
    pairs = [
        (c * n_gr + g, (c ^ cal_bits) * n_gr + (g ^ gr_bits))
        for c in range(n_cal)
        for g in range(n_gr)
    ]
    return lax.ppermute(value, AXES, pairs)


def per_device(features, coef, log_exposure, claims, cluster_id, period, period_effect):
    rows, width = features.shape
    n_cal, n_gr = lax.axis_size("cal"), lax.axis_size("gr")
    clusters = CL_DEV * n_cal
    per_dev = period_effect.shape[0] // n_cal
    fan = n_cal // n_gr
    cal, gr = lax.axis_index("cal"), lax.axis_index("gr")
    high, low = cal // fan, cal % fan
    swap = functools.partial(exchange, n_cal=n_cal, n_gr=n_gr)

    lin, held = linear_call(features, coef.reshape(1, width))
    bits = 1
    while bits < n_gr // 2:
        lin = lin + swap(lin, 0, bits)
        bits *= 2
    lin_far = swap(lin, 0, bits)

    half = width // 2
    top = low // (fan // 2)
    flat = [v.reshape(1, rows) for v in (log_exposure, claims, cluster_id, period)]
    send, picks = pl.pallas_call(
        functools.partial(picks_kernel, per_dev),
        out_shape=(
            jax.ShapeDtypeStruct((clusters, half), jnp.float32),
            jax.ShapeDtypeStruct((clusters, rows), jnp.bfloat16),
        ),
        in_specs=[SMEM, SMEM] + [VMEM] * 7,
        out_specs=(VMEM, VMEM),
        compiler_params=pltpu.CompilerParams(vmem_limit_bytes=LIMIT),
        cost_estimate=pl.CostEstimate(
            flops=2 * rows * clusters * half, bytes_accessed=rows * width, transcendentals=rows
        ),
        name="send_half",
    )(
        jnp.stack([cal * per_dev, 1 - top]).astype(jnp.int32),
        period_effect, lin, lin_far, *flat, held,
    )
    there = swap(send, fan // 2, 0)
    keep = pl.pallas_call(
        keep_kernel,
        out_shape=jax.ShapeDtypeStruct((clusters, half), jnp.float32),
        in_specs=[SMEM, VMEM, VMEM],
        out_specs=VMEM,
        compiler_params=pltpu.CompilerParams(vmem_limit_bytes=LIMIT),
        cost_estimate=pl.CostEstimate(
            flops=2 * rows * clusters * half, bytes_accessed=rows * width, transcendentals=0
        ),
        name="keep_half",
    )(top.astype(jnp.int32).reshape(1), picks, held)
    part = keep + there
    bits = fan // 4
    while bits:
        size = part.shape[1] // 2
        mine = (low // bits) % 2
        away = lax.dynamic_slice_in_dim(part, (1 - mine) * size, size, axis=1)
        part = lax.dynamic_slice_in_dim(part, mine * size, size, axis=1) + swap(away, bits, 0)
        bits //= 2

    group = clusters // n_gr
    owned = lax.dynamic_slice_in_dim(part, high * group, group, axis=0)
    arrived = []
    for k in range(n_gr - 1, 0, -1):
        piece = lax.dynamic_slice_in_dim(part, (high ^ k) * group, group, axis=0)
        arrived.append(swap(piece, k * fan, 0))
    for piece in arrived:
        owned = owned + piece
    gathered = [swap(owned, k * fan, 0) for k in range(n_gr - 1, 0, -1)]
    block = jnp.concatenate([owned] + gathered[::-1], axis=0)

    side = block
    bits = 1
    while bits < fan // 2:
        mine = (low // bits) % 2
        away = swap(side, bits, 0)
        side = jnp.where(
            mine == 0, jnp.concatenate([side, away], axis=1), jnp.concatenate([away, side], axis=1)
        )
        bits *= 2
    other = swap(side, fan // 2, 0)

    turn = gr ^ high
    have = block
    bits = n_gr // 2
    reach = 0
    near = block
    while bits:
        pairs = []
        for c in range(n_cal):
            for g in range(n_gr):
                if ((g ^ (c // fan)) & ~reach) == 0:
                    pairs.append((c * n_gr + g, c * n_gr + (g ^ bits)))
        got = lax.ppermute(have, AXES, pairs)
        reach |= bits
        if bits == 1:
            near, far = have, got
        else:
            have = jnp.where((turn & bits) != 0, got, have)
        bits //= 2
    mode = jnp.where((turn & 1) != 0, 2, 1)
    scale = 1.0 / (rows * n_cal)
    return pl.pallas_call(
        functools.partial(meat_kernel, scale),
        out_shape=jax.ShapeDtypeStruct((block.shape[1], width), jnp.float32),
        in_specs=[SMEM] + [VMEM] * 5,
        out_specs=VMEM,
        compiler_params=pltpu.CompilerParams(vmem_limit_bytes=LIMIT),
        name="meat",
    )(jnp.stack([mode, top]).astype(jnp.int32), block, near, far, side, other)


def solution(mesh):
    placed = (P("cal", "gr"), P("gr"), P("cal"), P("cal"), P("cal"), P("cal"), P())
    return jax.shard_map(
        per_device, mesh=mesh, in_specs=placed, out_specs=P("cal", "gr"), check_vma=False
    )
```

time: 146 us -> 55.9 us (0.38)
  blocking collectives: 49 us -> 0 us
  waiting for transfers between devices: 62.8 us -> 17.7 us
  starting transfers between devices: 3.65 us -> 20.7 us
  matrix products: 14 us -> 0 us
  between operations: 13.5 us -> 0.14 us
  Pallas kernels: 0 us -> 7.6 us
  local copies, waits for them, and re-layouts: 2.37 us -> 9.23 us
    reduce_scatter x1 -> x0, waiting for transfers between devices: 62.8 us -> none  [per_device(): lax.psum_scatter(partial_scores, 'cal', scatter_dimension=0, tiled=True)]
    all_gather x2 -> x0, blocking collectives: 40.5 us -> none  [the longest x1 34.5 us: per_device(): lax.all_gather(owned, 'cal', axis=0, tiled=True)]
    ppermute x0 -> x12, starting transfers between devices: none -> 20.7 us  [the longest x10 15.9 us: exchange(): return lax.ppermute(value, AXES, pairs)]
    ppermute x0 -> x12, waiting for transfers between devices: none -> 17.7 us  [the longest x10 15.4 us: exchange(): return lax.ppermute(value, AXES, pairs)]
    dot_general x6 -> x0, matrix products: 14 us -> none  [the longest x4 7.46 us: step(): lax.dot_general(picks, feat_blk, (((0,), (0,)), ((), ())), preferred_elem...]
    psum x1 -> x0, blocking collectives: 8.48 us -> none  [per_device(): linear = lax.psum(local_lin, 'gr')]
    pallas_call x0 -> x4, Pallas kernels: none -> 7.6 us  [the longest x1 3.49 us: linear_call(): pl.pallas_call(functools.partial(linear_kernel, pieces), out_shape=(jax.S...]
    unnamed x13 -> x18, local copies, waits for them, and re-layouts: 1.5 us -> 8.5 us
  transfers between devices with their start and end apart: 2 -> 12, of which waited for: 1 -> 9; matrix products, arithmetic and copies ran while one was open for 0% -> 0% of each run, Pallas kernels for 0% -> 1%
where the time goes in v1:
time: 55.9 us; the launch traced here: 55.6 us
  starting transfers between devices  20.7 us (37%)
  waiting for transfers between devices  17.7 us (32%)
  local copies, waits for them, and re-layouts  9.23 us (17%)
  Pallas kernels  7.6 us (14%)
    ppermute x10, starting transfers between devices, exchange(): return lax.ppermute(value, AXES, pairs)  15.9 us
    ppermute x10, waiting for transfers between devices, exchange(): return lax.ppermute(value, AXES, pairs)  15.4 us
    unnamed x18, local copies, waits for them, and re-layouts  8.5 us
    ppermute x2, starting transfers between devices, per_device(): got = lax.ppermute(have, AXES, pairs)  4.74 us
    pallas_call x1, Pallas kernels, linear_call(): pl.pallas_call(functools.partial(linear_kernel, pieces), out_shape=(jax.S...  3.49 us
    pallas_call x1, Pallas kernels, per_device(): pl.pallas_call(functools.partial(meat_kernel, scale), out_shape=jax.Shape...  2.62 us
    ppermute x2, waiting for transfers between devices, per_device(): got = lax.ppermute(have, AXES, pairs)  2.26 us
  transfers between devices with their start and end apart: 12, of which 9 were waited for; matrix products, arithmetic and copies ran while one was open for 0% of the time, Pallas kernels for 1%

profile of v1, /device:TPU:0, one launch (start us, length us, event | category | flops | bytes accessed | tf_op | source)
XLA Modules:
  0.0 55.6 jit_solution(18236143033106583135)
XLA Ops:
  0.0 0.0 copy-start.8
  0.0 0.7 %reshape.16.coef = bf16[1,1024]{1,0:T(2,128)(2,1)S(1)} reshape(bf16[1024]{0:T(1024)(128)(2,1)} %param.8) | data formatting | bytes 4096 | tf_op jit(solution)/shard_map/reshape | solution.py:120
  0.7 0.0 copy-start.3
  0.7 2.2 %copy-done.3 = bf16[2048,1024]{1,0:T(8,128)(2,1)S(1)} copy-done((bf16[2048,1024]{1,0:T(8,128)(2,1)S(1)}, bf16[2048,1024]{1,0:T(8,128)(2,1)}, u32[]{:S(2)}) %copy-start.3) | copy-done | bytes 4194328
  2.9 0.0 copy-start.4
  2.9 0.0 copy-start.5
  2.9 0.0 copy-start.6
  2.9 0.0 copy-start.7
  2.9 3.5 %linear.1 = (f32[1,2048]{1,0:T(1,128)S(1)}, bf16[2048,1024]{1,0:T(8,128)(2,1)S(1)}) custom-call(bf16[2048,1024]{1,0:T(8,128)(2,1)S(1)} %copy-done.3, bf16[1,1024]{1,0:T(2,128)(2,1)S(1)} %reshape.16.coef), custom_call_target="tpu_custom_call" | custom-call | flops 4194304 | bytes 4194304 | tf_op jit(solution)/shard_map/linear/pallas_call | solution.py:46
  6.4 0.0 copy-start
  6.4 1.9 %copy-done = bf16[2048,1024]{1,0:T(8,128)(2,1)} copy-done((bf16[2048,1024]{1,0:T(8,128)(2,1)}, bf16[2048,1024]{1,0:T(8,128)(2,1)S(1)}, u32[]{:S(2)}) %copy-start) | copy-done | bytes 4194328
  8.3 0.5 collective-permute-start
  8.8 0.8 %collective-permute-done = f32[1,2048]{1,0:T(1,128)S(1)} collective-permute-done((f32[1,2048]{1,0:T(1,128)S(1)}, f32[1,2048]{1,0:T(1,128)S(1)}, u32[]{:S(2)}, u32[]{:S(2)}) %collective-permute-start) | collective-permute-done | bytes 8224 | tf_op jit(solution)/shard_map/ppermute | solution.py:107
  9.6 2.9 %collective-permute-start.1 = (f32[1,2048]{1,0:T(1,128)S(1)}, f32[1,2048]{1,0:T(1,128)S(1)}, u32[]{:S(2)}, u32[]{:S(2)}) collective-permute-start(f32[1,2048]{1,0:T(1,128)S(1)} %add.34.lin_a), channel_id=1, source_target_pairs={{0,2},{1,3},{2,0},{3,1},{4,6},{5,7},{6,4},{7,5},{8,10},{9,11},{10,... | collective-permute-start | bytes 24584 | tf_op jit(solution)/shard_map/ppermute | solution.py:107
  12.5 0.1 pad_add_fusion.1.where
  12.6 1.6 %collective-permute-done.1.lin_b = f32[1,2048]{1,0:T(1,128)S(1)} collective-permute-done((f32[1,2048]{1,0:T(1,128)S(1)}, f32[1,2048]{1,0:T(1,128)S(1)}, u32[]{:S(2)}, u32[]{:S(2)}) %collective-permute-start.1) | collective-permute-done | bytes 8224 | tf_op jit(solution)/shard_map/ppermute | solution.py:107
  14.2 0.0 copy-done.8
  14.2 0.0 copy-done.4
  14.2 0.0 copy-done.5
  14.2 0.0 copy-done.6
  14.2 0.0 copy-done.7
  14.2 0.0 copy-start.1
  14.2 2.2 %copy-done.1 = bf16[2048,1024]{1,0:T(8,128)(2,1)S(1)} copy-done((bf16[2048,1024]{1,0:T(8,128)(2,1)S(1)}, bf16[2048,1024]{1,0:T(8,128)(2,1)}, u32[]{:S(2)}) %copy-start.1) | copy-done | bytes 4194328
  16.4 1.0 %send_half.1 = (f32[128,512]{1,0:T(8,128)S(1)}, bf16[128,2048]{1,0:T(8,128)(2,1)S(1)}) custom-call(s32[2]{0:T(128)S(1)} %pad_add_fusion.1.where, f32[16]{0:T(128)S(1)} %copy-done.8, f32[1,2048]{1,0:T(1,128)S(1)} %add.34.lin_a, f32[1,2048]{1,0:T(1,128)S(1)} %collective-permute-done.1.lin_b, f32[1,2048]{1,0:T(1,128)S(1)} %bitcast.8, f32[1,2048]{1,0:T(1,128)S(1)} %bitcast.9, ...), custom_call_target="tpu_custom_call" | custom-call | flops 268435456 | bytes 2097152 | tf_op jit(solution)/shard_map/send_half/pallas_call | solution.py:130
  17.4 2.1 %collective-permute-start.2 = (f32[128,512]{1,0:T(8,128)S(1)}, f32[128,512]{1,0:T(8,128)S(1)}, u32[]{:S(2)}, u32[]{:S(2)}) collective-permute-start(f32[128,512]{1,0:T(8,128)S(1)} %get-tuple-element.12), channel_id=1, source_target_pairs={{0,4},{1,5},{2,6},{3,7},{4,0},{5,1},{6,2},{7,3},{8,12},{9,13},{10,... | collective-permute-start | bytes 786440 | tf_op jit(solution)/shard_map/ppermute | solution.py:107
  19.5 0.0 copy-start.2
  19.5 2.2 %copy-done.2 = bf16[2048,1024]{1,0:T(8,128)(2,1)S(1)} copy-done((bf16[2048,1024]{1,0:T(8,128)(2,1)S(1)}, bf16[2048,1024]{1,0:T(8,128)(2,1)}, u32[]{:S(2)}) %copy-start.2) | copy-done | bytes 4194328
  21.7 0.4 keep_half.1
  22.2 2.9 %collective-permute-done.2 = f32[128,512]{1,0:T(8,128)S(1)} collective-permute-done((f32[128,512]{1,0:T(8,128)S(1)}, f32[128,512]{1,0:T(8,128)S(1)}, u32[]{:S(2)}, u32[]{:S(2)}) %collective-permute-start.2) | collective-permute-done | bytes 262176 | tf_op jit(solution)/shard_map/ppermute | solution.py:107
  25.1 1.9 %collective-permute-start.5 = (f32[32,512]{1,0:T(8,128)S(1)}, f32[32,512]{1,0:T(8,128)S(1)}, u32[]{:S(2)}, u32[]{:S(2)}) collective-permute-start(f32[32,512]{1,0:T(8,128)S(1)} %get-tuple-element.14), channel_id=1, source_target_pairs={{0,8},{1,9},{2,10},{3,11},{4,12},{5,13},{6,14},{7,15},{8,0},{9,1},... | collective-permute-start | bytes 196616 | tf_op jit(solution)/shard_map/ppermute | solution.py:107
  27.0 2.6 %collective-permute-start.4 = (f32[32,512]{1,0:T(8,128)S(1)}, f32[32,512]{1,0:T(8,128)S(1)}, u32[]{:S(2)}, u32[]{:S(2)}) collective-permute-start(f32[32,512]{1,0:T(8,128)S(1)} %get-tuple-element.15), channel_id=1, source_target_pairs={{0,16},{1,17},{2,18},{3,19},{4,20},{5,21},{6,22},{7,23},{8,24},{9,... | collective-permute-start | bytes 196616 | tf_op jit(solution)/shard_map/ppermute | solution.py:107
  29.5 0.0 collective-permute-start.3
  29.6 0.0 collective-permute-done.5
  29.6 4.1 %collective-permute-done.4 = f32[32,512]{1,0:T(8,128)S(1)} collective-permute-done((f32[32,512]{1,0:T(8,128)S(1)}, f32[32,512]{1,0:T(8,128)S(1)}, u32[]{:S(2)}, u32[]{:S(2)}) %collective-permute-start.4) | collective-permute-done | bytes 65568 | tf_op jit(solution)/shard_map/ppermute | solution.py:107
  33.7 2.0 %collective-permute-done.3 = f32[32,512]{1,0:T(8,128)S(1)} collective-permute-done((f32[32,512]{1,0:T(8,128)S(1)}, f32[32,512]{1,0:T(8,128)S(1)}, u32[]{:S(2)}, u32[]{:S(2)}) %collective-permute-start.3) | collective-permute-done | bytes 65568 | tf_op jit(solution)/shard_map/ppermute | solution.py:107
  35.7 0.8 %collective-permute-start.8 = (f32[32,512]{1,0:T(8,128)S(1)}, f32[32,512]{1,0:T(8,128)S(1)}, u32[]{:S(2)}, u32[]{:S(2)}) collective-permute-start(f32[32,512]{1,0:T(8,128)S(1)} %add_add_fusion), channel_id=1, source_target_pairs={{0,24},{1,25},{2,26},{3,27},{4,28},{5,29},{6,30},{7,31},{8,16},{9,... | collective-permute-start | bytes 196616 | tf_op jit(solution)/shard_map/ppermute | solution.py:107
  36.5 0.6 %collective-permute-start.7 = (f32[32,512]{1,0:T(8,128)S(1)}, f32[32,512]{1,0:T(8,128)S(1)}, u32[]{:S(2)}, u32[]{:S(2)}) collective-permute-start(f32[32,512]{1,0:T(8,128)S(1)} %add_add_fusion), channel_id=1, source_target_pairs={{0,16},{1,17},{2,18},{3,19},{4,20},{5,21},{6,22},{7,23},{8,24},{9,... | collective-permute-start | bytes 196616 | tf_op jit(solution)/shard_map/ppermute | solution.py:107
  37.1 3.1 %collective-permute-start.6 = (f32[32,512]{1,0:T(8,128)S(1)}, f32[32,512]{1,0:T(8,128)S(1)}, u32[]{:S(2)}, u32[]{:S(2)}) collective-permute-start(f32[32,512]{1,0:T(8,128)S(1)} %add_add_fusion), channel_id=1, source_target_pairs={{0,8},{1,9},{2,10},{3,11},{4,12},{5,13},{6,14},{7,15},{8,0},{9,1},... | collective-permute-start | bytes 196616 | tf_op jit(solution)/shard_map/ppermute | solution.py:107
  40.1 1.8 %collective-permute-done.8 = f32[32,512]{1,0:T(8,128)S(1)} collective-permute-done((f32[32,512]{1,0:T(8,128)S(1)}, f32[32,512]{1,0:T(8,128)S(1)}, u32[]{:S(2)}, u32[]{:S(2)}) %collective-permute-start.8) | collective-permute-done | bytes 65568 | tf_op jit(solution)/shard_map/ppermute | solution.py:107
  41.9 1.2 %collective-permute-done.7 = f32[32,512]{1,0:T(8,128)S(1)} collective-permute-done((f32[32,512]{1,0:T(8,128)S(1)}, f32[32,512]{1,0:T(8,128)S(1)}, u32[]{:S(2)}, u32[]{:S(2)}) %collective-permute-start.7) | collective-permute-done | bytes 65568 | tf_op jit(solution)/shard_map/ppermute | solution.py:107
  43.1 0.0 collective-permute-done.6
  43.1 3.4 %collective-permute-start.9 = (f32[128,512]{1,0:T(8,128)S(1)}, f32[128,512]{1,0:T(8,128)S(1)}, u32[]{:S(2)}, u32[]{:S(2)}) collective-permute-start(f32[128,512]{1,0:T(8,128)S(1)} %pad_maximum_fusion.own_rows.own), channel_id=1, source_target_pairs={{0,2},{4,6},{9,11},{13,15},{18,16},{22,20},{27,25},{31,29}} | collective-permute-start | bytes 786440 | tf_op jit(solution)/shard_map/ppermute | solution.py:201
  46.6 1.6 %collective-permute-start.11 = (f32[128,512]{1,0:T(8,128)S(1)}, f32[128,512]{1,0:T(8,128)S(1)}, u32[]{:S(2)}, u32[]{:S(2)}) collective-permute-start(f32[128,512]{1,0:T(8,128)S(1)} %pad_maximum_fusion.own_rows.own), channel_id=1, source_target_pairs={{0,4},{1,5},{2,6},{3,7},{4,0},{5,1},{6,2},{7,3},{8,12},{9,13},{10,... | collective-permute-start | bytes 786440 | tf_op jit(solution)/shard_map/ppermute | solution.py:107
  48.1 2.3 %collective-permute-done.9 = f32[128,512]{1,0:T(8,128)S(1)} collective-permute-done((f32[128,512]{1,0:T(8,128)S(1)}, f32[128,512]{1,0:T(8,128)S(1)}, u32[]{:S(2)}, u32[]{:S(2)}) %collective-permute-start.9) | collective-permute-done | bytes 262176 | tf_op jit(solution)/shard_map/ppermute | solution.py:201
  50.4 1.3 %collective-permute-start.10 = (f32[128,512]{1,0:T(8,128)S(1)}, f32[128,512]{1,0:T(8,128)S(1)}, u32[]{:S(2)}, u32[]{:S(2)}) collective-permute-start(f32[128,512]{1,0:T(8,128)S(1)} %broadcast_select_fusion.near_rows), channel_id=1, source_target_pairs={{0,1},{2,3},{4,5},{6,7},{9,8},{11,10},{13,12},{15,14},{16,17},{18,... | collective-permute-start | bytes 786440 | tf_op jit(solution)/shard_map/ppermute | solution.py:201
  51.8 0.1 pad_add_fusion.where
  51.8 1.2 %collective-permute-done.11.other = f32[128,512]{1,0:T(8,128)S(1)} collective-permute-done((f32[128,512]{1,0:T(8,128)S(1)}, f32[128,512]{1,0:T(8,128)S(1)}, u32[]{:S(2)}, u32[]{:S(2)}) %collective-permute-start.11) | collective-permute-done | bytes 262176 | tf_op jit(solution)/shard_map/ppermute | solution.py:107
  53.0 0.0 collective-permute-done.10.far_rows
  53.0 2.6 %meat.1 = f32[512,1024]{1,0:T(8,128)} custom-call(s32[2]{0:T(128)S(1)} %pad_add_fusion.where, f32[128,512]{1,0:T(8,128)S(1)} %pad_maximum_fusion.own_rows.own, f32[128,512]{1,0:T(8,128)S(1)} %broadcast_select_fusion.near_rows, f32[128,512]{1,0:T(8,128)S(1)} %collective-permute-done.10.far_rows, f32[128,512]{1,0:T(8,128)S(1)} %pad_maximum_fusion.own_rows.own, ...), custom_call_target="tpu_custom_call" | custom-call | tf_op jit(solution)/shard_map/meat/pallas_call | solution.py:210
  (6 shorter events, 0.1 us)
Async XLA Ops:
  0.0 14.2 %copy-start.8 = (f32[16]{0:T(128)S(1)}, f32[16]{0:T(128)}, u32[]{:S(2)}) copy-start(f32[16]{0:T(128)} %effect.1) | copy-start | bytes 196
  0.7 2.2 %copy-start.3 = (bf16[2048,1024]{1,0:T(8,128)(2,1)S(1)}, bf16[2048,1024]{1,0:T(8,128)(2,1)}, u32[]{:S(2)}) copy-start(bf16[2048,1024]{1,0:T(8,128)(2,1)} %feats.1) | copy-start | bytes 12582916
  2.9 11.3 %copy-start.4 = (f32[2048]{0:T(1024)S(1)}, f32[2048]{0:T(1024)}, u32[]{:S(2)}) copy-start(f32[2048]{0:T(1024)} %param.9) | copy-start | bytes 24580
  2.9 11.3 %copy-start.5 = (f32[2048]{0:T(1024)S(1)}, f32[2048]{0:T(1024)}, u32[]{:S(2)}) copy-start(f32[2048]{0:T(1024)} %param.10) | copy-start | bytes 24580
  2.9 11.3 %copy-start.6 = (s32[2048]{0:T(1024)S(1)}, s32[2048]{0:T(1024)}, u32[]{:S(2)}) copy-start(s32[2048]{0:T(1024)} %param.11) | copy-start | bytes 24580
  2.9 11.3 %copy-start.7 = (s32[2048]{0:T(1024)S(1)}, s32[2048]{0:T(1024)}, u32[]{:S(2)}) copy-start(s32[2048]{0:T(1024)} %param.12) | copy-start | bytes 24580
  6.4 1.9 %copy-start = (bf16[2048,1024]{1,0:T(8,128)(2,1)}, bf16[2048,1024]{1,0:T(8,128)(2,1)S(1)}, u32[]{:S(2)}) copy-start(bf16[2048,1024]{1,0:T(8,128)(2,1)S(1)} %get-tuple-element.10.held) | copy-start | bytes 12582916
  8.3 1.3 %collective-permute-start = (f32[1,2048]{1,0:T(1,128)S(1)}, f32[1,2048]{1,0:T(1,128)S(1)}, u32[]{:S(2)}, u32[]{:S(2)}) collective-permute-start(f32[1,2048]{1,0:T(1,128)S(1)} %get-tuple-element.9), channel_id=1, source_target_pairs={{0,1},{1,0},{2,3},{3,2},{4,5},{5,4},{6,7},{7,6},{8,9},{9,8},{10,11... | collective-permute-start | bytes 24584 | tf_op jit(solution)/shard_map/ppermute | solution.py:107
  9.6 4.5 %collective-permute-start.1 = (f32[1,2048]{1,0:T(1,128)S(1)}, f32[1,2048]{1,0:T(1,128)S(1)}, u32[]{:S(2)}, u32[]{:S(2)}) collective-permute-start(f32[1,2048]{1,0:T(1,128)S(1)} %add.34.lin_a), channel_id=1, source_target_pairs={{0,2},{1,3},{2,0},{3,1},{4,6},{5,7},{6,4},{7,5},{8,10},{9,11},{10,... | collective-permute-start | bytes 24584 | tf_op jit(solution)/shard_map/ppermute | solution.py:107
  14.2 2.2 %copy-start.1 = (bf16[2048,1024]{1,0:T(8,128)(2,1)S(1)}, bf16[2048,1024]{1,0:T(8,128)(2,1)}, u32[]{:S(2)}) copy-start(bf16[2048,1024]{1,0:T(8,128)(2,1)} %copy-done) | copy-start | bytes 12582916
  17.4 7.6 %collective-permute-start.2 = (f32[128,512]{1,0:T(8,128)S(1)}, f32[128,512]{1,0:T(8,128)S(1)}, u32[]{:S(2)}, u32[]{:S(2)}) collective-permute-start(f32[128,512]{1,0:T(8,128)S(1)} %get-tuple-element.12), channel_id=1, source_target_pairs={{0,4},{1,5},{2,6},{3,7},{4,0},{5,1},{6,2},{7,3},{8,12},{9,13},{10,... | collective-permute-start | bytes 786440 | tf_op jit(solution)/shard_map/ppermute | solution.py:107
  19.5 2.2 %copy-start.2 = (bf16[2048,1024]{1,0:T(8,128)(2,1)S(1)}, bf16[2048,1024]{1,0:T(8,128)(2,1)}, u32[]{:S(2)}) copy-start(bf16[2048,1024]{1,0:T(8,128)(2,1)} %copy-done) | copy-start | bytes 12582916
  25.1 4.5 %collective-permute-start.5 = (f32[32,512]{1,0:T(8,128)S(1)}, f32[32,512]{1,0:T(8,128)S(1)}, u32[]{:S(2)}, u32[]{:S(2)}) collective-permute-start(f32[32,512]{1,0:T(8,128)S(1)} %get-tuple-element.14), channel_id=1, source_target_pairs={{0,8},{1,9},{2,10},{3,11},{4,12},{5,13},{6,14},{7,15},{8,0},{9,1},... | collective-permute-start | bytes 196616 | tf_op jit(solution)/shard_map/ppermute | solution.py:107
  27.0 6.7 %collective-permute-start.4 = (f32[32,512]{1,0:T(8,128)S(1)}, f32[32,512]{1,0:T(8,128)S(1)}, u32[]{:S(2)}, u32[]{:S(2)}) collective-permute-start(f32[32,512]{1,0:T(8,128)S(1)} %get-tuple-element.15), channel_id=1, source_target_pairs={{0,16},{1,17},{2,18},{3,19},{4,20},{5,21},{6,22},{7,23},{8,24},{9,... | collective-permute-start | bytes 196616 | tf_op jit(solution)/shard_map/ppermute | solution.py:107
  29.5 6.1 %collective-permute-start.3 = (f32[32,512]{1,0:T(8,128)S(1)}, f32[32,512]{1,0:T(8,128)S(1)}, u32[]{:S(2)}, u32[]{:S(2)}) collective-permute-start(f32[32,512]{1,0:T(8,128)S(1)} %get-tuple-element.13), channel_id=1, source_target_pairs={{0,24},{1,25},{2,26},{3,27},{4,28},{5,29},{6,30},{7,31},{8,16},{9,... | collective-permute-start | bytes 196616 | tf_op jit(solution)/shard_map/ppermute | solution.py:107
  35.7 6.3 %collective-permute-start.8 = (f32[32,512]{1,0:T(8,128)S(1)}, f32[32,512]{1,0:T(8,128)S(1)}, u32[]{:S(2)}, u32[]{:S(2)}) collective-permute-start(f32[32,512]{1,0:T(8,128)S(1)} %add_add_fusion), channel_id=1, source_target_pairs={{0,24},{1,25},{2,26},{3,27},{4,28},{5,29},{6,30},{7,31},{8,16},{9,... | collective-permute-start | bytes 196616 | tf_op jit(solution)/shard_map/ppermute | solution.py:107
  36.5 6.6 %collective-permute-start.7 = (f32[32,512]{1,0:T(8,128)S(1)}, f32[32,512]{1,0:T(8,128)S(1)}, u32[]{:S(2)}, u32[]{:S(2)}) collective-permute-start(f32[32,512]{1,0:T(8,128)S(1)} %add_add_fusion), channel_id=1, source_target_pairs={{0,16},{1,17},{2,18},{3,19},{4,20},{5,21},{6,22},{7,23},{8,24},{9,... | collective-permute-start | bytes 196616 | tf_op jit(solution)/shard_map/ppermute | solution.py:107
  37.1 6.0 %collective-permute-start.6 = (f32[32,512]{1,0:T(8,128)S(1)}, f32[32,512]{1,0:T(8,128)S(1)}, u32[]{:S(2)}, u32[]{:S(2)}) collective-permute-start(f32[32,512]{1,0:T(8,128)S(1)} %add_add_fusion), channel_id=1, source_target_pairs={{0,8},{1,9},{2,10},{3,11},{4,12},{5,13},{6,14},{7,15},{8,0},{9,1},... | collective-permute-start | bytes 196616 | tf_op jit(solution)/shard_map/ppermute | solution.py:107
  43.1 7.3 %collective-permute-start.9 = (f32[128,512]{1,0:T(8,128)S(1)}, f32[128,512]{1,0:T(8,128)S(1)}, u32[]{:S(2)}, u32[]{:S(2)}) collective-permute-start(f32[128,512]{1,0:T(8,128)S(1)} %pad_maximum_fusion.own_rows.own), channel_id=1, source_target_pairs={{0,2},{4,6},{9,11},{13,15},{18,16},{22,20},{27,25},{31,29}} | collective-permute-start | bytes 786440 | tf_op jit(solution)/shard_map/ppermute | solution.py:201
  46.6 6.4 %collective-permute-start.11 = (f32[128,512]{1,0:T(8,128)S(1)}, f32[128,512]{1,0:T(8,128)S(1)}, u32[]{:S(2)}, u32[]{:S(2)}) collective-permute-start(f32[128,512]{1,0:T(8,128)S(1)} %pad_maximum_fusion.own_rows.own), channel_id=1, source_target_pairs={{0,4},{1,5},{2,6},{3,7},{4,0},{5,1},{6,2},{7,3},{8,12},{9,13},{10,... | collective-permute-start | bytes 786440 | tf_op jit(solution)/shard_map/ppermute | solution.py:107
  50.4 2.6 %collective-permute-start.10 = (f32[128,512]{1,0:T(8,128)S(1)}, f32[128,512]{1,0:T(8,128)S(1)}, u32[]{:S(2)}, u32[]{:S(2)}) collective-permute-start(f32[128,512]{1,0:T(8,128)S(1)} %broadcast_select_fusion.near_rows), channel_id=1, source_target_pairs={{0,1},{2,3},{4,5},{6,7},{9,8},{11,10},{13,12},{15,14},{16,17},{18,... | collective-permute-start | bytes 786440 | tf_op jit(solution)/shard_map/ppermute | solution.py:201

commit v2 on v0

v2 whole, which is shorter than its diff:
```python
import functools

import jax
import jax.numpy as jnp
from jax import lax
from jax.experimental import pallas as pl
from jax.experimental.pallas import tpu as pltpu
from jax.sharding import PartitionSpec as P

CL_DEV = 16
AXES = ("cal", "gr")
VMEM = pl.BlockSpec(memory_space=pltpu.VMEM)
SMEM = pl.BlockSpec(memory_space=pltpu.SMEM)
LIMIT = 24 * 1024 * 1024


def position():
    fan = lax.axis_size("cal") // lax.axis_size("gr")
    cal, gr = lax.axis_index("cal"), lax.axis_index("gr")
    return cal, cal // fan, cal % fan, gr


def top_half():
    fan = lax.axis_size("cal") // lax.axis_size("gr")
    return position()[2] // (fan // 2)


def split_two(value):
    high = value.astype(jnp.bfloat16)
    low = (value - high.astype(jnp.float32)).astype(jnp.bfloat16)
    return high, low


def linear_kernel(held, coef, lin, out):
    del out
    rows, width = held.shape
    weights = coef[...].reshape(1, width).astype(jnp.float32)
    step = min(512, rows)
    for i in range(0, rows, step):
        total = jnp.zeros((step, 128), jnp.float32)
        for j in range(0, width, 128):
            total = total + held[i : i + step, j : j + 128].astype(jnp.float32) * weights[:, j : j + 128]
        lin[:, i : i + step] = jnp.sum(total.T, axis=0, keepdims=True)


def picks_kernel(per_dev, group, terms, effect, *refs):
    exposure, claims, ids, period, held, far, near, picks = refs[terms:]
    cal, high, _, _ = position()
    base = cal * per_dev
    shift = jnp.zeros(claims.shape, jnp.float32)
    for k in range(per_dev):
        shift = jnp.where(period[...] == base + k, effect[base + k], shift)
    sums = [ref[...] for ref in refs[:terms]]
    while len(sums) > 1:
        sums = [a + b for a, b in zip(sums[::2], sums[1::2])]
    linear = sums[0]
    resid = claims[...] - jnp.exp(linear + exposure[...] + shift)
    resid = resid.astype(jnp.bfloat16).astype(jnp.float32)
    clusters, rows = picks.shape
    for k in range(clusters // group):
        first = (high ^ k) * group
        cluster = lax.broadcasted_iota(jnp.int32, (group, rows), 0) + first
        picks[k * group : (k + 1) * group, :] = jnp.where(cluster == ids[...], resid, 0.0).astype(jnp.bfloat16)
    half, deep = far.shape[1], far.shape[0]
    columns = pl.ds(pl.multiple_of((1 - top_half()) * half, half), half)
    far[...] = jnp.dot(picks[deep:, :], held[:, columns], preferred_element_type=jnp.float32)
    near[...] = jnp.dot(picks[:deep, :], held[:, columns], preferred_element_type=jnp.float32)


def keep_kernel(picks, held, *outs):
    half, group = outs[0].shape[1], outs[0].shape[0]
    columns = pl.ds(pl.multiple_of(top_half() * half, half), half)
    total = jnp.dot(picks[...], held[:, columns], preferred_element_type=jnp.float32)
    for k, out in enumerate(outs):
        out[...] = total[k * group : (k + 1) * group]


def meat_kernel(scale, have, *refs):
    got, own, other, out = refs[:-5], refs[-5:-3], refs[-3:-1], refs[-1]
    _, high, _, gr = position()
    rows = jnp.where((gr ^ high) % 2 == 0, have[...], jnp.concatenate([ref[...] for ref in got], axis=0))
    left_high, left_low = split_two(rows)
    left = jnp.concatenate([left_high, left_low], axis=0)
    half = own[0].shape[1]
    for k, part in enumerate((own, other)):
        high, low = split_two(jnp.concatenate([p[...] for p in part], axis=0))
        dims = (((0,), (0,)), ((), ()))
        total = lax.dot_general(
            left, jnp.concatenate([high, high], axis=0), dims, preferred_element_type=jnp.float32
        ) + lax.dot_general(left_high, low, dims, preferred_element_type=jnp.float32)
        spot = top_half() if k == 0 else 1 - top_half()
        out[:, pl.ds(pl.multiple_of(spot * half, half), half)] = total * scale


def exchange(value, cal_bits, gr_bits, n_cal, n_gr):
    pairs = [
        (c * n_gr + g, (c ^ cal_bits) * n_gr + (g ^ gr_bits))
        for c in range(n_cal)
        for g in range(n_gr)
    ]
    return lax.ppermute(value, AXES, pairs)


def per_device(features, coef, log_exposure, claims, cluster_id, period, period_effect):
    rows, width = features.shape
    n_cal, n_gr = lax.axis_size("cal"), lax.axis_size("gr")
    clusters = CL_DEV * n_cal
    per_dev = period_effect.shape[0] // n_cal
    fan = n_cal // n_gr
    cal, gr = lax.axis_index("cal"), lax.axis_index("gr")
    high, low = cal // fan, cal % fan
    swap = functools.partial(exchange, n_cal=n_cal, n_gr=n_gr)

    def kernel(body, out_shape, args, scalars, name, flops=0, alias={}):
        outs = out_shape if isinstance(out_shape, tuple) else (out_shape,)
        call = pl.pallas_call(
            body,
            out_shape=out_shape,
            in_specs=[SMEM] * scalars + [VMEM] * (len(args) - scalars),
            out_specs=tuple(VMEM for _ in outs) if isinstance(out_shape, tuple) else VMEM,
            compiler_params=pltpu.CompilerParams(vmem_limit_bytes=LIMIT),
            cost_estimate=pl.CostEstimate(flops=flops, bytes_accessed=flops // 256, transcendentals=0),
            name=name,
            input_output_aliases=alias,
        )
        return call(*args)

    f32, bf16 = jnp.float32, jnp.bfloat16
    lin, features = kernel(
        linear_kernel,
        (jax.ShapeDtypeStruct((1, rows), f32), jax.ShapeDtypeStruct((rows, width), bf16)),
        (features, coef), 0, "linear", 2 * rows * width, {0: 1},
    )
    linears = [lin] + [swap(lin, 0, k) for k in range(1, n_gr)]

    half = width // 2
    deep = clusters // 2
    group = clusters // n_gr
    flat = [v.reshape(1, rows) for v in (log_exposure, claims, cluster_id, period)]
    work = 2 * rows * deep * half
    far, near, picks = kernel(
        functools.partial(picks_kernel, per_dev, group, n_gr),
        (
            jax.ShapeDtypeStruct((deep, half), f32),
            jax.ShapeDtypeStruct((deep, half), f32),
            jax.ShapeDtypeStruct((clusters, rows), bf16),
        ),
        (period_effect, *linears, *flat, features),
        1, "send", 2 * work,
    )
    there = [swap(near, fan // 2, 0), swap(far, fan // 2, 0)]
    kept = kernel(
        keep_kernel, tuple(jax.ShapeDtypeStruct((group, half), f32) for _ in range(n_gr)),
        (picks, features), 0, "keep", 2 * work,
    )
    parts = []
    for k in range(n_gr):
        start = k * group % deep
        part = kept[k] + there[k * group // deep][start : start + group]
        bits = fan // 4
        while bits:
            size = part.shape[1] // 2
            mine = (low // bits) % 2
            away = lax.dynamic_slice_in_dim(part, (1 - mine) * size, size, axis=1)
            part = lax.dynamic_slice_in_dim(part, mine * size, size, axis=1) + swap(away, bits, 0)
            bits //= 2
        parts.append(part)

    arrived = [swap(parts[k], k * fan, 0) for k in range(n_gr - 1, 0, -1)]
    owned = parts[0]
    for part in arrived[::-1]:
        owned = owned + part
    gathered = [owned] + [swap(owned, k * fan, 0) for k in range(n_gr - 1, 0, -1)][::-1]
    blocks = [gathered[0], jnp.concatenate(gathered[1:], axis=0)]
    sides, others = [], []
    for side in blocks:
        bits = 1
        while bits < fan // 2:
            mine = (low // bits) % 2
            away = swap(side, bits, 0)
            side = jnp.where(
                mine == 0, jnp.concatenate([side, away], axis=1), jnp.concatenate([away, side], axis=1)
            )
            bits *= 2
        sides.append(side)
        others.append(swap(side, fan // 2, 0))

    have = jnp.concatenate(gathered, axis=0)
    have, others[0] = lax.optimization_barrier((have, others[0]))
    turn = gr ^ high
    bits = n_gr // 2
    while bits > 1:
        pairs = []
        for c in range(n_cal):
            for g in range(n_gr):
                step = (g ^ (c // fan)) & (2 * bits - 1)
                flip = bits if step == 0 or step == 2 * bits - 1 else bits // 2
                pairs.append((c * n_gr + g, c * n_gr + (g ^ flip)))
        if bits > 2:
            pairs = [(c * n_gr + g, c * n_gr + (g ^ bits)) for c in range(n_cal) for g in range(n_gr)]
        got = lax.ppermute(have, AXES, pairs)
        have = jnp.where((turn & bits) != 0, got, have)
        bits //= 2
    got = [swap(have[k * group : (k + 1) * group], 0, 1) for k in range(n_gr)]
    scale = 1.0 / (rows * n_cal)
    return kernel(
        functools.partial(meat_kernel, scale),
        jax.ShapeDtypeStruct((blocks[0].shape[1], width), f32),
        (have, *got, *sides, *others),
        0, "meat", 6 * clusters * width * blocks[0].shape[1],
    )


def solution(mesh):
    placed = (P("cal", "gr"), P("gr"), P("cal"), P("cal"), P("cal"), P("cal"), P())
    return jax.shard_map(
        per_device, mesh=mesh, in_specs=placed, out_specs=P("cal", "gr"), check_vma=False
    )
```

time: 146 us -> 45 us (0.31)
  blocking collectives: 49 us -> 0 us
  waiting for transfers between devices: 62.8 us -> 18.3 us
  starting transfers between devices: 3.65 us -> 19.1 us
  matrix products: 14 us -> 0 us
  between operations: 13.5 us -> 0.15 us
  Pallas kernels: 0 us -> 4.84 us
    reduce_scatter x1 -> x0, waiting for transfers between devices: 62.8 us -> none  [per_device(): lax.psum_scatter(partial_scores, 'cal', scatter_dimension=0, tiled=True)]
    all_gather x2 -> x0, blocking collectives: 40.5 us -> none  [the longest x1 34.5 us: per_device(): lax.all_gather(owned, 'cal', axis=0, tiled=True)]
    ppermute x0 -> x18, starting transfers between devices: none -> 19.1 us  [the longest x17 18.2 us: exchange(): return lax.ppermute(value, AXES, pairs)]
    ppermute x0 -> x18, waiting for transfers between devices: none -> 18.3 us  [the longest x17 16.1 us: exchange(): return lax.ppermute(value, AXES, pairs)]
    dot_general x6 -> x0, matrix products: 14 us -> none  [the longest x4 7.46 us: step(): lax.dot_general(picks, feat_blk, (((0,), (0,)), ((), ())), preferred_elem...]
    psum x1 -> x0, blocking collectives: 8.48 us -> none  [per_device(): linear = lax.psum(local_lin, 'gr')]
    pallas_call x0 -> x4, Pallas kernels: none -> 4.84 us  [kernel(): return call(*args)]
    all_to_all x1 -> x0, starting transfers between devices: 3.61 us -> none  [per_device(): lax.all_to_all(full_scores, 'cal', split_axis=1, concat_axis=0, tiled=True)]
  transfers between devices with their start and end apart: 2 -> 18, of which waited for: 1 -> 9; matrix products, arithmetic and copies ran while one was open for 0% -> 0% of each run, Pallas kernels for 0% -> 1%
where the time goes in v2:
time: 45 us; the launch traced here: 44.8 us
  starting transfers between devices  19.1 us (42%)
  waiting for transfers between devices  18.3 us (41%)
  Pallas kernels  4.84 us (11%)
  local copies, waits for them, and re-layouts  2.27 us (5%)
    ppermute x17, starting transfers between devices, exchange(): return lax.ppermute(value, AXES, pairs)  18.2 us
    ppermute x17, waiting for transfers between devices, exchange(): return lax.ppermute(value, AXES, pairs)  16.1 us
    pallas_call x4, Pallas kernels, kernel(): return call(*args)  4.84 us
    ppermute x1, waiting for transfers between devices, per_device(): got = lax.ppermute(have, AXES, pairs)  2.24 us
    unnamed x15, local copies, waits for them, and re-layouts  2.24 us
    ppermute x1, starting transfers between devices, per_device(): got = lax.ppermute(have, AXES, pairs)  0.91 us
  transfers between devices with their start and end apart: 18, of which 9 were waited for; matrix products, arithmetic and copies ran while one was open for 0% of the time, Pallas kernels for 1%

profile of v2, /device:TPU:0, one launch (start us, length us, event | category | flops | bytes accessed | tf_op | source)
XLA Modules:
  0.0 44.8 jit_solution(2213186932682294595)
XLA Ops:
  0.0 0.0 copy-start.4
  0.0 2.2 %copy.13.held = bf16[2048,1024]{1,0:T(8,128)(2,1)S(1)} copy(bf16[2048,1024]{1,0:T(8,128)(2,1)} %param.7) | data formatting | bytes 8388608
  2.2 0.0 copy-done.4
  2.2 0.0 copy-start
  2.2 0.0 copy-start.1
  2.2 0.0 copy-start.2
  2.2 0.0 copy-start.3
  2.2 0.0 copy-start.5
  2.2 0.9 %linear.1 = (f32[1,2048]{1,0:T(1,128)S(1)}, bf16[2048,1024]{1,0:T(8,128)(2,1)S(1)}) custom-call(bf16[2048,1024]{1,0:T(8,128)(2,1)S(1)} %copy.13.held, bf16[1024]{0:T(1024)(128)(2,1)S(1)} %copy-done.4), custom_call_target="tpu_custom_call", output_to_operand_aliasing={{1}: (0, {})} | custom-call | flops 4194304 | bytes 16384 | tf_op jit(solution)/shard_map/linear/pallas_call | solution.py:126
  3.1 0.5 %collective-permute-start = (f32[1,2048]{1,0:T(1,128)S(1)}, f32[1,2048]{1,0:T(1,128)S(1)}, u32[]{:S(2)}, u32[]{:S(2)}) collective-permute-start(f32[1,2048]{1,0:T(1,128)S(1)} %get-tuple-element.16.refs_0_), channel_id=1, source_target_pairs={{0,1},{1,0},{2,3},{3,2},{4,5},{5,4},{6,7},{7,6},{8,9},{9,8},{10,11... | collective-permute-start | bytes 24584 | tf_op jit(solution)/shard_map/ppermute | solution.py:101
  3.7 2.6 %collective-permute-start.1 = (f32[1,2048]{1,0:T(1,128)S(1)}, f32[1,2048]{1,0:T(1,128)S(1)}, u32[]{:S(2)}, u32[]{:S(2)}) collective-permute-start(f32[1,2048]{1,0:T(1,128)S(1)} %get-tuple-element.16.refs_0_), channel_id=1, source_target_pairs={{0,2},{1,3},{2,0},{3,1},{4,6},{5,7},{6,4},{7,5},{8,10},{9,11},{10,... | collective-permute-start | bytes 24584 | tf_op jit(solution)/shard_map/ppermute | solution.py:101
  6.2 0.1 collective-permute-start.2
  6.3 0.0 collective-permute-done.refs_1_
  6.3 1.6 %collective-permute-done.1.refs_2_ = f32[1,2048]{1,0:T(1,128)S(1)} collective-permute-done((f32[1,2048]{1,0:T(1,128)S(1)}, f32[1,2048]{1,0:T(1,128)S(1)}, u32[]{:S(2)}, u32[]{:S(2)}) %collective-permute-start.1) | collective-permute-done | bytes 8224 | tf_op jit(solution)/shard_map/ppermute | solution.py:101
  7.9 1.4 %collective-permute-done.2.refs_3_ = f32[1,2048]{1,0:T(1,128)S(1)} collective-permute-done((f32[1,2048]{1,0:T(1,128)S(1)}, f32[1,2048]{1,0:T(1,128)S(1)}, u32[]{:S(2)}, u32[]{:S(2)}) %collective-permute-start.2) | collective-permute-done | bytes 8224 | tf_op jit(solution)/shard_map/ppermute | solution.py:101
  9.3 0.0 copy-done
  9.3 0.0 copy-done.1
  9.3 0.0 copy-done.2
  9.3 0.0 copy-done.3
  9.3 0.0 copy-done.5
  9.3 1.4 %send.1 = (f32[64,512]{1,0:T(8,128)S(1)}, f32[64,512]{1,0:T(8,128)S(1)}, bf16[128,2048]{1,0:T(8,128)(2,1)S(1)}) custom-call(f32[16]{0:T(128)S(1)} %copy-done.5, f32[1,2048]{1,0:T(1,128)S(1)} %get-tuple-element.16.refs_0_, f32[1,2048]{1,0:T(1,128)S(1)} %collective-permute-done.refs_1_, f32[1,2048]{1,0:T(1,128)S(1)} %collective-permute-done.1.refs_2_, ...), custom_call_target="tpu_custom_call" | custom-call | flops 268435456 | bytes 1048576 | tf_op jit(solution)/shard_map/send/pallas_call | solution.py:126
  10.7 1.6 %collective-permute-start.5 = (f32[64,512]{1,0:T(8,128)S(1)}, f32[64,512]{1,0:T(8,128)S(1)}, u32[]{:S(2)}, u32[]{:S(2)}) collective-permute-start(f32[64,512]{1,0:T(8,128)S(1)} %get-tuple-element.23), channel_id=1, source_target_pairs={{0,4},{1,5},{2,6},{3,7},{4,0},{5,1},{6,2},{7,3},{8,12},{9,13},{10,... | collective-permute-start | bytes 393224 | tf_op jit(solution)/shard_map/ppermute | solution.py:101
  12.4 0.5 %collective-permute-start.3 = (f32[64,512]{1,0:T(8,128)S(1)}, f32[64,512]{1,0:T(8,128)S(1)}, u32[]{:S(2)}, u32[]{:S(2)}) collective-permute-start(f32[64,512]{1,0:T(8,128)S(1)} %get-tuple-element.20), channel_id=1, source_target_pairs={{0,4},{1,5},{2,6},{3,7},{4,0},{5,1},{6,2},{7,3},{8,12},{9,13},{10,... | collective-permute-start | bytes 393224 | tf_op jit(solution)/shard_map/ppermute | solution.py:101
  12.8 0.5 %keep.1 = (f32[32,512]{1,0:T(8,128)S(1)}, f32[32,512]{1,0:T(8,128)S(1)}, f32[32,512]{1,0:T(8,128)S(1)}, f32[32,512]{1,0:T(8,128)S(1)}) custom-call(bf16[128,2048]{1,0:T(8,128)(2,1)S(1)} %get-tuple-element.18.picks, bf16[2048,1024]{1,0:T(8,128)(2,1)S(1)} %get-tuple-element.17.refs_8_.held), custom_call_target="tpu_custom_call" | custom-call | flops 268435456 | bytes 1048576 | tf_op jit(solution)/shard_map/keep/pallas_call | solution.py:126
  13.3 3.9 %collective-permute-done.5 = f32[64,512]{1,0:T(8,128)S(1)} collective-permute-done((f32[64,512]{1,0:T(8,128)S(1)}, f32[64,512]{1,0:T(8,128)S(1)}, u32[]{:S(2)}, u32[]{:S(2)}) %collective-permute-start.5) | collective-permute-done | bytes 131104 | tf_op jit(solution)/shard_map/ppermute | solution.py:101
  17.2 2.7 %collective-permute-start.6 = (f32[32,512]{1,0:T(8,128)S(1)}, f32[32,512]{1,0:T(8,128)S(1)}, u32[]{:S(2)}, u32[]{:S(2)}) collective-permute-start(f32[32,512]{1,0:T(8,128)S(1)} %get-tuple-element.31), channel_id=1, source_target_pairs={{0,16},{1,17},{2,18},{3,19},{4,20},{5,21},{6,22},{7,23},{8,24},{9,... | collective-permute-start | bytes 196616 | tf_op jit(solution)/shard_map/ppermute | solution.py:101
  19.8 1.3 %collective-permute-start.7 = (f32[32,512]{1,0:T(8,128)S(1)}, f32[32,512]{1,0:T(8,128)S(1)}, u32[]{:S(2)}, u32[]{:S(2)}) collective-permute-start(f32[32,512]{1,0:T(8,128)S(1)} %get-tuple-element.32), channel_id=1, source_target_pairs={{0,24},{1,25},{2,26},{3,27},{4,28},{5,29},{6,30},{7,31},{8,16},{9,... | collective-permute-start | bytes 196616 | tf_op jit(solution)/shard_map/ppermute | solution.py:101
  21.2 0.0 collective-permute-done.3
  21.2 0.3 collective-permute-start.4
  21.5 3.0 %collective-permute-done.6 = f32[32,512]{1,0:T(8,128)S(1)} collective-permute-done((f32[32,512]{1,0:T(8,128)S(1)}, f32[32,512]{1,0:T(8,128)S(1)}, u32[]{:S(2)}, u32[]{:S(2)}) %collective-permute-start.6) | collective-permute-done | bytes 65568 | tf_op jit(solution)/shard_map/ppermute | solution.py:101
  24.5 1.5 %collective-permute-done.7 = f32[32,512]{1,0:T(8,128)S(1)} collective-permute-done((f32[32,512]{1,0:T(8,128)S(1)}, f32[32,512]{1,0:T(8,128)S(1)}, u32[]{:S(2)}, u32[]{:S(2)}) %collective-permute-start.7) | collective-permute-done | bytes 65568 | tf_op jit(solution)/shard_map/ppermute | solution.py:101
  26.0 0.2 collective-permute-done.4
  26.3 0.1 collective-permute-start.8
  26.3 2.7 %collective-permute-start.9 = (f32[32,512]{1,0:T(8,128)S(1)}, f32[32,512]{1,0:T(8,128)S(1)}, u32[]{:S(2)}, u32[]{:S(2)}) collective-permute-start(f32[32,512]{1,0:T(8,128)S(1)} %fusion.2.refs_4_), channel_id=1, source_target_pairs={{0,16},{1,17},{2,18},{3,19},{4,20},{5,21},{6,22},{7,23},{8,24},{9,... | collective-permute-start | bytes 196616 | tf_op jit(solution)/shard_map/ppermute | solution.py:101
  29.1 1.7 %collective-permute-start.10 = (f32[32,512]{1,0:T(8,128)S(1)}, f32[32,512]{1,0:T(8,128)S(1)}, u32[]{:S(2)}, u32[]{:S(2)}) collective-permute-start(f32[32,512]{1,0:T(8,128)S(1)} %fusion.2.refs_4_), channel_id=1, source_target_pairs={{0,24},{1,25},{2,26},{3,27},{4,28},{5,29},{6,30},{7,31},{8,16},{9,... | collective-permute-start | bytes 196616 | tf_op jit(solution)/shard_map/ppermute | solution.py:101
  30.7 1.6 %collective-permute-start.11 = (f32[32,512]{1,0:T(8,128)S(1)}, f32[32,512]{1,0:T(8,128)S(1)}, u32[]{:S(2)}, u32[]{:S(2)}) collective-permute-start(f32[32,512]{1,0:T(8,128)S(1)} %fusion.2.refs_4_), channel_id=1, source_target_pairs={{0,4},{1,5},{2,6},{3,7},{4,0},{5,1},{6,2},{7,3},{8,12},{9,13},{10,... | collective-permute-start | bytes 196616 | tf_op jit(solution)/shard_map/ppermute | solution.py:101
  32.3 0.0 collective-permute-done.8
  32.3 0.0 collective-permute-done.9
  32.3 2.9 %collective-permute-done.10 = f32[32,512]{1,0:T(8,128)S(1)} collective-permute-done((f32[32,512]{1,0:T(8,128)S(1)}, f32[32,512]{1,0:T(8,128)S(1)}, u32[]{:S(2)}, u32[]{:S(2)}) %collective-permute-start.10) | collective-permute-done | bytes 65568 | tf_op jit(solution)/shard_map/ppermute | solution.py:101
  35.1 0.0 collective-permute-done.11.refs_6_
  35.1 0.9 %collective-permute-start.12 = (f32[128,512]{1,0:T(8,128)S(1)}, f32[128,512]{1,0:T(8,128)S(1)}, u32[]{:S(2)}, u32[]{:S(2)}) collective-permute-start(f32[128,512]{1,0:T(8,128)S(1)} %pad_maximum_fusion), channel_id=1, source_target_pairs={{0,2},{1,0},{2,3},{3,1},{4,6},{5,4},{6,7},{7,5},{8,9},{9,11},{10,8... | collective-permute-start | bytes 786440 | tf_op jit(solution)/shard_map/ppermute | solution.py:201
  36.1 1.6 %collective-permute-start.17 = (f32[96,512]{1,0:T(8,128)S(1)}, f32[96,512]{1,0:T(8,128)S(1)}, u32[]{:S(2)}, u32[]{:S(2)}) collective-permute-start(f32[96,512]{1,0:T(8,128)S(1)} %constant_dynamic-update-slice_fusion.refs_5_), channel_id=1, source_target_pairs={{0,4},{1,5},{2,6},{3,7},{4,0},{5,1},{6,2},{7,3},{8,12},{9,13},{10,... | collective-permute-start | bytes 589832 | tf_op jit(solution)/shard_map/ppermute | solution.py:101
  37.7 2.2 %collective-permute-done.12 = f32[128,512]{1,0:T(8,128)S(1)} collective-permute-done((f32[128,512]{1,0:T(8,128)S(1)}, f32[128,512]{1,0:T(8,128)S(1)}, u32[]{:S(2)}, u32[]{:S(2)}) %collective-permute-start.12) | collective-permute-done | bytes 262176 | tf_op jit(solution)/shard_map/ppermute | solution.py:201
  40.0 0.1 collective-permute-start.13
  40.1 0.5 %collective-permute-start.14 = (f32[32,512]{1,0:T(8,128)S(1)}, f32[32,512]{1,0:T(8,128)S(1)}, u32[]{:S(2)}, u32[]{:S(2)}) collective-permute-start(f32[32,512]{1,0:T(8,128)S(1)} %get-tuple-element.29), channel_id=1, source_target_pairs={{0,1},{1,0},{2,3},{3,2},{4,5},{5,4},{6,7},{7,6},{8,9},{9,8},{10,11... | collective-permute-start | bytes 196616 | tf_op jit(solution)/shard_map/ppermute | solution.py:101
  40.6 0.1 collective-permute-start.15
  40.7 0.4 collective-permute-start.16
  41.1 1.6 %collective-permute-done.17.refs_7_ = f32[96,512]{1,0:T(8,128)S(1)} collective-permute-done((f32[96,512]{1,0:T(8,128)S(1)}, f32[96,512]{1,0:T(8,128)S(1)}, u32[]{:S(2)}, u32[]{:S(2)}) %collective-permute-start.17) | collective-permute-done | bytes 196640 | tf_op jit(solution)/shard_map/ppermute | solution.py:101
  42.7 0.0 collective-permute-done.13.refs_0_
  42.7 0.0 collective-permute-done.14.refs_1_
  42.7 0.0 collective-permute-done.15.refs_2_
  42.7 0.0 collective-permute-done.16.refs_3_
  42.7 2.1 %meat.1 = f32[512,1024]{1,0:T(8,128)} custom-call(f32[128,512]{1,0:T(8,128)S(1)} %broadcast_select_fusion.have, f32[32,512]{1,0:T(8,128)S(1)} %collective-permute-done.13.refs_0_, f32[32,512]{1,0:T(8,128)S(1)} %collective-permute-done.14.refs_1_, f32[32,512]{1,0:T(8,128)S(1)} %collective-permute-done.15.refs_2_, ...), custom_call_target="tpu_custom_call" | custom-call | flops 402653184 | bytes 1572864 | tf_op jit(solution)/shard_map/meat/pallas_call | solution.py:126
  (9 shorter events, 0.1 us)
Async XLA Ops:
  0.0 2.2 %copy-start.4 = (bf16[1024]{0:T(1024)(128)(2,1)S(1)}, bf16[1024]{0:T(1024)(128)(2,1)}, u32[]{:S(2)}) copy-start(bf16[1024]{0:T(1024)(128)(2,1)} %coef.1) | copy-start | bytes 6148
  2.2 7.1 %copy-start = (f32[2048]{0:T(1024)S(1)}, f32[2048]{0:T(1024)}, u32[]{:S(2)}) copy-start(f32[2048]{0:T(1024)} %param.9) | copy-start | bytes 24580
  2.2 7.1 %copy-start.1 = (f32[2048]{0:T(1024)S(1)}, f32[2048]{0:T(1024)}, u32[]{:S(2)}) copy-start(f32[2048]{0:T(1024)} %param.10) | copy-start | bytes 24580
  2.2 7.1 %copy-start.2 = (s32[2048]{0:T(1024)S(1)}, s32[2048]{0:T(1024)}, u32[]{:S(2)}) copy-start(s32[2048]{0:T(1024)} %param.11) | copy-start | bytes 24580
  2.2 7.1 %copy-start.3 = (s32[2048]{0:T(1024)S(1)}, s32[2048]{0:T(1024)}, u32[]{:S(2)}) copy-start(s32[2048]{0:T(1024)} %param.12) | copy-start | bytes 24580
  2.2 7.1 %copy-start.5 = (f32[16]{0:T(128)S(1)}, f32[16]{0:T(128)}, u32[]{:S(2)}) copy-start(f32[16]{0:T(128)} %effect.1) | copy-start | bytes 196
  3.1 3.2 %collective-permute-start = (f32[1,2048]{1,0:T(1,128)S(1)}, f32[1,2048]{1,0:T(1,128)S(1)}, u32[]{:S(2)}, u32[]{:S(2)}) collective-permute-start(f32[1,2048]{1,0:T(1,128)S(1)} %get-tuple-element.16.refs_0_), channel_id=1, source_target_pairs={{0,1},{1,0},{2,3},{3,2},{4,5},{5,4},{6,7},{7,6},{8,9},{9,8},{10,11... | collective-permute-start | bytes 24584 | tf_op jit(solution)/shard_map/ppermute | solution.py:101
  3.7 4.2 %collective-permute-start.1 = (f32[1,2048]{1,0:T(1,128)S(1)}, f32[1,2048]{1,0:T(1,128)S(1)}, u32[]{:S(2)}, u32[]{:S(2)}) collective-permute-start(f32[1,2048]{1,0:T(1,128)S(1)} %get-tuple-element.16.refs_0_), channel_id=1, source_target_pairs={{0,2},{1,3},{2,0},{3,1},{4,6},{5,7},{6,4},{7,5},{8,10},{9,11},{10,... | collective-permute-start | bytes 24584 | tf_op jit(solution)/shard_map/ppermute | solution.py:101
  6.2 3.1 %collective-permute-start.2 = (f32[1,2048]{1,0:T(1,128)S(1)}, f32[1,2048]{1,0:T(1,128)S(1)}, u32[]{:S(2)}, u32[]{:S(2)}) collective-permute-start(f32[1,2048]{1,0:T(1,128)S(1)} %get-tuple-element.16.refs_0_), channel_id=1, source_target_pairs={{0,3},{1,2},{2,1},{3,0},{4,7},{5,6},{6,5},{7,4},{8,11},{9,10},{10,... | collective-permute-start | bytes 24584 | tf_op jit(solution)/shard_map/ppermute | solution.py:101
  10.7 6.4 %collective-permute-start.5 = (f32[64,512]{1,0:T(8,128)S(1)}, f32[64,512]{1,0:T(8,128)S(1)}, u32[]{:S(2)}, u32[]{:S(2)}) collective-permute-start(f32[64,512]{1,0:T(8,128)S(1)} %get-tuple-element.23), channel_id=1, source_target_pairs={{0,4},{1,5},{2,6},{3,7},{4,0},{5,1},{6,2},{7,3},{8,12},{9,13},{10,... | collective-permute-start | bytes 393224 | tf_op jit(solution)/shard_map/ppermute | solution.py:101
  12.4 8.8 %collective-permute-start.3 = (f32[64,512]{1,0:T(8,128)S(1)}, f32[64,512]{1,0:T(8,128)S(1)}, u32[]{:S(2)}, u32[]{:S(2)}) collective-permute-start(f32[64,512]{1,0:T(8,128)S(1)} %get-tuple-element.20), channel_id=1, source_target_pairs={{0,4},{1,5},{2,6},{3,7},{4,0},{5,1},{6,2},{7,3},{8,12},{9,13},{10,... | collective-permute-start | bytes 393224 | tf_op jit(solution)/shard_map/ppermute | solution.py:101
  17.2 7.3 %collective-permute-start.6 = (f32[32,512]{1,0:T(8,128)S(1)}, f32[32,512]{1,0:T(8,128)S(1)}, u32[]{:S(2)}, u32[]{:S(2)}) collective-permute-start(f32[32,512]{1,0:T(8,128)S(1)} %get-tuple-element.31), channel_id=1, source_target_pairs={{0,16},{1,17},{2,18},{3,19},{4,20},{5,21},{6,22},{7,23},{8,24},{9,... | collective-permute-start | bytes 196616 | tf_op jit(solution)/shard_map/ppermute | solution.py:101
  19.8 6.2 %collective-permute-start.7 = (f32[32,512]{1,0:T(8,128)S(1)}, f32[32,512]{1,0:T(8,128)S(1)}, u32[]{:S(2)}, u32[]{:S(2)}) collective-permute-start(f32[32,512]{1,0:T(8,128)S(1)} %get-tuple-element.32), channel_id=1, source_target_pairs={{0,24},{1,25},{2,26},{3,27},{4,28},{5,29},{6,30},{7,31},{8,16},{9,... | collective-permute-start | bytes 196616 | tf_op jit(solution)/shard_map/ppermute | solution.py:101
  21.2 5.0 %collective-permute-start.4 = (f32[32,512]{1,0:T(8,128)S(1)}, f32[32,512]{1,0:T(8,128)S(1)}, u32[]{:S(2)}, u32[]{:S(2)}) collective-permute-start(f32[32,512]{1,0:T(8,128)S(1)} %slice_add_fusion.2), channel_id=1, source_target_pairs={{0,8},{1,9},{2,10},{3,11},{4,12},{5,13},{6,14},{7,15},{8,0},{9,1},... | collective-permute-start | bytes 196616 | tf_op jit(solution)/shard_map/ppermute | solution.py:101
  26.3 6.0 %collective-permute-start.8 = (f32[32,512]{1,0:T(8,128)S(1)}, f32[32,512]{1,0:T(8,128)S(1)}, u32[]{:S(2)}, u32[]{:S(2)}) collective-permute-start(f32[32,512]{1,0:T(8,128)S(1)} %fusion.2.refs_4_), channel_id=1, source_target_pairs={{0,8},{1,9},{2,10},{3,11},{4,12},{5,13},{6,14},{7,15},{8,0},{9,1},... | collective-permute-start | bytes 196616 | tf_op jit(solution)/shard_map/ppermute | solution.py:101
  26.3 5.9 %collective-permute-start.9 = (f32[32,512]{1,0:T(8,128)S(1)}, f32[32,512]{1,0:T(8,128)S(1)}, u32[]{:S(2)}, u32[]{:S(2)}) collective-permute-start(f32[32,512]{1,0:T(8,128)S(1)} %fusion.2.refs_4_), channel_id=1, source_target_pairs={{0,16},{1,17},{2,18},{3,19},{4,20},{5,21},{6,22},{7,23},{8,24},{9,... | collective-permute-start | bytes 196616 | tf_op jit(solution)/shard_map/ppermute | solution.py:101
  29.1 6.1 %collective-permute-start.10 = (f32[32,512]{1,0:T(8,128)S(1)}, f32[32,512]{1,0:T(8,128)S(1)}, u32[]{:S(2)}, u32[]{:S(2)}) collective-permute-start(f32[32,512]{1,0:T(8,128)S(1)} %fusion.2.refs_4_), channel_id=1, source_target_pairs={{0,24},{1,25},{2,26},{3,27},{4,28},{5,29},{6,30},{7,31},{8,16},{9,... | collective-permute-start | bytes 196616 | tf_op jit(solution)/shard_map/ppermute | solution.py:101
  30.7 4.4 %collective-permute-start.11 = (f32[32,512]{1,0:T(8,128)S(1)}, f32[32,512]{1,0:T(8,128)S(1)}, u32[]{:S(2)}, u32[]{:S(2)}) collective-permute-start(f32[32,512]{1,0:T(8,128)S(1)} %fusion.2.refs_4_), channel_id=1, source_target_pairs={{0,4},{1,5},{2,6},{3,7},{4,0},{5,1},{6,2},{7,3},{8,12},{9,13},{10,... | collective-permute-start | bytes 196616 | tf_op jit(solution)/shard_map/ppermute | solution.py:101
  35.1 4.8 %collective-permute-start.12 = (f32[128,512]{1,0:T(8,128)S(1)}, f32[128,512]{1,0:T(8,128)S(1)}, u32[]{:S(2)}, u32[]{:S(2)}) collective-permute-start(f32[128,512]{1,0:T(8,128)S(1)} %pad_maximum_fusion), channel_id=1, source_target_pairs={{0,2},{1,0},{2,3},{3,1},{4,6},{5,4},{6,7},{7,5},{8,9},{9,11},{10,8... | collective-permute-start | bytes 786440 | tf_op jit(solution)/shard_map/ppermute | solution.py:201
  36.1 6.6 %collective-permute-start.17 = (f32[96,512]{1,0:T(8,128)S(1)}, f32[96,512]{1,0:T(8,128)S(1)}, u32[]{:S(2)}, u32[]{:S(2)}) collective-permute-start(f32[96,512]{1,0:T(8,128)S(1)} %constant_dynamic-update-slice_fusion.refs_5_), channel_id=1, source_target_pairs={{0,4},{1,5},{2,6},{3,7},{4,0},{5,1},{6,2},{7,3},{8,12},{9,13},{10,... | collective-permute-start | bytes 589832 | tf_op jit(solution)/shard_map/ppermute | solution.py:101
  40.0 2.7 %collective-permute-start.13 = (f32[32,512]{1,0:T(8,128)S(1)}, f32[32,512]{1,0:T(8,128)S(1)}, u32[]{:S(2)}, u32[]{:S(2)}) collective-permute-start(f32[32,512]{1,0:T(8,128)S(1)} %get-tuple-element.30), channel_id=1, source_target_pairs={{0,1},{1,0},{2,3},{3,2},{4,5},{5,4},{6,7},{7,6},{8,9},{9,8},{10,11... | collective-permute-start | bytes 196616 | tf_op jit(solution)/shard_map/ppermute | solution.py:101
  40.1 2.6 %collective-permute-start.14 = (f32[32,512]{1,0:T(8,128)S(1)}, f32[32,512]{1,0:T(8,128)S(1)}, u32[]{:S(2)}, u32[]{:S(2)}) collective-permute-start(f32[32,512]{1,0:T(8,128)S(1)} %get-tuple-element.29), channel_id=1, source_target_pairs={{0,1},{1,0},{2,3},{3,2},{4,5},{5,4},{6,7},{7,6},{8,9},{9,8},{10,11... | collective-permute-start | bytes 196616 | tf_op jit(solution)/shard_map/ppermute | solution.py:101
  40.6 2.1 %collective-permute-start.15 = (f32[32,512]{1,0:T(8,128)S(1)}, f32[32,512]{1,0:T(8,128)S(1)}, u32[]{:S(2)}, u32[]{:S(2)}) collective-permute-start(f32[32,512]{1,0:T(8,128)S(1)} %get-tuple-element.28), channel_id=1, source_target_pairs={{0,1},{1,0},{2,3},{3,2},{4,5},{5,4},{6,7},{7,6},{8,9},{9,8},{10,11... | collective-permute-start | bytes 196616 | tf_op jit(solution)/shard_map/ppermute | solution.py:101
  40.7 2.0 %collective-permute-start.16 = (f32[32,512]{1,0:T(8,128)S(1)}, f32[32,512]{1,0:T(8,128)S(1)}, u32[]{:S(2)}, u32[]{:S(2)}) collective-permute-start(f32[32,512]{1,0:T(8,128)S(1)} %get-tuple-element.27), channel_id=1, source_target_pairs={{0,1},{1,0},{2,3},{3,2},{4,5},{5,4},{6,7},{7,6},{8,9},{9,8},{10,11... | collective-permute-start | bytes 196616 | tf_op jit(solution)/shard_map/ppermute | solution.py:101

commit v3 on v2

--- a/solution.py
+++ b/solution.py
@@ -11,6 +11,7 @@
 AXES = ("cal", "gr")
 VMEM = pl.BlockSpec(memory_space=pltpu.VMEM)
 SMEM = pl.BlockSpec(memory_space=pltpu.SMEM)
+ANY = pl.BlockSpec(memory_space=pl.ANY)
 LIMIT = 24 * 1024 * 1024
 
 
@@ -43,8 +44,14 @@
         lin[:, i : i + step] = jnp.sum(total.T, axis=0, keepdims=True)
 
 
+def spread(total, outs):
+    size = outs[0].shape[0]
+    for k, out in enumerate(outs):
+        out[...] = total[k * size : (k + 1) * size]
+
+
 def picks_kernel(per_dev, group, terms, effect, *refs):
-    exposure, claims, ids, period, held, far, near, picks = refs[terms:]
+    exposure, claims, ids, period, held, *far, picks = refs[terms:]
     cal, high, _, _ = position()
     base = cal * per_dev
     shift = jnp.zeros(claims.shape, jnp.float32)
@@ -61,35 +68,68 @@
         first = (high ^ k) * group
         cluster = lax.broadcasted_iota(jnp.int32, (group, rows), 0) + first
         picks[k * group : (k + 1) * group, :] = jnp.where(cluster == ids[...], resid, 0.0).astype(jnp.bfloat16)
-    half, deep = far.shape[1], far.shape[0]
+    half, deep = far[0].shape[1], clusters // 2
     columns = pl.ds(pl.multiple_of((1 - top_half()) * half, half), half)
-    far[...] = jnp.dot(picks[deep:, :], held[:, columns], preferred_element_type=jnp.float32)
-    near[...] = jnp.dot(picks[:deep, :], held[:, columns], preferred_element_type=jnp.float32)
-
-
-def keep_kernel(picks, held, *outs):
+    spread(jnp.dot(picks[deep:, :], held[:, columns], preferred_element_type=jnp.float32), far)
+
+
+def rest_kernel(picks, held, *outs):
     half, group = outs[0].shape[1], outs[0].shape[0]
+    deep = picks.shape[0] // 2
+    columns = pl.ds(pl.multiple_of((1 - top_half()) * half, half), half)
+    spread(jnp.dot(picks[:deep, :], held[:, columns], preferred_element_type=jnp.float32), outs[: deep // group])
     columns = pl.ds(pl.multiple_of(top_half() * half, half), half)
-    total = jnp.dot(picks[...], held[:, columns], preferred_element_type=jnp.float32)
-    for k, out in enumerate(outs):
-        out[...] = total[k * group : (k + 1) * group]
-
-
-def meat_kernel(scale, have, *refs):
-    got, own, other, out = refs[:-5], refs[-5:-3], refs[-3:-1], refs[-1]
+    spread(jnp.dot(picks[...], held[:, columns], preferred_element_type=jnp.float32), outs[deep // group :])
+
+
+def meat_columns(scale, left, parts, store):
+    high, low = split_two(jnp.concatenate([p[...] for p in parts], axis=0))
+    deep = jnp.concatenate([high, high], axis=0)
+    left_high = left[: left.shape[0] // 2]
+    dims = (((0,), (0,)), ((), ()))
+    half = high.shape[1]
+    block = min(256, half)
+    for n in range(half // block):
+        part = slice(n * block, (n + 1) * block)
+        total = lax.dot_general(
+            left, deep[:, part], dims, preferred_element_type=jnp.float32
+        ) + lax.dot_general(left_high, low[:, part], dims, preferred_element_type=jnp.float32)
+        store(n, total * scale)
+
+
+def own_kernel(scale, have, *refs):
+    refs, (out, left) = refs[:-2], refs[-2:]
+    got, own = refs[:-2], refs[-2:]
     _, high, _, gr = position()
     rows = jnp.where((gr ^ high) % 2 == 0, have[...], jnp.concatenate([ref[...] for ref in got], axis=0))
-    left_high, left_low = split_two(rows)
-    left = jnp.concatenate([left_high, left_low], axis=0)
-    half = own[0].shape[1]
-    for k, part in enumerate((own, other)):
-        high, low = split_two(jnp.concatenate([p[...] for p in part], axis=0))
-        dims = (((0,), (0,)), ((), ()))
-        total = lax.dot_general(
-            left, jnp.concatenate([high, high], axis=0), dims, preferred_element_type=jnp.float32
-        ) + lax.dot_general(left_high, low, dims, preferred_element_type=jnp.float32)
-        spot = top_half() if k == 0 else 1 - top_half()
-        out[:, pl.ds(pl.multiple_of(spot * half, half), half)] = total * scale
+    both = jnp.concatenate(split_two(rows), axis=0)
+    left[...] = both
+
+    def store(n, value):
+        out[n] = value
+
+    meat_columns(scale, both, own, store)
+
+
+def other_kernel(scale, first, left, *refs):
+    other, (out, held, sems) = refs[:-3], refs[-3:]
+    parts, _, block = held.shape
+    copies = []
+
+    def send(source, n, spot):
+        columns = pl.ds(pl.multiple_of((spot * parts + n) * block, block), block)
+        copies.append(pltpu.make_async_copy(source.at[n], out.at[:, columns], sems.at[len(copies)]))
+        copies[-1].start()
+
+    def store(n, value):
+        held[n] = value
+        send(held, n, 1 - top_half())
+
+    for n in range(parts):
+        send(first, n, top_half())
+    meat_columns(scale, left[...], other, store)
+    for copy in copies:
+        copy.wait()
 
 
 def exchange(value, cal_bits, gr_bits, n_cal, n_gr):
@@ -131,32 +171,27 @@
         (jax.ShapeDtypeStruct((1, rows), f32), jax.ShapeDtypeStruct((rows, width), bf16)),
         (features, coef), 0, "linear", 2 * rows * width, {0: 1},
     )
-    linears = [lin] + [swap(lin, 0, k) for k in range(1, n_gr)]
+    linears = [lin] + [swap(lin, 0, k) for k in range(n_gr - 1, 0, -1)]
 
     half = width // 2
     deep = clusters // 2
     group = clusters // n_gr
     flat = [v.reshape(1, rows) for v in (log_exposure, claims, cluster_id, period)]
     work = 2 * rows * deep * half
-    far, near, picks = kernel(
+    score = jax.ShapeDtypeStruct((group, half), f32)
+    *far, picks = kernel(
         functools.partial(picks_kernel, per_dev, group, n_gr),
-        (
-            jax.ShapeDtypeStruct((deep, half), f32),
-            jax.ShapeDtypeStruct((deep, half), f32),
-            jax.ShapeDtypeStruct((clusters, rows), bf16),
-        ),
+        (score,) * (n_gr // 2) + (jax.ShapeDtypeStruct((clusters, rows), bf16),),
         (period_effect, *linears, *flat, features),
-        1, "send", 2 * work,
-    )
-    there = [swap(near, fan // 2, 0), swap(far, fan // 2, 0)]
-    kept = kernel(
-        keep_kernel, tuple(jax.ShapeDtypeStruct((group, half), f32) for _ in range(n_gr)),
-        (picks, features), 0, "keep", 2 * work,
-    )
+        1, "send_far", work,
+    )
+    far = [swap(value, fan // 2, 0) for value in far]
+    rest = kernel(rest_kernel, (score,) * (n_gr // 2 + n_gr), (picks, features), 0, "rest", 3 * work)
+    there = [swap(value, fan // 2, 0) for value in rest[: n_gr // 2]] + far
+    kept = rest[n_gr // 2 :]
     parts = []
     for k in range(n_gr):
-        start = k * group % deep
-        part = kept[k] + there[k * group // deep][start : start + group]
+        part = kept[k] + there[k]
         bits = fan // 4
         while bits:
             size = part.shape[1] // 2
@@ -166,11 +201,12 @@
             bits //= 2
         parts.append(part)
 
-    arrived = [swap(parts[k], k * fan, 0) for k in range(n_gr - 1, 0, -1)]
-    owned = parts[0]
-    for part in arrived[::-1]:
-        owned = owned + part
-    gathered = [owned] + [swap(owned, k * fan, 0) for k in range(n_gr - 1, 0, -1)][::-1]
+    arrived = {k: swap(parts[k], k * fan, 0) for k in range(n_gr - 1, 0, -1)}
+    owned = lax.optimization_barrier(arrived[n_gr // 2] + arrived[n_gr // 2 + 1])
+    for k in [*range(n_gr // 2 + 2, n_gr), *range(1, n_gr // 2)]:
+        owned = owned + arrived[k]
+    owned = owned + parts[0]
+    gathered = [owned] + [swap(owned, k * fan, 0) for k in range(n_gr - 1, 0, -1)]
     blocks = [gathered[0], jnp.concatenate(gathered[1:], axis=0)]
     sides, others = [], []
     for side in blocks:
@@ -203,12 +239,25 @@
         bits //= 2
     got = [swap(have[k * group : (k + 1) * group], 0, 1) for k in range(n_gr)]
     scale = 1.0 / (rows * n_cal)
-    return kernel(
-        functools.partial(meat_kernel, scale),
-        jax.ShapeDtypeStruct((blocks[0].shape[1], width), f32),
-        (have, *got, *sides, *others),
-        0, "meat", 6 * clusters * width * blocks[0].shape[1],
-    )
+    wide, block = have.shape[1], min(256, half)
+    parts = half // block
+    work = 6 * clusters * half * wide
+    first, left = kernel(
+        functools.partial(own_kernel, scale),
+        (jax.ShapeDtypeStruct((parts, wide, block), f32), jax.ShapeDtypeStruct((2 * clusters, wide), bf16)),
+        (have, *got, *sides), 0, "meat_own", work,
+    )
+    args = (first, left, *others)
+    return pl.pallas_call(
+        functools.partial(other_kernel, scale),
+        out_shape=jax.ShapeDtypeStruct((wide, width), f32),
+        in_specs=[VMEM] * len(args),
+        out_specs=ANY,
+        scratch_shapes=[pltpu.VMEM((parts, wide, block), f32), pltpu.SemaphoreType.DMA((2 * parts,))],
+        compiler_params=pltpu.CompilerParams(vmem_limit_bytes=LIMIT),
+        cost_estimate=pl.CostEstimate(flops=work, bytes_accessed=4 * wide * width, transcendentals=0),
+        name="meat_other",
+    )(*args)
 
 
 def solution(mesh):

time: 45 us -> 42.4 us (0.942)
  waiting for transfers between devices: 18.3 us -> 13.1 us
  starting transfers between devices: 19.1 us -> 21.9 us
    ppermute x17 -> x19, waiting for transfers between devices: 16.1 us -> 10.7 us  [exchange(): return lax.ppermute(value, AXES, pairs)]
    ppermute x17 -> x19, starting transfers between devices: 18.2 us -> 21.3 us  [exchange(): return lax.ppermute(value, AXES, pairs)]
    pallas_call x4, Pallas kernels: 4.84 us -> 3.24 us  [kernel(): return call(*args)]
    pallas_call x0 -> x1, Pallas kernels: none -> 1.47 us  [per_device(): pl.pallas_call(functools.partial(other_kernel, scale), out_shape=jax.Shap...]
  transfers between devices with their start and end apart: 18 -> 20, of which waited for: 9 -> 14; matrix products, arithmetic and copies ran while one was open for 0% -> 0% of each run, Pallas kernels for 1% -> 3%
where the time goes in v3:
time: 42.4 us; the launch traced here: 42.3 us
  starting transfers between devices  21.9 us (52%)
  waiting for transfers between devices  13.1 us (31%)
  Pallas kernels  4.71 us (11%)
  local copies, waits for them, and re-layouts  2.27 us (5%)
    ppermute x19, starting transfers between devices, exchange(): return lax.ppermute(value, AXES, pairs)  21.3 us
    ppermute x19, waiting for transfers between devices, exchange(): return lax.ppermute(value, AXES, pairs)  10.7 us
    pallas_call x4, Pallas kernels, kernel(): return call(*args)  3.24 us
    ppermute x1, waiting for transfers between devices, per_device(): got = lax.ppermute(have, AXES, pairs)  2.43 us
    unnamed x15, local copies, waits for them, and re-layouts  2.24 us
    pallas_call x1, Pallas kernels, per_device(): pl.pallas_call(functools.partial(other_kernel, scale), out_shape=jax.Shap...  1.47 us
  transfers between devices with their start and end apart: 20, of which 14 were waited for; matrix products, arithmetic and copies ran while one was open for 0% of the time, Pallas kernels for 3%

profile of v3, /device:TPU:0, one launch (start us, length us, event | category | flops | bytes accessed | tf_op | source)
XLA Modules:
  0.0 42.3 jit_solution(6888717262785250019)
XLA Ops:
  0.0 0.0 copy-start.4
  0.0 2.2 %copy.13.held = bf16[2048,1024]{1,0:T(8,128)(2,1)S(1)} copy(bf16[2048,1024]{1,0:T(8,128)(2,1)} %param.7) | data formatting | bytes 8388608
  2.2 0.0 copy-done.4
  2.2 0.0 copy-start
  2.2 0.0 copy-start.1
  2.2 0.0 copy-start.2
  2.2 0.0 copy-start.3
  2.2 0.0 copy-start.5
  2.2 0.9 %linear.1 = (f32[1,2048]{1,0:T(1,128)S(1)}, bf16[2048,1024]{1,0:T(8,128)(2,1)S(1)}) custom-call(bf16[2048,1024]{1,0:T(8,128)(2,1)S(1)} %copy.13.held, bf16[1024]{0:T(1024)(128)(2,1)S(1)} %copy-done.4), custom_call_target="tpu_custom_call", output_to_operand_aliasing={{1}: (0, {})} | custom-call | flops 4194304 | bytes 16384 | tf_op jit(solution)/shard_map/linear/pallas_call | solution.py:166
  3.1 2.4 %collective-permute-start = (f32[1,2048]{1,0:T(1,128)S(1)}, f32[1,2048]{1,0:T(1,128)S(1)}, u32[]{:S(2)}, u32[]{:S(2)}) collective-permute-start(f32[1,2048]{1,0:T(1,128)S(1)} %get-tuple-element.20.refs_0_), channel_id=1, source_target_pairs={{0,3},{1,2},{2,1},{3,0},{4,7},{5,6},{6,5},{7,4},{8,11},{9,10},{10,... | collective-permute-start | bytes 24584 | tf_op jit(solution)/shard_map/ppermute | solution.py:141
  5.6 0.6 %collective-permute-start.1 = (f32[1,2048]{1,0:T(1,128)S(1)}, f32[1,2048]{1,0:T(1,128)S(1)}, u32[]{:S(2)}, u32[]{:S(2)}) collective-permute-start(f32[1,2048]{1,0:T(1,128)S(1)} %get-tuple-element.20.refs_0_), channel_id=1, source_target_pairs={{0,2},{1,3},{2,0},{3,1},{4,6},{5,7},{6,4},{7,5},{8,10},{9,11},{10,... | collective-permute-start | bytes 24584 | tf_op jit(solution)/shard_map/ppermute | solution.py:141
  6.2 0.0 collective-permute-start.2
  6.3 0.7 %collective-permute-done.refs_1_ = f32[1,2048]{1,0:T(1,128)S(1)} collective-permute-done((f32[1,2048]{1,0:T(1,128)S(1)}, f32[1,2048]{1,0:T(1,128)S(1)}, u32[]{:S(2)}, u32[]{:S(2)}) %collective-permute-start) | collective-permute-done | bytes 8224 | tf_op jit(solution)/shard_map/ppermute | solution.py:141
  7.0 2.3 %collective-permute-done.1.refs_2_ = f32[1,2048]{1,0:T(1,128)S(1)} collective-permute-done((f32[1,2048]{1,0:T(1,128)S(1)}, f32[1,2048]{1,0:T(1,128)S(1)}, u32[]{:S(2)}, u32[]{:S(2)}) %collective-permute-start.1) | collective-permute-done | bytes 8224 | tf_op jit(solution)/shard_map/ppermute | solution.py:141
  9.2 0.0 collective-permute-done.2.refs_3_
  9.2 0.0 copy-done
  9.2 0.0 copy-done.1
  9.2 0.0 copy-done.2
  9.3 0.0 copy-done.3
  9.3 0.0 copy-done.5
  9.3 1.0 %send_far.1 = (f32[32,512]{1,0:T(8,128)S(1)}, f32[32,512]{1,0:T(8,128)S(1)}, bf16[128,2048]{1,0:T(8,128)(2,1)S(1)}) custom-call(f32[16]{0:T(128)S(1)} %copy-done.5, f32[1,2048]{1,0:T(1,128)S(1)} %get-tuple-element.20.refs_0_, f32[1,2048]{1,0:T(1,128)S(1)} %collective-permute-done.refs_1_, f32[1,2048]{1,0:T(1,128)S(1)} %collective-permute-done.1.refs_2_, ...), custom_call_target="tpu_custom_call" | custom-call | flops 134217728 | bytes 524288 | tf_op jit(solution)/shard_map/send_far/pallas_call | solution.py:166
  10.3 1.6 %collective-permute-start.5 = (f32[32,512]{1,0:T(8,128)S(1)}, f32[32,512]{1,0:T(8,128)S(1)}, u32[]{:S(2)}, u32[]{:S(2)}) collective-permute-start(f32[32,512]{1,0:T(8,128)S(1)} %get-tuple-element.26), channel_id=1, source_target_pairs={{0,4},{1,5},{2,6},{3,7},{4,0},{5,1},{6,2},{7,3},{8,12},{9,13},{10,... | collective-permute-start | bytes 196616 | tf_op jit(solution)/shard_map/ppermute | solution.py:141
  11.9 0.5 %collective-permute-start.3 = (f32[32,512]{1,0:T(8,128)S(1)}, f32[32,512]{1,0:T(8,128)S(1)}, u32[]{:S(2)}, u32[]{:S(2)}) collective-permute-start(f32[32,512]{1,0:T(8,128)S(1)} %get-tuple-element.24), channel_id=1, source_target_pairs={{0,4},{1,5},{2,6},{3,7},{4,0},{5,1},{6,2},{7,3},{8,12},{9,13},{10,... | collective-permute-start | bytes 196616 | tf_op jit(solution)/shard_map/ppermute | solution.py:141
  12.4 0.8 %rest.1 = (f32[32,512]{1,0:T(8,128)S(1)}, f32[32,512]{1,0:T(8,128)S(1)}, f32[32,512]{1,0:T(8,128)S(1)}, f32[32,512]{1,0:T(8,128)S(1)}, f32[32,512]{1,0:T(8,128)S(1)}, /*index=5*/f32[32,512]{1,0:T(8,128)S(1)}) custom-call(bf16[128,2048]{1,0:T(8,128)(2,1)S(1)} %get-tuple-element.22.picks, bf16[2048,1024]{1,0:T(8,128)(2,1)S(1)} %get-tuple-element.21.refs_8_.held), custom_call_target="tpu_custom_call" | custom-call | flops 402653184 | bytes 1572864 | tf_op jit(solution)/shard_map/rest/pallas_call | solution.py:166
  13.2 1.6 %collective-permute-start.7 = (f32[32,512]{1,0:T(8,128)S(1)}, f32[32,512]{1,0:T(8,128)S(1)}, u32[]{:S(2)}, u32[]{:S(2)}) collective-permute-start(f32[32,512]{1,0:T(8,128)S(1)} %get-tuple-element.28), channel_id=1, source_target_pairs={{0,4},{1,5},{2,6},{3,7},{4,0},{5,1},{6,2},{7,3},{8,12},{9,13},{10,... | collective-permute-start | bytes 196616 | tf_op jit(solution)/shard_map/ppermute | solution.py:141
  14.8 0.5 %collective-permute-start.9 = (f32[32,512]{1,0:T(8,128)S(1)}, f32[32,512]{1,0:T(8,128)S(1)}, u32[]{:S(2)}, u32[]{:S(2)}) collective-permute-start(f32[32,512]{1,0:T(8,128)S(1)} %get-tuple-element.30), channel_id=1, source_target_pairs={{0,4},{1,5},{2,6},{3,7},{4,0},{5,1},{6,2},{7,3},{8,12},{9,13},{10,... | collective-permute-start | bytes 196616 | tf_op jit(solution)/shard_map/ppermute | solution.py:141
  15.3 0.0 collective-permute-done.5
  15.4 3.7 %collective-permute-start.6 = (f32[32,512]{1,0:T(8,128)S(1)}, f32[32,512]{1,0:T(8,128)S(1)}, u32[]{:S(2)}, u32[]{:S(2)}) collective-permute-start(f32[32,512]{1,0:T(8,128)S(1)} %add.23), channel_id=1, source_target_pairs={{0,24},{1,25},{2,26},{3,27},{4,28},{5,29},{6,30},{7,31},{8,16},{9,... | collective-permute-start | bytes 196616 | tf_op jit(solution)/shard_map/ppermute | solution.py:141
  19.0 0.0 collective-permute-done.3
  19.0 0.6 %collective-permute-start.4 = (f32[32,512]{1,0:T(8,128)S(1)}, f32[32,512]{1,0:T(8,128)S(1)}, u32[]{:S(2)}, u32[]{:S(2)}) collective-permute-start(f32[32,512]{1,0:T(8,128)S(1)} %add.22), channel_id=1, source_target_pairs={{0,16},{1,17},{2,18},{3,19},{4,20},{5,21},{6,22},{7,23},{8,24},{9,... | collective-permute-start | bytes 196616 | tf_op jit(solution)/shard_map/ppermute | solution.py:141
  19.6 0.0 collective-permute-done.7
  19.6 1.6 %collective-permute-start.8 = (f32[32,512]{1,0:T(8,128)S(1)}, f32[32,512]{1,0:T(8,128)S(1)}, u32[]{:S(2)}, u32[]{:S(2)}) collective-permute-start(f32[32,512]{1,0:T(8,128)S(1)} %add.25), channel_id=1, source_target_pairs={{0,8},{1,9},{2,10},{3,11},{4,12},{5,13},{6,14},{7,15},{8,0},{9,1},... | collective-permute-start | bytes 196616 | tf_op jit(solution)/shard_map/ppermute | solution.py:141
  21.3 0.3 collective-permute-done.6
  21.6 2.8 %collective-permute-done.4 = f32[32,512]{1,0:T(8,128)S(1)} collective-permute-done((f32[32,512]{1,0:T(8,128)S(1)}, f32[32,512]{1,0:T(8,128)S(1)}, u32[]{:S(2)}, u32[]{:S(2)}) %collective-permute-start.4) | collective-permute-done | bytes 65568 | tf_op jit(solution)/shard_map/ppermute | solution.py:141
  24.4 0.0 collective-permute-done.9
  24.4 0.3 collective-permute-done.8
  24.7 2.2 %collective-permute-start.10 = (f32[32,512]{1,0:T(8,128)S(1)}, f32[32,512]{1,0:T(8,128)S(1)}, u32[]{:S(2)}, u32[]{:S(2)}) collective-permute-start(f32[32,512]{1,0:T(8,128)S(1)} %add_add_fusion.refs_4_), channel_id=1, source_target_pairs={{0,24},{1,25},{2,26},{3,27},{4,28},{5,29},{6,30},{7,31},{8,16},{9,... | collective-permute-start | bytes 196616 | tf_op jit(solution)/shard_map/ppermute | solution.py:141
  26.9 0.2 collective-permute-start.11
  27.1 2.1 %collective-permute-start.12 = (f32[32,512]{1,0:T(8,128)S(1)}, f32[32,512]{1,0:T(8,128)S(1)}, u32[]{:S(2)}, u32[]{:S(2)}) collective-permute-start(f32[32,512]{1,0:T(8,128)S(1)} %add_add_fusion.refs_4_), channel_id=1, source_target_pairs={{0,8},{1,9},{2,10},{3,11},{4,12},{5,13},{6,14},{7,15},{8,0},{9,1},... | collective-permute-start | bytes 196616 | tf_op jit(solution)/shard_map/ppermute | solution.py:141
  29.1 1.2 %collective-permute-start.13 = (f32[32,512]{1,0:T(8,128)S(1)}, f32[32,512]{1,0:T(8,128)S(1)}, u32[]{:S(2)}, u32[]{:S(2)}) collective-permute-start(f32[32,512]{1,0:T(8,128)S(1)} %add_add_fusion.refs_4_), channel_id=1, source_target_pairs={{0,4},{1,5},{2,6},{3,7},{4,0},{5,1},{6,2},{7,3},{8,12},{9,13},{10,... | collective-permute-start | bytes 196616 | tf_op jit(solution)/shard_map/ppermute | solution.py:141
  30.3 1.0 %collective-permute-done.10 = f32[32,512]{1,0:T(8,128)S(1)} collective-permute-done((f32[32,512]{1,0:T(8,128)S(1)}, f32[32,512]{1,0:T(8,128)S(1)}, u32[]{:S(2)}, u32[]{:S(2)}) %collective-permute-start.10) | collective-permute-done | bytes 65568 | tf_op jit(solution)/shard_map/ppermute | solution.py:141
  31.3 1.4 %collective-permute-done.11 = f32[32,512]{1,0:T(8,128)S(1)} collective-permute-done((f32[32,512]{1,0:T(8,128)S(1)}, f32[32,512]{1,0:T(8,128)S(1)}, u32[]{:S(2)}, u32[]{:S(2)}) %collective-permute-start.11) | collective-permute-done | bytes 65568 | tf_op jit(solution)/shard_map/ppermute | solution.py:141
  32.7 0.0 collective-permute-done.12
  32.7 0.7 %collective-permute-done.13.refs_0_ = f32[32,512]{1,0:T(8,128)S(1)} collective-permute-done((f32[32,512]{1,0:T(8,128)S(1)}, f32[32,512]{1,0:T(8,128)S(1)}, u32[]{:S(2)}, u32[]{:S(2)}) %collective-permute-start.13) | collective-permute-done | bytes 65568 | tf_op jit(solution)/shard_map/ppermute | solution.py:141
  33.4 0.6 %collective-permute-start.14 = (f32[128,512]{1,0:T(8,128)S(1)}, f32[128,512]{1,0:T(8,128)S(1)}, u32[]{:S(2)}, u32[]{:S(2)}) collective-permute-start(f32[128,512]{1,0:T(8,128)S(1)} %pad_maximum_fusion), channel_id=1, source_target_pairs={{0,2},{1,0},{2,3},{3,1},{4,6},{5,4},{6,7},{7,5},{8,9},{9,11},{10,8... | collective-permute-start | bytes 786440 | tf_op jit(solution)/shard_map/ppermute | solution.py:237
  34.1 1.4 %collective-permute-start.19 = (f32[96,512]{1,0:T(8,128)S(1)}, f32[96,512]{1,0:T(8,128)S(1)}, u32[]{:S(2)}, u32[]{:S(2)}) collective-permute-start(f32[96,512]{1,0:T(8,128)S(1)} %constant_dynamic-update-slice_fusion.refs_5_), channel_id=1, source_target_pairs={{0,4},{1,5},{2,6},{3,7},{4,0},{5,1},{6,2},{7,3},{8,12},{9,13},{10,... | collective-permute-start | bytes 589832 | tf_op jit(solution)/shard_map/ppermute | solution.py:141
  35.5 2.4 %collective-permute-done.14 = f32[128,512]{1,0:T(8,128)S(1)} collective-permute-done((f32[128,512]{1,0:T(8,128)S(1)}, f32[128,512]{1,0:T(8,128)S(1)}, u32[]{:S(2)}, u32[]{:S(2)}) %collective-permute-start.14) | collective-permute-done | bytes 262176 | tf_op jit(solution)/shard_map/ppermute | solution.py:237
  38.0 0.1 collective-permute-start.15
  38.1 0.5 %collective-permute-start.16 = (f32[32,512]{1,0:T(8,128)S(1)}, f32[32,512]{1,0:T(8,128)S(1)}, u32[]{:S(2)}, u32[]{:S(2)}) collective-permute-start(f32[32,512]{1,0:T(8,128)S(1)} %get-tuple-element.37), channel_id=1, source_target_pairs={{0,1},{1,0},{2,3},{3,2},{4,5},{5,4},{6,7},{7,6},{8,9},{9,8},{10,11... | collective-permute-start | bytes 196616 | tf_op jit(solution)/shard_map/ppermute | solution.py:141
  38.6 0.1 collective-permute-start.17
  38.7 0.4 %collective-permute-start.18 = (f32[32,512]{1,0:T(8,128)S(1)}, f32[32,512]{1,0:T(8,128)S(1)}, u32[]{:S(2)}, u32[]{:S(2)}) collective-permute-start(f32[32,512]{1,0:T(8,128)S(1)} %get-tuple-element.35), channel_id=1, source_target_pairs={{0,1},{1,0},{2,3},{3,2},{4,5},{5,4},{6,7},{7,6},{8,9},{9,8},{10,11... | collective-permute-start | bytes 196616 | tf_op jit(solution)/shard_map/ppermute | solution.py:141
  39.1 0.2 collective-permute-done.15.refs_0_
  39.3 0.2 collective-permute-done.16.refs_1_
  39.5 0.4 collective-permute-done.17.refs_2_
  39.8 0.2 collective-permute-done.18.refs_3_
  40.0 0.5 %meat_own.1 = (f32[2,512,256]{2,1,0:T(8,128)S(1)}, bf16[256,512]{1,0:T(8,128)(2,1)S(1)}) custom-call(f32[128,512]{1,0:T(8,128)S(1)} %broadcast_select_fusion.have, f32[32,512]{1,0:T(8,128)S(1)} %collective-permute-done.15.refs_0_, f32[32,512]{1,0:T(8,128)S(1)} %collective-permute-done.16.refs_1_, f32[32,512]{1,0:T(8,128)S(1)} %collective-permute-done.17.refs_2_, ...), custom_call_target="tpu_custom_call" | custom-call | flops 201326592 | bytes 786432 | tf_op jit(solution)/shard_map/meat_own/pallas_call | solution.py:166
  40.5 0.3 collective-permute-done.19.refs_1_
  40.8 1.5 %meat_other.1 = f32[512,1024]{1,0:T(8,128)} custom-call(f32[2,512,256]{2,1,0:T(8,128)S(1)} %get-tuple-element.32.first, bf16[256,512]{1,0:T(8,128)(2,1)S(1)} %get-tuple-element.33.left, f32[32,512]{1,0:T(8,128)S(1)} %collective-permute-done.13.refs_0_, f32[96,512]{1,0:T(8,128)S(1)} %collective-permute-done.19.refs_1_), custom_call_target="tpu_custom_call" | custom-call | flops 201326592 | bytes 2097152 | tf_op jit(solution)/shard_map/meat_other/pallas_call | solution.py:251
  (11 shorter events, 0.2 us)
Async XLA Ops:
  0.0 2.2 %copy-start.4 = (bf16[1024]{0:T(1024)(128)(2,1)S(1)}, bf16[1024]{0:T(1024)(128)(2,1)}, u32[]{:S(2)}) copy-start(bf16[1024]{0:T(1024)(128)(2,1)} %coef.1) | copy-start | bytes 6148
  2.2 7.0 %copy-start = (f32[2048]{0:T(1024)S(1)}, f32[2048]{0:T(1024)}, u32[]{:S(2)}) copy-start(f32[2048]{0:T(1024)} %param.9) | copy-start | bytes 24580
  2.2 7.0 %copy-start.1 = (f32[2048]{0:T(1024)S(1)}, f32[2048]{0:T(1024)}, u32[]{:S(2)}) copy-start(f32[2048]{0:T(1024)} %param.10) | copy-start | bytes 24580
  2.2 7.0 %copy-start.2 = (s32[2048]{0:T(1024)S(1)}, s32[2048]{0:T(1024)}, u32[]{:S(2)}) copy-start(s32[2048]{0:T(1024)} %param.11) | copy-start | bytes 24580
  2.2 7.0 %copy-start.3 = (s32[2048]{0:T(1024)S(1)}, s32[2048]{0:T(1024)}, u32[]{:S(2)}) copy-start(s32[2048]{0:T(1024)} %param.12) | copy-start | bytes 24580
  2.2 7.0 %copy-start.5 = (f32[16]{0:T(128)S(1)}, f32[16]{0:T(128)}, u32[]{:S(2)}) copy-start(f32[16]{0:T(128)} %effect.1) | copy-start | bytes 196
  3.1 3.8 %collective-permute-start = (f32[1,2048]{1,0:T(1,128)S(1)}, f32[1,2048]{1,0:T(1,128)S(1)}, u32[]{:S(2)}, u32[]{:S(2)}) collective-permute-start(f32[1,2048]{1,0:T(1,128)S(1)} %get-tuple-element.20.refs_0_), channel_id=1, source_target_pairs={{0,3},{1,2},{2,1},{3,0},{4,7},{5,6},{6,5},{7,4},{8,11},{9,10},{10,... | collective-permute-start | bytes 24584 | tf_op jit(solution)/shard_map/ppermute | solution.py:141
  5.6 3.7 %collective-permute-start.1 = (f32[1,2048]{1,0:T(1,128)S(1)}, f32[1,2048]{1,0:T(1,128)S(1)}, u32[]{:S(2)}, u32[]{:S(2)}) collective-permute-start(f32[1,2048]{1,0:T(1,128)S(1)} %get-tuple-element.20.refs_0_), channel_id=1, source_target_pairs={{0,2},{1,3},{2,0},{3,1},{4,6},{5,7},{6,4},{7,5},{8,10},{9,11},{10,... | collective-permute-start | bytes 24584 | tf_op jit(solution)/shard_map/ppermute | solution.py:141
  6.2 3.0 %collective-permute-start.2 = (f32[1,2048]{1,0:T(1,128)S(1)}, f32[1,2048]{1,0:T(1,128)S(1)}, u32[]{:S(2)}, u32[]{:S(2)}) collective-permute-start(f32[1,2048]{1,0:T(1,128)S(1)} %get-tuple-element.20.refs_0_), channel_id=1, source_target_pairs={{0,1},{1,0},{2,3},{3,2},{4,5},{5,4},{6,7},{7,6},{8,9},{9,8},{10,11... | collective-permute-start | bytes 24584 | tf_op jit(solution)/shard_map/ppermute | solution.py:141
  10.3 5.0 %collective-permute-start.5 = (f32[32,512]{1,0:T(8,128)S(1)}, f32[32,512]{1,0:T(8,128)S(1)}, u32[]{:S(2)}, u32[]{:S(2)}) collective-permute-start(f32[32,512]{1,0:T(8,128)S(1)} %get-tuple-element.26), channel_id=1, source_target_pairs={{0,4},{1,5},{2,6},{3,7},{4,0},{5,1},{6,2},{7,3},{8,12},{9,13},{10,... | collective-permute-start | bytes 196616 | tf_op jit(solution)/shard_map/ppermute | solution.py:141
  11.9 7.1 %collective-permute-start.3 = (f32[32,512]{1,0:T(8,128)S(1)}, f32[32,512]{1,0:T(8,128)S(1)}, u32[]{:S(2)}, u32[]{:S(2)}) collective-permute-start(f32[32,512]{1,0:T(8,128)S(1)} %get-tuple-element.24), channel_id=1, source_target_pairs={{0,4},{1,5},{2,6},{3,7},{4,0},{5,1},{6,2},{7,3},{8,12},{9,13},{10,... | collective-permute-start | bytes 196616 | tf_op jit(solution)/shard_map/ppermute | solution.py:141
  13.2 6.4 %collective-permute-start.7 = (f32[32,512]{1,0:T(8,128)S(1)}, f32[32,512]{1,0:T(8,128)S(1)}, u32[]{:S(2)}, u32[]{:S(2)}) collective-permute-start(f32[32,512]{1,0:T(8,128)S(1)} %get-tuple-element.28), channel_id=1, source_target_pairs={{0,4},{1,5},{2,6},{3,7},{4,0},{5,1},{6,2},{7,3},{8,12},{9,13},{10,... | collective-permute-start | bytes 196616 | tf_op jit(solution)/shard_map/ppermute | solution.py:141
  14.8 9.6 %collective-permute-start.9 = (f32[32,512]{1,0:T(8,128)S(1)}, f32[32,512]{1,0:T(8,128)S(1)}, u32[]{:S(2)}, u32[]{:S(2)}) collective-permute-start(f32[32,512]{1,0:T(8,128)S(1)} %get-tuple-element.30), channel_id=1, source_target_pairs={{0,4},{1,5},{2,6},{3,7},{4,0},{5,1},{6,2},{7,3},{8,12},{9,13},{10,... | collective-permute-start | bytes 196616 | tf_op jit(solution)/shard_map/ppermute | solution.py:141
  15.4 6.2 %collective-permute-start.6 = (f32[32,512]{1,0:T(8,128)S(1)}, f32[32,512]{1,0:T(8,128)S(1)}, u32[]{:S(2)}, u32[]{:S(2)}) collective-permute-start(f32[32,512]{1,0:T(8,128)S(1)} %add.23), channel_id=1, source_target_pairs={{0,24},{1,25},{2,26},{3,27},{4,28},{5,29},{6,30},{7,31},{8,16},{9,... | collective-permute-start | bytes 196616 | tf_op jit(solution)/shard_map/ppermute | solution.py:141
  19.0 5.3 %collective-permute-start.4 = (f32[32,512]{1,0:T(8,128)S(1)}, f32[32,512]{1,0:T(8,128)S(1)}, u32[]{:S(2)}, u32[]{:S(2)}) collective-permute-start(f32[32,512]{1,0:T(8,128)S(1)} %add.22), channel_id=1, source_target_pairs={{0,16},{1,17},{2,18},{3,19},{4,20},{5,21},{6,22},{7,23},{8,24},{9,... | collective-permute-start | bytes 196616 | tf_op jit(solution)/shard_map/ppermute | solution.py:141
  19.6 5.0 %collective-permute-start.8 = (f32[32,512]{1,0:T(8,128)S(1)}, f32[32,512]{1,0:T(8,128)S(1)}, u32[]{:S(2)}, u32[]{:S(2)}) collective-permute-start(f32[32,512]{1,0:T(8,128)S(1)} %add.25), channel_id=1, source_target_pairs={{0,8},{1,9},{2,10},{3,11},{4,12},{5,13},{6,14},{7,15},{8,0},{9,1},... | collective-permute-start | bytes 196616 | tf_op jit(solution)/shard_map/ppermute | solution.py:141
  24.7 6.6 %collective-permute-start.10 = (f32[32,512]{1,0:T(8,128)S(1)}, f32[32,512]{1,0:T(8,128)S(1)}, u32[]{:S(2)}, u32[]{:S(2)}) collective-permute-start(f32[32,512]{1,0:T(8,128)S(1)} %add_add_fusion.refs_4_), channel_id=1, source_target_pairs={{0,24},{1,25},{2,26},{3,27},{4,28},{5,29},{6,30},{7,31},{8,16},{9,... | collective-permute-start | bytes 196616 | tf_op jit(solution)/shard_map/ppermute | solution.py:141
  26.9 5.9 %collective-permute-start.11 = (f32[32,512]{1,0:T(8,128)S(1)}, f32[32,512]{1,0:T(8,128)S(1)}, u32[]{:S(2)}, u32[]{:S(2)}) collective-permute-start(f32[32,512]{1,0:T(8,128)S(1)} %add_add_fusion.refs_4_), channel_id=1, source_target_pairs={{0,16},{1,17},{2,18},{3,19},{4,20},{5,21},{6,22},{7,23},{8,24},{9,... | collective-permute-start | bytes 196616 | tf_op jit(solution)/shard_map/ppermute | solution.py:141
  27.1 5.6 %collective-permute-start.12 = (f32[32,512]{1,0:T(8,128)S(1)}, f32[32,512]{1,0:T(8,128)S(1)}, u32[]{:S(2)}, u32[]{:S(2)}) collective-permute-start(f32[32,512]{1,0:T(8,128)S(1)} %add_add_fusion.refs_4_), channel_id=1, source_target_pairs={{0,8},{1,9},{2,10},{3,11},{4,12},{5,13},{6,14},{7,15},{8,0},{9,1},... | collective-permute-start | bytes 196616 | tf_op jit(solution)/shard_map/ppermute | solution.py:141
  29.1 4.3 %collective-permute-start.13 = (f32[32,512]{1,0:T(8,128)S(1)}, f32[32,512]{1,0:T(8,128)S(1)}, u32[]{:S(2)}, u32[]{:S(2)}) collective-permute-start(f32[32,512]{1,0:T(8,128)S(1)} %add_add_fusion.refs_4_), channel_id=1, source_target_pairs={{0,4},{1,5},{2,6},{3,7},{4,0},{5,1},{6,2},{7,3},{8,12},{9,13},{10,... | collective-permute-start | bytes 196616 | tf_op jit(solution)/shard_map/ppermute | solution.py:141
  33.4 4.5 %collective-permute-start.14 = (f32[128,512]{1,0:T(8,128)S(1)}, f32[128,512]{1,0:T(8,128)S(1)}, u32[]{:S(2)}, u32[]{:S(2)}) collective-permute-start(f32[128,512]{1,0:T(8,128)S(1)} %pad_maximum_fusion), channel_id=1, source_target_pairs={{0,2},{1,0},{2,3},{3,1},{4,6},{5,4},{6,7},{7,5},{8,9},{9,11},{10,8... | collective-permute-start | bytes 786440 | tf_op jit(solution)/shard_map/ppermute | solution.py:237
  34.1 6.7 %collective-permute-start.19 = (f32[96,512]{1,0:T(8,128)S(1)}, f32[96,512]{1,0:T(8,128)S(1)}, u32[]{:S(2)}, u32[]{:S(2)}) collective-permute-start(f32[96,512]{1,0:T(8,128)S(1)} %constant_dynamic-update-slice_fusion.refs_5_), channel_id=1, source_target_pairs={{0,4},{1,5},{2,6},{3,7},{4,0},{5,1},{6,2},{7,3},{8,12},{9,13},{10,... | collective-permute-start | bytes 589832 | tf_op jit(solution)/shard_map/ppermute | solution.py:141
  38.0 1.3 %collective-permute-start.15 = (f32[32,512]{1,0:T(8,128)S(1)}, f32[32,512]{1,0:T(8,128)S(1)}, u32[]{:S(2)}, u32[]{:S(2)}) collective-permute-start(f32[32,512]{1,0:T(8,128)S(1)} %get-tuple-element.38), channel_id=1, source_target_pairs={{0,1},{1,0},{2,3},{3,2},{4,5},{5,4},{6,7},{7,6},{8,9},{9,8},{10,11... | collective-permute-start | bytes 196616 | tf_op jit(solution)/shard_map/ppermute | solution.py:141
  38.1 1.4 %collective-permute-start.16 = (f32[32,512]{1,0:T(8,128)S(1)}, f32[32,512]{1,0:T(8,128)S(1)}, u32[]{:S(2)}, u32[]{:S(2)}) collective-permute-start(f32[32,512]{1,0:T(8,128)S(1)} %get-tuple-element.37), channel_id=1, source_target_pairs={{0,1},{1,0},{2,3},{3,2},{4,5},{5,4},{6,7},{7,6},{8,9},{9,8},{10,11... | collective-permute-start | bytes 196616 | tf_op jit(solution)/shard_map/ppermute | solution.py:141
  38.6 1.3 %collective-permute-start.17 = (f32[32,512]{1,0:T(8,128)S(1)}, f32[32,512]{1,0:T(8,128)S(1)}, u32[]{:S(2)}, u32[]{:S(2)}) collective-permute-start(f32[32,512]{1,0:T(8,128)S(1)} %get-tuple-element.36), channel_id=1, source_target_pairs={{0,1},{1,0},{2,3},{3,2},{4,5},{5,4},{6,7},{7,6},{8,9},{9,8},{10,11... | collective-permute-start | bytes 196616 | tf_op jit(solution)/shard_map/ppermute | solution.py:141
  38.7 1.3 %collective-permute-start.18 = (f32[32,512]{1,0:T(8,128)S(1)}, f32[32,512]{1,0:T(8,128)S(1)}, u32[]{:S(2)}, u32[]{:S(2)}) collective-permute-start(f32[32,512]{1,0:T(8,128)S(1)} %get-tuple-element.35), channel_id=1, source_target_pairs={{0,1},{1,0},{2,3},{3,2},{4,5},{5,4},{6,7},{7,6},{8,9},{9,8},{10,11... | collective-permute-start | bytes 196616 | tf_op jit(solution)/shard_map/ppermute | solution.py:141

commit v4 on v3

--- a/solution.py
+++ b/solution.py
@@ -55,8 +55,11 @@
     cal, high, _, _ = position()
     base = cal * per_dev
     shift = jnp.zeros(claims.shape, jnp.float32)
+    effects = effect[...].reshape(1, effect.shape[0])
+    place = lax.broadcasted_iota(jnp.int32, effects.shape, 1)
     for k in range(per_dev):
-        shift = jnp.where(period[...] == base + k, effect[base + k], shift)
+        value = jnp.sum(jnp.where(place == base + k, effects, 0.0), axis=1, keepdims=True)
+        shift = jnp.where(period[...] == base + k, value, shift)
     sums = [ref[...] for ref in refs[:terms]]
     while len(sums) > 1:
         sums = [a + b for a, b in zip(sums[::2], sums[1::2])]
@@ -171,7 +174,7 @@
         (jax.ShapeDtypeStruct((1, rows), f32), jax.ShapeDtypeStruct((rows, width), bf16)),
         (features, coef), 0, "linear", 2 * rows * width, {0: 1},
     )
-    linears = [lin] + [swap(lin, 0, k) for k in range(n_gr - 1, 0, -1)]
+    linears = [lin] + [swap(lin, 0, k) for k in [*range(n_gr // 2, n_gr), *range(1, n_gr // 2)]]
 
     half = width // 2
     deep = clusters // 2
@@ -183,7 +186,7 @@
         functools.partial(picks_kernel, per_dev, group, n_gr),
         (score,) * (n_gr // 2) + (jax.ShapeDtypeStruct((clusters, rows), bf16),),
         (period_effect, *linears, *flat, features),
-        1, "send_far", work,
+        0, "send_far", work,
     )
     far = [swap(value, fan // 2, 0) for value in far]
     rest = kernel(rest_kernel, (score,) * (n_gr // 2 + n_gr), (picks, features), 0, "rest", 3 * work)
@@ -237,7 +240,7 @@
         got = lax.ppermute(have, AXES, pairs)
         have = jnp.where((turn & bits) != 0, got, have)
         bits //= 2
-    got = [swap(have[k * group : (k + 1) * group], 0, 1) for k in range(n_gr)]
+    got = [swap(have[k * deep : (k + 1) * deep], 0, 1) for k in range(2)]
     scale = 1.0 / (rows * n_cal)
     wide, block = have.shape[1], min(256, half)
     parts = half // block

time: 42.4 us -> 42 us (level)
  Pallas kernels: 4.71 us -> 4.28 us
    ppermute x19 -> x17, waiting for transfers between devices: 10.7 us -> 11.1 us  [exchange(): return lax.ppermute(value, AXES, pairs)]
    pallas_call x4, Pallas kernels: 3.24 us -> 2.81 us  [kernel(): return call(*args)]
    ppermute x19 -> x17, starting transfers between devices: 21.3 us -> 20.9 us  [exchange(): return lax.ppermute(value, AXES, pairs)]
  transfers between devices with their start and end apart: 20 -> 18, of which waited for: 14 -> 12; matrix products, arithmetic and copies ran while one was open for 0% -> 0% of each run, Pallas kernels for 3% -> 3%
where the time goes in v4:
time: 42 us; the launch traced here: 41.8 us
  starting transfers between devices  21.5 us (51%)
  waiting for transfers between devices  13.5 us (32%)
  Pallas kernels  4.28 us (10%)
  local copies, waits for them, and re-layouts  2.27 us (5%)
    ppermute x17, starting transfers between devices, exchange(): return lax.ppermute(value, AXES, pairs)  20.9 us
    ppermute x17, waiting for transfers between devices, exchange(): return lax.ppermute(value, AXES, pairs)  11.1 us
    pallas_call x4, Pallas kernels, kernel(): return call(*args)  2.81 us
    ppermute x1, waiting for transfers between devices, per_device(): got = lax.ppermute(have, AXES, pairs)  2.4 us
    unnamed x15, local copies, waits for them, and re-layouts  2.24 us
    pallas_call x1, Pallas kernels, per_device(): pl.pallas_call(functools.partial(other_kernel, scale), out_shape=jax.Shap...  1.47 us
  transfers between devices with their start and end apart: 18, of which 12 were waited for; matrix products, arithmetic and copies ran while one was open for 0% of the time, Pallas kernels for 3%

profile of v4, /device:TPU:0, one launch (start us, length us, event | category | flops | bytes accessed | tf_op | source)
XLA Modules:
  0.0 41.8 jit_solution(11951599747133494039)
XLA Ops:
  0.0 0.0 copy-start.4
  0.0 2.2 %copy.13.held = bf16[2048,1024]{1,0:T(8,128)(2,1)S(1)} copy(bf16[2048,1024]{1,0:T(8,128)(2,1)} %param.7) | data formatting | bytes 8388608
  2.2 0.0 copy-done.4
  2.2 0.0 copy-start
  2.2 0.0 copy-start.1
  2.2 0.0 copy-start.2
  2.2 0.0 copy-start.3
  2.2 0.0 copy-start.5
  2.2 0.9 %linear.1 = (f32[1,2048]{1,0:T(1,128)S(1)}, bf16[2048,1024]{1,0:T(8,128)(2,1)S(1)}) custom-call(bf16[2048,1024]{1,0:T(8,128)(2,1)S(1)} %copy.13.held, bf16[1024]{0:T(1024)(128)(2,1)S(1)} %copy-done.4), custom_call_target="tpu_custom_call", output_to_operand_aliasing={{1}: (0, {})} | custom-call | flops 4194304 | bytes 16384 | tf_op jit(solution)/shard_map/linear/pallas_call | solution.py:169
  3.1 3.0 %collective-permute-start = (f32[1,2048]{1,0:T(1,128)S(1)}, f32[1,2048]{1,0:T(1,128)S(1)}, u32[]{:S(2)}, u32[]{:S(2)}) collective-permute-start(f32[1,2048]{1,0:T(1,128)S(1)} %get-tuple-element.20.refs_0_), channel_id=1, source_target_pairs={{0,2},{1,3},{2,0},{3,1},{4,6},{5,7},{6,4},{7,5},{8,10},{9,11},{10,... | collective-permute-start | bytes 24584 | tf_op jit(solution)/shard_map/ppermute | solution.py:144
  6.1 0.0 collective-permute-start.1
  6.1 0.2 collective-permute-start.2
  6.3 1.4 %collective-permute-done.refs_1_ = f32[1,2048]{1,0:T(1,128)S(1)} collective-permute-done((f32[1,2048]{1,0:T(1,128)S(1)}, f32[1,2048]{1,0:T(1,128)S(1)}, u32[]{:S(2)}, u32[]{:S(2)}) %collective-permute-start) | collective-permute-done | bytes 8224 | tf_op jit(solution)/shard_map/ppermute | solution.py:144
  7.8 1.4 %collective-permute-done.1.refs_2_ = f32[1,2048]{1,0:T(1,128)S(1)} collective-permute-done((f32[1,2048]{1,0:T(1,128)S(1)}, f32[1,2048]{1,0:T(1,128)S(1)}, u32[]{:S(2)}, u32[]{:S(2)}) %collective-permute-start.1) | collective-permute-done | bytes 8224 | tf_op jit(solution)/shard_map/ppermute | solution.py:144
  9.2 0.0 collective-permute-done.2.refs_3_
  9.2 0.0 copy-done
  9.2 0.0 copy-done.1
  9.2 0.0 copy-done.2
  9.2 0.0 copy-done.3
  9.3 0.0 copy-done.5
  9.3 0.6 %send_far.1 = (f32[32,512]{1,0:T(8,128)S(1)}, f32[32,512]{1,0:T(8,128)S(1)}, bf16[128,2048]{1,0:T(8,128)(2,1)S(1)}) custom-call(f32[16]{0:T(128)S(1)} %copy-done.5, f32[1,2048]{1,0:T(1,128)S(1)} %get-tuple-element.20.refs_0_, f32[1,2048]{1,0:T(1,128)S(1)} %collective-permute-done.refs_1_, f32[1,2048]{1,0:T(1,128)S(1)} %collective-permute-done.1.refs_2_, ...), custom_call_target="tpu_custom_call" | custom-call | flops 134217728 | bytes 524288 | tf_op jit(solution)/shard_map/send_far/pallas_call | solution.py:169
  9.9 1.6 %collective-permute-start.5 = (f32[32,512]{1,0:T(8,128)S(1)}, f32[32,512]{1,0:T(8,128)S(1)}, u32[]{:S(2)}, u32[]{:S(2)}) collective-permute-start(f32[32,512]{1,0:T(8,128)S(1)} %get-tuple-element.26), channel_id=1, source_target_pairs={{0,4},{1,5},{2,6},{3,7},{4,0},{5,1},{6,2},{7,3},{8,12},{9,13},{10,... | collective-permute-start | bytes 196616 | tf_op jit(solution)/shard_map/ppermute | solution.py:144
  11.5 0.5 %collective-permute-start.3 = (f32[32,512]{1,0:T(8,128)S(1)}, f32[32,512]{1,0:T(8,128)S(1)}, u32[]{:S(2)}, u32[]{:S(2)}) collective-permute-start(f32[32,512]{1,0:T(8,128)S(1)} %get-tuple-element.24), channel_id=1, source_target_pairs={{0,4},{1,5},{2,6},{3,7},{4,0},{5,1},{6,2},{7,3},{8,12},{9,13},{10,... | collective-permute-start | bytes 196616 | tf_op jit(solution)/shard_map/ppermute | solution.py:144
  12.0 0.8 %rest.1 = (f32[32,512]{1,0:T(8,128)S(1)}, f32[32,512]{1,0:T(8,128)S(1)}, f32[32,512]{1,0:T(8,128)S(1)}, f32[32,512]{1,0:T(8,128)S(1)}, f32[32,512]{1,0:T(8,128)S(1)}, /*index=5*/f32[32,512]{1,0:T(8,128)S(1)}) custom-call(bf16[128,2048]{1,0:T(8,128)(2,1)S(1)} %get-tuple-element.22.picks, bf16[2048,1024]{1,0:T(8,128)(2,1)S(1)} %get-tuple-element.21.refs_8_.held), custom_call_target="tpu_custom_call" | custom-call | flops 402653184 | bytes 1572864 | tf_op jit(solution)/shard_map/rest/pallas_call | solution.py:169
  12.8 1.6 %collective-permute-start.7 = (f32[32,512]{1,0:T(8,128)S(1)}, f32[32,512]{1,0:T(8,128)S(1)}, u32[]{:S(2)}, u32[]{:S(2)}) collective-permute-start(f32[32,512]{1,0:T(8,128)S(1)} %get-tuple-element.28), channel_id=1, source_target_pairs={{0,4},{1,5},{2,6},{3,7},{4,0},{5,1},{6,2},{7,3},{8,12},{9,13},{10,... | collective-permute-start | bytes 196616 | tf_op jit(solution)/shard_map/ppermute | solution.py:144
  14.4 0.5 %collective-permute-start.9 = (f32[32,512]{1,0:T(8,128)S(1)}, f32[32,512]{1,0:T(8,128)S(1)}, u32[]{:S(2)}, u32[]{:S(2)}) collective-permute-start(f32[32,512]{1,0:T(8,128)S(1)} %get-tuple-element.30), channel_id=1, source_target_pairs={{0,4},{1,5},{2,6},{3,7},{4,0},{5,1},{6,2},{7,3},{8,12},{9,13},{10,... | collective-permute-start | bytes 196616 | tf_op jit(solution)/shard_map/ppermute | solution.py:144
  14.9 0.0 collective-permute-done.5
  14.9 3.7 %collective-permute-start.6 = (f32[32,512]{1,0:T(8,128)S(1)}, f32[32,512]{1,0:T(8,128)S(1)}, u32[]{:S(2)}, u32[]{:S(2)}) collective-permute-start(f32[32,512]{1,0:T(8,128)S(1)} %add.23), channel_id=1, source_target_pairs={{0,24},{1,25},{2,26},{3,27},{4,28},{5,29},{6,30},{7,31},{8,16},{9,... | collective-permute-start | bytes 196616 | tf_op jit(solution)/shard_map/ppermute | solution.py:144
  18.6 0.0 collective-permute-done.3
  18.6 0.6 %collective-permute-start.4 = (f32[32,512]{1,0:T(8,128)S(1)}, f32[32,512]{1,0:T(8,128)S(1)}, u32[]{:S(2)}, u32[]{:S(2)}) collective-permute-start(f32[32,512]{1,0:T(8,128)S(1)} %add.22), channel_id=1, source_target_pairs={{0,16},{1,17},{2,18},{3,19},{4,20},{5,21},{6,22},{7,23},{8,24},{9,... | collective-permute-start | bytes 196616 | tf_op jit(solution)/shard_map/ppermute | solution.py:144
  19.2 0.0 collective-permute-done.7
  19.2 1.6 %collective-permute-start.8 = (f32[32,512]{1,0:T(8,128)S(1)}, f32[32,512]{1,0:T(8,128)S(1)}, u32[]{:S(2)}, u32[]{:S(2)}) collective-permute-start(f32[32,512]{1,0:T(8,128)S(1)} %add.25), channel_id=1, source_target_pairs={{0,8},{1,9},{2,10},{3,11},{4,12},{5,13},{6,14},{7,15},{8,0},{9,1},... | collective-permute-start | bytes 196616 | tf_op jit(solution)/shard_map/ppermute | solution.py:144
  20.8 0.3 collective-permute-done.6
  21.2 2.8 %collective-permute-done.4 = f32[32,512]{1,0:T(8,128)S(1)} collective-permute-done((f32[32,512]{1,0:T(8,128)S(1)}, f32[32,512]{1,0:T(8,128)S(1)}, u32[]{:S(2)}, u32[]{:S(2)}) %collective-permute-start.4) | collective-permute-done | bytes 65568 | tf_op jit(solution)/shard_map/ppermute | solution.py:144
  24.0 0.0 collective-permute-done.9
  24.0 0.2 collective-permute-done.8
  24.2 2.2 %collective-permute-start.10 = (f32[32,512]{1,0:T(8,128)S(1)}, f32[32,512]{1,0:T(8,128)S(1)}, u32[]{:S(2)}, u32[]{:S(2)}) collective-permute-start(f32[32,512]{1,0:T(8,128)S(1)} %add_add_fusion.refs_2_), channel_id=1, source_target_pairs={{0,24},{1,25},{2,26},{3,27},{4,28},{5,29},{6,30},{7,31},{8,16},{9,... | collective-permute-start | bytes 196616 | tf_op jit(solution)/shard_map/ppermute | solution.py:144
  26.5 0.2 collective-permute-start.11
  26.6 2.0 %collective-permute-start.12 = (f32[32,512]{1,0:T(8,128)S(1)}, f32[32,512]{1,0:T(8,128)S(1)}, u32[]{:S(2)}, u32[]{:S(2)}) collective-permute-start(f32[32,512]{1,0:T(8,128)S(1)} %add_add_fusion.refs_2_), channel_id=1, source_target_pairs={{0,8},{1,9},{2,10},{3,11},{4,12},{5,13},{6,14},{7,15},{8,0},{9,1},... | collective-permute-start | bytes 196616 | tf_op jit(solution)/shard_map/ppermute | solution.py:144
  28.7 1.2 %collective-permute-start.13 = (f32[32,512]{1,0:T(8,128)S(1)}, f32[32,512]{1,0:T(8,128)S(1)}, u32[]{:S(2)}, u32[]{:S(2)}) collective-permute-start(f32[32,512]{1,0:T(8,128)S(1)} %add_add_fusion.refs_2_), channel_id=1, source_target_pairs={{0,4},{1,5},{2,6},{3,7},{4,0},{5,1},{6,2},{7,3},{8,12},{9,13},{10,... | collective-permute-start | bytes 196616 | tf_op jit(solution)/shard_map/ppermute | solution.py:144
  29.9 0.9 %collective-permute-done.10 = f32[32,512]{1,0:T(8,128)S(1)} collective-permute-done((f32[32,512]{1,0:T(8,128)S(1)}, f32[32,512]{1,0:T(8,128)S(1)}, u32[]{:S(2)}, u32[]{:S(2)}) %collective-permute-start.10) | collective-permute-done | bytes 65568 | tf_op jit(solution)/shard_map/ppermute | solution.py:144
  30.7 1.5 %collective-permute-done.11 = f32[32,512]{1,0:T(8,128)S(1)} collective-permute-done((f32[32,512]{1,0:T(8,128)S(1)}, f32[32,512]{1,0:T(8,128)S(1)}, u32[]{:S(2)}, u32[]{:S(2)}) %collective-permute-start.11) | collective-permute-done | bytes 65568 | tf_op jit(solution)/shard_map/ppermute | solution.py:144
  32.3 0.0 collective-permute-done.12
  32.3 0.7 %collective-permute-done.13.refs_0_ = f32[32,512]{1,0:T(8,128)S(1)} collective-permute-done((f32[32,512]{1,0:T(8,128)S(1)}, f32[32,512]{1,0:T(8,128)S(1)}, u32[]{:S(2)}, u32[]{:S(2)}) %collective-permute-start.13) | collective-permute-done | bytes 65568 | tf_op jit(solution)/shard_map/ppermute | solution.py:144
  33.0 0.6 %collective-permute-start.14 = (f32[128,512]{1,0:T(8,128)S(1)}, f32[128,512]{1,0:T(8,128)S(1)}, u32[]{:S(2)}, u32[]{:S(2)}) collective-permute-start(f32[128,512]{1,0:T(8,128)S(1)} %pad_maximum_fusion), channel_id=1, source_target_pairs={{0,2},{1,0},{2,3},{3,1},{4,6},{5,4},{6,7},{7,5},{8,9},{9,11},{10,8... | collective-permute-start | bytes 786440 | tf_op jit(solution)/shard_map/ppermute | solution.py:240
  33.6 1.5 %collective-permute-start.17 = (f32[96,512]{1,0:T(8,128)S(1)}, f32[96,512]{1,0:T(8,128)S(1)}, u32[]{:S(2)}, u32[]{:S(2)}) collective-permute-start(f32[96,512]{1,0:T(8,128)S(1)} %constant_dynamic-update-slice_fusion.refs_3_), channel_id=1, source_target_pairs={{0,4},{1,5},{2,6},{3,7},{4,0},{5,1},{6,2},{7,3},{8,12},{9,13},{10,... | collective-permute-start | bytes 589832 | tf_op jit(solution)/shard_map/ppermute | solution.py:144
  35.0 2.4 %collective-permute-done.14 = f32[128,512]{1,0:T(8,128)S(1)} collective-permute-done((f32[128,512]{1,0:T(8,128)S(1)}, f32[128,512]{1,0:T(8,128)S(1)}, u32[]{:S(2)}, u32[]{:S(2)}) %collective-permute-start.14) | collective-permute-done | bytes 262176 | tf_op jit(solution)/shard_map/ppermute | solution.py:240
  37.5 0.1 collective-permute-start.15
  37.6 0.5 %collective-permute-start.16 = (f32[64,512]{1,0:T(8,128)S(1)}, f32[64,512]{1,0:T(8,128)S(1)}, u32[]{:S(2)}, u32[]{:S(2)}) collective-permute-start(f32[64,512]{1,0:T(8,128)S(1)} %get-tuple-element.35), channel_id=1, source_target_pairs={{0,1},{1,0},{2,3},{3,2},{4,5},{5,4},{6,7},{7,6},{8,9},{9,8},{10,11... | collective-permute-start | bytes 393224 | tf_op jit(solution)/shard_map/ppermute | solution.py:144
  38.1 0.8 %collective-permute-done.15.refs_0_ = f32[64,512]{1,0:T(8,128)S(1)} collective-permute-done((f32[64,512]{1,0:T(8,128)S(1)}, f32[64,512]{1,0:T(8,128)S(1)}, u32[]{:S(2)}, u32[]{:S(2)}) %collective-permute-start.15) | collective-permute-done | bytes 131104 | tf_op jit(solution)/shard_map/ppermute | solution.py:144
  38.9 0.2 collective-permute-done.16.refs_1_
  39.1 0.5 %meat_own.1 = (f32[2,512,256]{2,1,0:T(8,128)S(1)}, bf16[256,512]{1,0:T(8,128)(2,1)S(1)}) custom-call(f32[128,512]{1,0:T(8,128)S(1)} %broadcast_select_fusion.have, f32[64,512]{1,0:T(8,128)S(1)} %collective-permute-done.15.refs_0_, f32[64,512]{1,0:T(8,128)S(1)} %collective-permute-done.16.refs_1_, f32[32,512]{1,0:T(8,128)S(1)} %add_add_fusion.refs_2_, ...), custom_call_target="tpu_custom_call" | custom-call | flops 201326592 | bytes 786432 | tf_op jit(solution)/shard_map/meat_own/pallas_call | solution.py:169
  39.6 0.8 %collective-permute-done.17.refs_1_ = f32[96,512]{1,0:T(8,128)S(1)} collective-permute-done((f32[96,512]{1,0:T(8,128)S(1)}, f32[96,512]{1,0:T(8,128)S(1)}, u32[]{:S(2)}, u32[]{:S(2)}) %collective-permute-start.17) | collective-permute-done | bytes 196640 | tf_op jit(solution)/shard_map/ppermute | solution.py:144
  40.4 1.5 %meat_other.1 = f32[512,1024]{1,0:T(8,128)} custom-call(f32[2,512,256]{2,1,0:T(8,128)S(1)} %get-tuple-element.32.first, bf16[256,512]{1,0:T(8,128)(2,1)S(1)} %get-tuple-element.33.left, f32[32,512]{1,0:T(8,128)S(1)} %collective-permute-done.13.refs_0_, f32[96,512]{1,0:T(8,128)S(1)} %collective-permute-done.17.refs_1_), custom_call_target="tpu_custom_call" | custom-call | flops 201326592 | bytes 2097152 | tf_op jit(solution)/shard_map/meat_other/pallas_call | solution.py:254
  (11 shorter events, 0.2 us)
Async XLA Ops:
  0.0 2.2 %copy-start.4 = (bf16[1024]{0:T(1024)(128)(2,1)S(1)}, bf16[1024]{0:T(1024)(128)(2,1)}, u32[]{:S(2)}) copy-start(bf16[1024]{0:T(1024)(128)(2,1)} %coef.1) | copy-start | bytes 6148
  2.2 7.0 %copy-start = (f32[2048]{0:T(1024)S(1)}, f32[2048]{0:T(1024)}, u32[]{:S(2)}) copy-start(f32[2048]{0:T(1024)} %param.9) | copy-start | bytes 24580
  2.2 7.0 %copy-start.1 = (f32[2048]{0:T(1024)S(1)}, f32[2048]{0:T(1024)}, u32[]{:S(2)}) copy-start(f32[2048]{0:T(1024)} %param.10) | copy-start | bytes 24580
  2.2 7.0 %copy-start.2 = (s32[2048]{0:T(1024)S(1)}, s32[2048]{0:T(1024)}, u32[]{:S(2)}) copy-start(s32[2048]{0:T(1024)} %param.11) | copy-start | bytes 24580
  2.2 7.0 %copy-start.3 = (s32[2048]{0:T(1024)S(1)}, s32[2048]{0:T(1024)}, u32[]{:S(2)}) copy-start(s32[2048]{0:T(1024)} %param.12) | copy-start | bytes 24580
  2.2 7.0 %copy-start.5 = (f32[16]{0:T(128)S(1)}, f32[16]{0:T(128)}, u32[]{:S(2)}) copy-start(f32[16]{0:T(128)} %effect.1) | copy-start | bytes 196
  3.1 4.6 %collective-permute-start = (f32[1,2048]{1,0:T(1,128)S(1)}, f32[1,2048]{1,0:T(1,128)S(1)}, u32[]{:S(2)}, u32[]{:S(2)}) collective-permute-start(f32[1,2048]{1,0:T(1,128)S(1)} %get-tuple-element.20.refs_0_), channel_id=1, source_target_pairs={{0,2},{1,3},{2,0},{3,1},{4,6},{5,7},{6,4},{7,5},{8,10},{9,11},{10,... | collective-permute-start | bytes 24584 | tf_op jit(solution)/shard_map/ppermute | solution.py:144
  6.1 3.1 %collective-permute-start.1 = (f32[1,2048]{1,0:T(1,128)S(1)}, f32[1,2048]{1,0:T(1,128)S(1)}, u32[]{:S(2)}, u32[]{:S(2)}) collective-permute-start(f32[1,2048]{1,0:T(1,128)S(1)} %get-tuple-element.20.refs_0_), channel_id=1, source_target_pairs={{0,3},{1,2},{2,1},{3,0},{4,7},{5,6},{6,5},{7,4},{8,11},{9,10},{10,... | collective-permute-start | bytes 24584 | tf_op jit(solution)/shard_map/ppermute | solution.py:144
  6.1 3.1 %collective-permute-start.2 = (f32[1,2048]{1,0:T(1,128)S(1)}, f32[1,2048]{1,0:T(1,128)S(1)}, u32[]{:S(2)}, u32[]{:S(2)}) collective-permute-start(f32[1,2048]{1,0:T(1,128)S(1)} %get-tuple-element.20.refs_0_), channel_id=1, source_target_pairs={{0,1},{1,0},{2,3},{3,2},{4,5},{5,4},{6,7},{7,6},{8,9},{9,8},{10,11... | collective-permute-start | bytes 24584 | tf_op jit(solution)/shard_map/ppermute | solution.py:144
  9.9 5.0 %collective-permute-start.5 = (f32[32,512]{1,0:T(8,128)S(1)}, f32[32,512]{1,0:T(8,128)S(1)}, u32[]{:S(2)}, u32[]{:S(2)}) collective-permute-start(f32[32,512]{1,0:T(8,128)S(1)} %get-tuple-element.26), channel_id=1, source_target_pairs={{0,4},{1,5},{2,6},{3,7},{4,0},{5,1},{6,2},{7,3},{8,12},{9,13},{10,... | collective-permute-start | bytes 196616 | tf_op jit(solution)/shard_map/ppermute | solution.py:144
  11.5 7.1 %collective-permute-start.3 = (f32[32,512]{1,0:T(8,128)S(1)}, f32[32,512]{1,0:T(8,128)S(1)}, u32[]{:S(2)}, u32[]{:S(2)}) collective-permute-start(f32[32,512]{1,0:T(8,128)S(1)} %get-tuple-element.24), channel_id=1, source_target_pairs={{0,4},{1,5},{2,6},{3,7},{4,0},{5,1},{6,2},{7,3},{8,12},{9,13},{10,... | collective-permute-start | bytes 196616 | tf_op jit(solution)/shard_map/ppermute | solution.py:144
  12.8 6.4 %collective-permute-start.7 = (f32[32,512]{1,0:T(8,128)S(1)}, f32[32,512]{1,0:T(8,128)S(1)}, u32[]{:S(2)}, u32[]{:S(2)}) collective-permute-start(f32[32,512]{1,0:T(8,128)S(1)} %get-tuple-element.28), channel_id=1, source_target_pairs={{0,4},{1,5},{2,6},{3,7},{4,0},{5,1},{6,2},{7,3},{8,12},{9,13},{10,... | collective-permute-start | bytes 196616 | tf_op jit(solution)/shard_map/ppermute | solution.py:144
  14.4 9.6 %collective-permute-start.9 = (f32[32,512]{1,0:T(8,128)S(1)}, f32[32,512]{1,0:T(8,128)S(1)}, u32[]{:S(2)}, u32[]{:S(2)}) collective-permute-start(f32[32,512]{1,0:T(8,128)S(1)} %get-tuple-element.30), channel_id=1, source_target_pairs={{0,4},{1,5},{2,6},{3,7},{4,0},{5,1},{6,2},{7,3},{8,12},{9,13},{10,... | collective-permute-start | bytes 196616 | tf_op jit(solution)/shard_map/ppermute | solution.py:144
  14.9 6.2 %collective-permute-start.6 = (f32[32,512]{1,0:T(8,128)S(1)}, f32[32,512]{1,0:T(8,128)S(1)}, u32[]{:S(2)}, u32[]{:S(2)}) collective-permute-start(f32[32,512]{1,0:T(8,128)S(1)} %add.23), channel_id=1, source_target_pairs={{0,24},{1,25},{2,26},{3,27},{4,28},{5,29},{6,30},{7,31},{8,16},{9,... | collective-permute-start | bytes 196616 | tf_op jit(solution)/shard_map/ppermute | solution.py:144
  18.6 5.3 %collective-permute-start.4 = (f32[32,512]{1,0:T(8,128)S(1)}, f32[32,512]{1,0:T(8,128)S(1)}, u32[]{:S(2)}, u32[]{:S(2)}) collective-permute-start(f32[32,512]{1,0:T(8,128)S(1)} %add.22), channel_id=1, source_target_pairs={{0,16},{1,17},{2,18},{3,19},{4,20},{5,21},{6,22},{7,23},{8,24},{9,... | collective-permute-start | bytes 196616 | tf_op jit(solution)/shard_map/ppermute | solution.py:144
  19.2 5.0 %collective-permute-start.8 = (f32[32,512]{1,0:T(8,128)S(1)}, f32[32,512]{1,0:T(8,128)S(1)}, u32[]{:S(2)}, u32[]{:S(2)}) collective-permute-start(f32[32,512]{1,0:T(8,128)S(1)} %add.25), channel_id=1, source_target_pairs={{0,8},{1,9},{2,10},{3,11},{4,12},{5,13},{6,14},{7,15},{8,0},{9,1},... | collective-permute-start | bytes 196616 | tf_op jit(solution)/shard_map/ppermute | solution.py:144
  24.2 6.5 %collective-permute-start.10 = (f32[32,512]{1,0:T(8,128)S(1)}, f32[32,512]{1,0:T(8,128)S(1)}, u32[]{:S(2)}, u32[]{:S(2)}) collective-permute-start(f32[32,512]{1,0:T(8,128)S(1)} %add_add_fusion.refs_2_), channel_id=1, source_target_pairs={{0,24},{1,25},{2,26},{3,27},{4,28},{5,29},{6,30},{7,31},{8,16},{9,... | collective-permute-start | bytes 196616 | tf_op jit(solution)/shard_map/ppermute | solution.py:144
  26.5 5.8 %collective-permute-start.11 = (f32[32,512]{1,0:T(8,128)S(1)}, f32[32,512]{1,0:T(8,128)S(1)}, u32[]{:S(2)}, u32[]{:S(2)}) collective-permute-start(f32[32,512]{1,0:T(8,128)S(1)} %add_add_fusion.refs_2_), channel_id=1, source_target_pairs={{0,16},{1,17},{2,18},{3,19},{4,20},{5,21},{6,22},{7,23},{8,24},{9,... | collective-permute-start | bytes 196616 | tf_op jit(solution)/shard_map/ppermute | solution.py:144
  26.6 5.6 %collective-permute-start.12 = (f32[32,512]{1,0:T(8,128)S(1)}, f32[32,512]{1,0:T(8,128)S(1)}, u32[]{:S(2)}, u32[]{:S(2)}) collective-permute-start(f32[32,512]{1,0:T(8,128)S(1)} %add_add_fusion.refs_2_), channel_id=1, source_target_pairs={{0,8},{1,9},{2,10},{3,11},{4,12},{5,13},{6,14},{7,15},{8,0},{9,1},... | collective-permute-start | bytes 196616 | tf_op jit(solution)/shard_map/ppermute | solution.py:144
  28.7 4.3 %collective-permute-start.13 = (f32[32,512]{1,0:T(8,128)S(1)}, f32[32,512]{1,0:T(8,128)S(1)}, u32[]{:S(2)}, u32[]{:S(2)}) collective-permute-start(f32[32,512]{1,0:T(8,128)S(1)} %add_add_fusion.refs_2_), channel_id=1, source_target_pairs={{0,4},{1,5},{2,6},{3,7},{4,0},{5,1},{6,2},{7,3},{8,12},{9,13},{10,... | collective-permute-start | bytes 196616 | tf_op jit(solution)/shard_map/ppermute | solution.py:144
  33.0 4.5 %collective-permute-start.14 = (f32[128,512]{1,0:T(8,128)S(1)}, f32[128,512]{1,0:T(8,128)S(1)}, u32[]{:S(2)}, u32[]{:S(2)}) collective-permute-start(f32[128,512]{1,0:T(8,128)S(1)} %pad_maximum_fusion), channel_id=1, source_target_pairs={{0,2},{1,0},{2,3},{3,1},{4,6},{5,4},{6,7},{7,5},{8,9},{9,11},{10,8... | collective-permute-start | bytes 786440 | tf_op jit(solution)/shard_map/ppermute | solution.py:240
  33.6 6.8 %collective-permute-start.17 = (f32[96,512]{1,0:T(8,128)S(1)}, f32[96,512]{1,0:T(8,128)S(1)}, u32[]{:S(2)}, u32[]{:S(2)}) collective-permute-start(f32[96,512]{1,0:T(8,128)S(1)} %constant_dynamic-update-slice_fusion.refs_3_), channel_id=1, source_target_pairs={{0,4},{1,5},{2,6},{3,7},{4,0},{5,1},{6,2},{7,3},{8,12},{9,13},{10,... | collective-permute-start | bytes 589832 | tf_op jit(solution)/shard_map/ppermute | solution.py:144
  37.5 1.4 %collective-permute-start.15 = (f32[64,512]{1,0:T(8,128)S(1)}, f32[64,512]{1,0:T(8,128)S(1)}, u32[]{:S(2)}, u32[]{:S(2)}) collective-permute-start(f32[64,512]{1,0:T(8,128)S(1)} %get-tuple-element.36), channel_id=1, source_target_pairs={{0,1},{1,0},{2,3},{3,2},{4,5},{5,4},{6,7},{7,6},{8,9},{9,8},{10,11... | collective-permute-start | bytes 393224 | tf_op jit(solution)/shard_map/ppermute | solution.py:144
  37.6 1.5 %collective-permute-start.16 = (f32[64,512]{1,0:T(8,128)S(1)}, f32[64,512]{1,0:T(8,128)S(1)}, u32[]{:S(2)}, u32[]{:S(2)}) collective-permute-start(f32[64,512]{1,0:T(8,128)S(1)} %get-tuple-element.35), channel_id=1, source_target_pairs={{0,1},{1,0},{2,3},{3,2},{4,5},{5,4},{6,7},{7,6},{8,9},{9,8},{10,11... | collective-permute-start | bytes 393224 | tf_op jit(solution)/shard_map/ppermute | solution.py:144

commit v5 on v4

--- a/solution.py
+++ b/solution.py
@@ -209,8 +209,8 @@
     for k in [*range(n_gr // 2 + 2, n_gr), *range(1, n_gr // 2)]:
         owned = owned + arrived[k]
     owned = owned + parts[0]
-    gathered = [owned] + [swap(owned, k * fan, 0) for k in range(n_gr - 1, 0, -1)]
-    blocks = [gathered[0], jnp.concatenate(gathered[1:], axis=0)]
+    gathered = [owned] + [swap(owned, k * fan, 0) for k in [3, 2, 1]]
+    blocks = [jnp.concatenate(gathered[0:2], axis=0), jnp.concatenate(gathered[2:4], axis=0)]
     sides, others = [], []
     for side in blocks:
         bits = 1
@@ -225,7 +225,6 @@
         others.append(swap(side, fan // 2, 0))
 
     have = jnp.concatenate(gathered, axis=0)
-    have, others[0] = lax.optimization_barrier((have, others[0]))
     turn = gr ^ high
     bits = n_gr // 2
     while bits > 1:
@@ -237,10 +236,11 @@
                 pairs.append((c * n_gr + g, c * n_gr + (g ^ flip)))
         if bits > 2:
             pairs = [(c * n_gr + g, c * n_gr + (g ^ bits)) for c in range(n_cal) for g in range(n_gr)]
-        got = lax.ppermute(have, AXES, pairs)
+        got = jnp.concatenate([lax.ppermute(have[i : i + clusters // 4], AXES, pairs) for i in range(0, clusters, clusters // 4)], axis=0)
+        got, *others[:1] = lax.optimization_barrier((got, *others[:1]))
         have = jnp.where((turn & bits) != 0, got, have)
         bits //= 2
-    got = [swap(have[k * deep : (k + 1) * deep], 0, 1) for k in range(2)]
+    got = [swap(have[i : i + clusters // 4], 0, 1) for i in range(0, clusters, clusters // 4)]
     scale = 1.0 / (rows * n_cal)
     wide, block = have.shape[1], min(256, half)
     parts = half // block

time: 42 us -> 40.7 us (0.969)
  waiting for transfers between devices: 13.5 us -> 10.4 us
  starting transfers between devices: 21.5 us -> 23.3 us
    ppermute x17 -> x19, waiting for transfers between devices: 11.1 us -> 9.38 us  [exchange(): return lax.ppermute(value, AXES, pairs)]
    ppermute x1 -> x4, starting transfers between devices: 0.58 us -> 2.02 us  [per_device(): lax.ppermute(have[i:i + clusters // 4], AXES, pairs)]
    ppermute x1 -> x4, waiting for transfers between devices: 2.4 us -> 1.04 us  [per_device(): lax.ppermute(have[i:i + clusters // 4], AXES, pairs)]
    ppermute x17 -> x19, starting transfers between devices: 20.9 us -> 21.3 us  [exchange(): return lax.ppermute(value, AXES, pairs)]
    unnamed x15 -> x14, local copies, waits for them, and re-layouts: 2.24 us -> 2.23 us
  transfers between devices with their start and end apart: 18 -> 23, of which waited for: 12 -> 14; matrix products, arithmetic and copies ran while one was open for 0% -> 0% of each run, Pallas kernels for 3% -> 3%
where the time goes in v5:
time: 40.7 us; the launch traced here: 40.5 us
  starting transfers between devices  23.3 us (57%)
  waiting for transfers between devices  10.4 us (26%)
  Pallas kernels  4.28 us (11%)
  local copies, waits for them, and re-layouts  2.26 us (6%)
    ppermute x19, starting transfers between devices, exchange(): return lax.ppermute(value, AXES, pairs)  21.3 us
    ppermute x19, waiting for transfers between devices, exchange(): return lax.ppermute(value, AXES, pairs)  9.38 us
    pallas_call x4, Pallas kernels, kernel(): return call(*args)  2.81 us
    unnamed x14, local copies, waits for them, and re-layouts  2.23 us
    ppermute x4, starting transfers between devices, per_device(): lax.ppermute(have[i:i + clusters // 4], AXES, pairs)  2.02 us
    pallas_call x1, Pallas kernels, per_device(): pl.pallas_call(functools.partial(other_kernel, scale), out_shape=jax.Shap...  1.47 us
    ppermute x4, waiting for transfers between devices, per_device(): lax.ppermute(have[i:i + clusters // 4], AXES, pairs)  1.04 us
  transfers between devices with their start and end apart: 23, of which 14 were waited for; matrix products, arithmetic and copies ran while one was open for 0% of the time, Pallas kernels for 3%

profile of v5, /device:TPU:0, one launch (start us, length us, event | category | flops | bytes accessed | tf_op | source)
XLA Modules:
  0.0 40.5 jit_solution(15669942670376211314)
XLA Ops:
  0.0 0.0 copy-start.4
  0.0 2.2 %copy.12.held = bf16[2048,1024]{1,0:T(8,128)(2,1)S(1)} copy(bf16[2048,1024]{1,0:T(8,128)(2,1)} %param.7) | data formatting | bytes 8388608
  2.2 0.0 copy-done.4
  2.2 0.0 copy-start
  2.2 0.0 copy-start.1
  2.2 0.0 copy-start.2
  2.2 0.0 copy-start.3
  2.2 0.0 copy-start.5
  2.2 0.9 %linear.1 = (f32[1,2048]{1,0:T(1,128)S(1)}, bf16[2048,1024]{1,0:T(8,128)(2,1)S(1)}) custom-call(bf16[2048,1024]{1,0:T(8,128)(2,1)S(1)} %copy.12.held, bf16[1024]{0:T(1024)(128)(2,1)S(1)} %copy-done.4), custom_call_target="tpu_custom_call", output_to_operand_aliasing={{1}: (0, {})} | custom-call | flops 4194304 | bytes 16384 | tf_op jit(solution)/shard_map/linear/pallas_call | solution.py:169
  3.1 3.0 %collective-permute-start = (f32[1,2048]{1,0:T(1,128)S(1)}, f32[1,2048]{1,0:T(1,128)S(1)}, u32[]{:S(2)}, u32[]{:S(2)}) collective-permute-start(f32[1,2048]{1,0:T(1,128)S(1)} %get-tuple-element.20.refs_0_), channel_id=1, source_target_pairs={{0,2},{1,3},{2,0},{3,1},{4,6},{5,7},{6,4},{7,5},{8,10},{9,11},{10,... | collective-permute-start | bytes 24584 | tf_op jit(solution)/shard_map/ppermute | solution.py:144
  6.1 0.0 collective-permute-start.1
  6.1 0.2 collective-permute-start.2
  6.3 1.4 %collective-permute-done.refs_1_ = f32[1,2048]{1,0:T(1,128)S(1)} collective-permute-done((f32[1,2048]{1,0:T(1,128)S(1)}, f32[1,2048]{1,0:T(1,128)S(1)}, u32[]{:S(2)}, u32[]{:S(2)}) %collective-permute-start) | collective-permute-done | bytes 8224 | tf_op jit(solution)/shard_map/ppermute | solution.py:144
  7.8 1.4 %collective-permute-done.1.refs_2_ = f32[1,2048]{1,0:T(1,128)S(1)} collective-permute-done((f32[1,2048]{1,0:T(1,128)S(1)}, f32[1,2048]{1,0:T(1,128)S(1)}, u32[]{:S(2)}, u32[]{:S(2)}) %collective-permute-start.1) | collective-permute-done | bytes 8224 | tf_op jit(solution)/shard_map/ppermute | solution.py:144
  9.2 0.0 collective-permute-done.2.refs_3_
  9.2 0.0 copy-done
  9.2 0.0 copy-done.1
  9.2 0.0 copy-done.2
  9.2 0.0 copy-done.3
  9.3 0.0 copy-done.5
  9.3 0.6 %send_far.1 = (f32[32,512]{1,0:T(8,128)S(1)}, f32[32,512]{1,0:T(8,128)S(1)}, bf16[128,2048]{1,0:T(8,128)(2,1)S(1)}) custom-call(f32[16]{0:T(128)S(1)} %copy-done.5, f32[1,2048]{1,0:T(1,128)S(1)} %get-tuple-element.20.refs_0_, f32[1,2048]{1,0:T(1,128)S(1)} %collective-permute-done.refs_1_, f32[1,2048]{1,0:T(1,128)S(1)} %collective-permute-done.1.refs_2_, ...), custom_call_target="tpu_custom_call" | custom-call | flops 134217728 | bytes 524288 | tf_op jit(solution)/shard_map/send_far/pallas_call | solution.py:169
  9.9 1.6 %collective-permute-start.5 = (f32[32,512]{1,0:T(8,128)S(1)}, f32[32,512]{1,0:T(8,128)S(1)}, u32[]{:S(2)}, u32[]{:S(2)}) collective-permute-start(f32[32,512]{1,0:T(8,128)S(1)} %get-tuple-element.26), channel_id=1, source_target_pairs={{0,4},{1,5},{2,6},{3,7},{4,0},{5,1},{6,2},{7,3},{8,12},{9,13},{10,... | collective-permute-start | bytes 196616 | tf_op jit(solution)/shard_map/ppermute | solution.py:144
  11.5 0.5 %collective-permute-start.3 = (f32[32,512]{1,0:T(8,128)S(1)}, f32[32,512]{1,0:T(8,128)S(1)}, u32[]{:S(2)}, u32[]{:S(2)}) collective-permute-start(f32[32,512]{1,0:T(8,128)S(1)} %get-tuple-element.24), channel_id=1, source_target_pairs={{0,4},{1,5},{2,6},{3,7},{4,0},{5,1},{6,2},{7,3},{8,12},{9,13},{10,... | collective-permute-start | bytes 196616 | tf_op jit(solution)/shard_map/ppermute | solution.py:144
  12.0 0.8 %rest.1 = (f32[32,512]{1,0:T(8,128)S(1)}, f32[32,512]{1,0:T(8,128)S(1)}, f32[32,512]{1,0:T(8,128)S(1)}, f32[32,512]{1,0:T(8,128)S(1)}, f32[32,512]{1,0:T(8,128)S(1)}, /*index=5*/f32[32,512]{1,0:T(8,128)S(1)}) custom-call(bf16[128,2048]{1,0:T(8,128)(2,1)S(1)} %get-tuple-element.22.picks, bf16[2048,1024]{1,0:T(8,128)(2,1)S(1)} %get-tuple-element.21.refs_8_.held), custom_call_target="tpu_custom_call" | custom-call | flops 402653184 | bytes 1572864 | tf_op jit(solution)/shard_map/rest/pallas_call | solution.py:169
  12.8 1.6 %collective-permute-start.7 = (f32[32,512]{1,0:T(8,128)S(1)}, f32[32,512]{1,0:T(8,128)S(1)}, u32[]{:S(2)}, u32[]{:S(2)}) collective-permute-start(f32[32,512]{1,0:T(8,128)S(1)} %get-tuple-element.28), channel_id=1, source_target_pairs={{0,4},{1,5},{2,6},{3,7},{4,0},{5,1},{6,2},{7,3},{8,12},{9,13},{10,... | collective-permute-start | bytes 196616 | tf_op jit(solution)/shard_map/ppermute | solution.py:144
  14.4 0.5 %collective-permute-start.9 = (f32[32,512]{1,0:T(8,128)S(1)}, f32[32,512]{1,0:T(8,128)S(1)}, u32[]{:S(2)}, u32[]{:S(2)}) collective-permute-start(f32[32,512]{1,0:T(8,128)S(1)} %get-tuple-element.30), channel_id=1, source_target_pairs={{0,4},{1,5},{2,6},{3,7},{4,0},{5,1},{6,2},{7,3},{8,12},{9,13},{10,... | collective-permute-start | bytes 196616 | tf_op jit(solution)/shard_map/ppermute | solution.py:144
  14.9 0.0 collective-permute-done.5
  14.9 3.7 %collective-permute-start.6 = (f32[32,512]{1,0:T(8,128)S(1)}, f32[32,512]{1,0:T(8,128)S(1)}, u32[]{:S(2)}, u32[]{:S(2)}) collective-permute-start(f32[32,512]{1,0:T(8,128)S(1)} %add.23), channel_id=1, source_target_pairs={{0,24},{1,25},{2,26},{3,27},{4,28},{5,29},{6,30},{7,31},{8,16},{9,... | collective-permute-start | bytes 196616 | tf_op jit(solution)/shard_map/ppermute | solution.py:144
  18.6 0.0 collective-permute-done.3
  18.6 0.6 %collective-permute-start.4 = (f32[32,512]{1,0:T(8,128)S(1)}, f32[32,512]{1,0:T(8,128)S(1)}, u32[]{:S(2)}, u32[]{:S(2)}) collective-permute-start(f32[32,512]{1,0:T(8,128)S(1)} %add.22), channel_id=1, source_target_pairs={{0,16},{1,17},{2,18},{3,19},{4,20},{5,21},{6,22},{7,23},{8,24},{9,... | collective-permute-start | bytes 196616 | tf_op jit(solution)/shard_map/ppermute | solution.py:144
  19.2 0.0 collective-permute-done.7
  19.2 1.6 %collective-permute-start.8 = (f32[32,512]{1,0:T(8,128)S(1)}, f32[32,512]{1,0:T(8,128)S(1)}, u32[]{:S(2)}, u32[]{:S(2)}) collective-permute-start(f32[32,512]{1,0:T(8,128)S(1)} %add.25), channel_id=1, source_target_pairs={{0,8},{1,9},{2,10},{3,11},{4,12},{5,13},{6,14},{7,15},{8,0},{9,1},... | collective-permute-start | bytes 196616 | tf_op jit(solution)/shard_map/ppermute | solution.py:144
  20.8 0.3 collective-permute-done.6
  21.2 2.8 %collective-permute-done.4 = f32[32,512]{1,0:T(8,128)S(1)} collective-permute-done((f32[32,512]{1,0:T(8,128)S(1)}, f32[32,512]{1,0:T(8,128)S(1)}, u32[]{:S(2)}, u32[]{:S(2)}) %collective-permute-start.4) | collective-permute-done | bytes 65568 | tf_op jit(solution)/shard_map/ppermute | solution.py:144
  24.0 0.0 collective-permute-done.9
  24.0 0.2 collective-permute-done.8
  24.2 2.2 %collective-permute-start.11 = (f32[32,512]{1,0:T(8,128)S(1)}, f32[32,512]{1,0:T(8,128)S(1)}, u32[]{:S(2)}, u32[]{:S(2)}) collective-permute-start(f32[32,512]{1,0:T(8,128)S(1)} %add_add_fusion), channel_id=1, source_target_pairs={{0,24},{1,25},{2,26},{3,27},{4,28},{5,29},{6,30},{7,31},{8,16},{9,... | collective-permute-start | bytes 196616 | tf_op jit(solution)/shard_map/ppermute | solution.py:144
  26.5 0.2 collective-permute-start.13
  26.6 2.0 %collective-permute-start.15 = (f32[32,512]{1,0:T(8,128)S(1)}, f32[32,512]{1,0:T(8,128)S(1)}, u32[]{:S(2)}, u32[]{:S(2)}) collective-permute-start(f32[32,512]{1,0:T(8,128)S(1)} %add_add_fusion), channel_id=1, source_target_pairs={{0,8},{1,9},{2,10},{3,11},{4,12},{5,13},{6,14},{7,15},{8,0},{9,1},... | collective-permute-start | bytes 196616 | tf_op jit(solution)/shard_map/ppermute | solution.py:144
  28.7 0.6 %collective-permute-start.10 = (f32[32,512]{1,0:T(8,128)S(1)}, f32[32,512]{1,0:T(8,128)S(1)}, u32[]{:S(2)}, u32[]{:S(2)}) collective-permute-start(f32[32,512]{1,0:T(8,128)S(1)} %add_add_fusion), channel_id=1, source_target_pairs={{0,2},{1,0},{2,3},{3,1},{4,6},{5,4},{6,7},{7,5},{8,9},{9,11},{10,8... | collective-permute-start | bytes 196616 | tf_op jit(solution)/shard_map/ppermute | solution.py:239
  29.3 1.5 %collective-permute-done.11 = f32[32,512]{1,0:T(8,128)S(1)} collective-permute-done((f32[32,512]{1,0:T(8,128)S(1)}, f32[32,512]{1,0:T(8,128)S(1)}, u32[]{:S(2)}, u32[]{:S(2)}) %collective-permute-start.11) | collective-permute-done | bytes 65568 | tf_op jit(solution)/shard_map/ppermute | solution.py:144
  30.8 0.9 %collective-permute-start.17 = (f32[64,512]{1,0:T(8,128)S(1)}, f32[64,512]{1,0:T(8,128)S(1)}, u32[]{:S(2)}, u32[]{:S(2)}) collective-permute-start(f32[64,512]{1,0:T(8,128)S(1)} %pad_maximum_fusion.1.refs_4_), channel_id=1, source_target_pairs={{0,4},{1,5},{2,6},{3,7},{4,0},{5,1},{6,2},{7,3},{8,12},{9,13},{10,... | collective-permute-start | bytes 393224 | tf_op jit(solution)/shard_map/ppermute | solution.py:144
  31.6 0.9 %collective-permute-start.12 = (f32[32,512]{1,0:T(8,128)S(1)}, f32[32,512]{1,0:T(8,128)S(1)}, u32[]{:S(2)}, u32[]{:S(2)}) collective-permute-start(f32[32,512]{1,0:T(8,128)S(1)} %collective-permute-done.11), channel_id=1, source_target_pairs={{0,2},{1,0},{2,3},{3,1},{4,6},{5,4},{6,7},{7,5},{8,9},{9,11},{10,8... | collective-permute-start | bytes 196616 | tf_op jit(solution)/shard_map/ppermute | solution.py:239
  32.5 0.0 collective-permute-done.13
  32.5 0.5 %collective-permute-start.14 = (f32[32,512]{1,0:T(8,128)S(1)}, f32[32,512]{1,0:T(8,128)S(1)}, u32[]{:S(2)}, u32[]{:S(2)}) collective-permute-start(f32[32,512]{1,0:T(8,128)S(1)} %collective-permute-done.13), channel_id=1, source_target_pairs={{0,2},{1,0},{2,3},{3,1},{4,6},{5,4},{6,7},{7,5},{8,9},{9,11},{10,8... | collective-permute-start | bytes 196616 | tf_op jit(solution)/shard_map/ppermute | solution.py:239
  33.0 0.0 collective-permute-done.15
  33.0 0.1 collective-permute-start.16
  33.1 0.0 collective-permute-done.10
  33.1 1.6 %collective-permute-start.22 = (f32[64,512]{1,0:T(8,128)S(1)}, f32[64,512]{1,0:T(8,128)S(1)}, u32[]{:S(2)}, u32[]{:S(2)}) collective-permute-start(f32[64,512]{1,0:T(8,128)S(1)} %constant_dynamic-update-slice_fusion.refs_5_), channel_id=1, source_target_pairs={{0,4},{1,5},{2,6},{3,7},{4,0},{5,1},{6,2},{7,3},{8,12},{9,13},{10,... | collective-permute-start | bytes 393224 | tf_op jit(solution)/shard_map/ppermute | solution.py:144
  34.7 0.0 collective-permute-done.12
  34.7 0.4 collective-permute-done.14
  35.0 0.7 %collective-permute-done.16 = f32[32,512]{1,0:T(8,128)S(1)} collective-permute-done((f32[32,512]{1,0:T(8,128)S(1)}, f32[32,512]{1,0:T(8,128)S(1)}, u32[]{:S(2)}, u32[]{:S(2)}) %collective-permute-start.16) | collective-permute-done | bytes 65568 | tf_op jit(solution)/shard_map/ppermute | solution.py:239
  35.7 0.1 collective-permute-done.17.refs_0_
  35.9 0.5 %collective-permute-start.18 = (f32[32,512]{1,0:T(8,128)S(1)}, f32[32,512]{1,0:T(8,128)S(1)}, u32[]{:S(2)}, u32[]{:S(2)}) collective-permute-start(f32[32,512]{1,0:T(8,128)S(1)} %get-tuple-element.38), channel_id=1, source_target_pairs={{0,1},{1,0},{2,3},{3,2},{4,5},{5,4},{6,7},{7,6},{8,9},{9,8},{10,11... | collective-permute-start | bytes 196616 | tf_op jit(solution)/shard_map/ppermute | solution.py:144
  36.4 0.1 collective-permute-start.19
  36.5 0.4 %collective-permute-start.20 = (f32[32,512]{1,0:T(8,128)S(1)}, f32[32,512]{1,0:T(8,128)S(1)}, u32[]{:S(2)}, u32[]{:S(2)}) collective-permute-start(f32[32,512]{1,0:T(8,128)S(1)} %get-tuple-element.36), channel_id=1, source_target_pairs={{0,1},{1,0},{2,3},{3,2},{4,5},{5,4},{6,7},{7,6},{8,9},{9,8},{10,11... | collective-permute-start | bytes 196616 | tf_op jit(solution)/shard_map/ppermute | solution.py:144
  36.9 0.1 collective-permute-start.21
  37.0 0.3 collective-permute-done.18.refs_0_
  37.3 0.4 collective-permute-done.19.refs_1_
  37.7 0.2 collective-permute-done.20.refs_2_
  37.8 0.4 collective-permute-done.21.refs_3_
  38.2 0.5 %meat_own.1 = (f32[2,512,256]{2,1,0:T(8,128)S(1)}, bf16[256,512]{1,0:T(8,128)(2,1)S(1)}) custom-call(f32[128,512]{1,0:T(8,128)S(1)} %maximum_select_fusion.have, f32[32,512]{1,0:T(8,128)S(1)} %collective-permute-done.18.refs_0_, f32[32,512]{1,0:T(8,128)S(1)} %collective-permute-done.19.refs_1_, f32[32,512]{1,0:T(8,128)S(1)} %collective-permute-done.20.refs_2_, ...), custom_call_target="tpu_custom_call" | custom-call | flops 201326592 | bytes 786432 | tf_op jit(solution)/shard_map/meat_own/pallas_call | solution.py:169
  38.7 0.4 collective-permute-done.22.refs_1_
  39.1 1.5 %meat_other.1 = f32[512,1024]{1,0:T(8,128)} custom-call(f32[2,512,256]{2,1,0:T(8,128)S(1)} %get-tuple-element.32.first, bf16[256,512]{1,0:T(8,128)(2,1)S(1)} %get-tuple-element.33.left, f32[64,512]{1,0:T(8,128)S(1)} %collective-permute-done.17.refs_0_, f32[64,512]{1,0:T(8,128)S(1)} %collective-permute-done.22.refs_1_), custom_call_target="tpu_custom_call" | custom-call | flops 201326592 | bytes 2097152 | tf_op jit(solution)/shard_map/meat_other/pallas_call | solution.py:254
  (11 shorter events, 0.2 us)
Async XLA Ops:
  0.0 2.2 %copy-start.4 = (bf16[1024]{0:T(1024)(128)(2,1)S(1)}, bf16[1024]{0:T(1024)(128)(2,1)}, u32[]{:S(2)}) copy-start(bf16[1024]{0:T(1024)(128)(2,1)} %coef.1) | copy-start | bytes 6148
  2.2 7.0 %copy-start = (f32[2048]{0:T(1024)S(1)}, f32[2048]{0:T(1024)}, u32[]{:S(2)}) copy-start(f32[2048]{0:T(1024)} %param.9) | copy-start | bytes 24580
  2.2 7.0 %copy-start.1 = (f32[2048]{0:T(1024)S(1)}, f32[2048]{0:T(1024)}, u32[]{:S(2)}) copy-start(f32[2048]{0:T(1024)} %param.10) | copy-start | bytes 24580
  2.2 7.0 %copy-start.2 = (s32[2048]{0:T(1024)S(1)}, s32[2048]{0:T(1024)}, u32[]{:S(2)}) copy-start(s32[2048]{0:T(1024)} %param.11) | copy-start | bytes 24580
  2.2 7.0 %copy-start.3 = (s32[2048]{0:T(1024)S(1)}, s32[2048]{0:T(1024)}, u32[]{:S(2)}) copy-start(s32[2048]{0:T(1024)} %param.12) | copy-start | bytes 24580
  2.2 7.0 %copy-start.5 = (f32[16]{0:T(128)S(1)}, f32[16]{0:T(128)}, u32[]{:S(2)}) copy-start(f32[16]{0:T(128)} %effect.1) | copy-start | bytes 196
  3.1 4.6 %collective-permute-start = (f32[1,2048]{1,0:T(1,128)S(1)}, f32[1,2048]{1,0:T(1,128)S(1)}, u32[]{:S(2)}, u32[]{:S(2)}) collective-permute-start(f32[1,2048]{1,0:T(1,128)S(1)} %get-tuple-element.20.refs_0_), channel_id=1, source_target_pairs={{0,2},{1,3},{2,0},{3,1},{4,6},{5,7},{6,4},{7,5},{8,10},{9,11},{10,... | collective-permute-start | bytes 24584 | tf_op jit(solution)/shard_map/ppermute | solution.py:144
  6.1 3.1 %collective-permute-start.1 = (f32[1,2048]{1,0:T(1,128)S(1)}, f32[1,2048]{1,0:T(1,128)S(1)}, u32[]{:S(2)}, u32[]{:S(2)}) collective-permute-start(f32[1,2048]{1,0:T(1,128)S(1)} %get-tuple-element.20.refs_0_), channel_id=1, source_target_pairs={{0,3},{1,2},{2,1},{3,0},{4,7},{5,6},{6,5},{7,4},{8,11},{9,10},{10,... | collective-permute-start | bytes 24584 | tf_op jit(solution)/shard_map/ppermute | solution.py:144
  6.1 3.1 %collective-permute-start.2 = (f32[1,2048]{1,0:T(1,128)S(1)}, f32[1,2048]{1,0:T(1,128)S(1)}, u32[]{:S(2)}, u32[]{:S(2)}) collective-permute-start(f32[1,2048]{1,0:T(1,128)S(1)} %get-tuple-element.20.refs_0_), channel_id=1, source_target_pairs={{0,1},{1,0},{2,3},{3,2},{4,5},{5,4},{6,7},{7,6},{8,9},{9,8},{10,11... | collective-permute-start | bytes 24584 | tf_op jit(solution)/shard_map/ppermute | solution.py:144
  9.9 5.0 %collective-permute-start.5 = (f32[32,512]{1,0:T(8,128)S(1)}, f32[32,512]{1,0:T(8,128)S(1)}, u32[]{:S(2)}, u32[]{:S(2)}) collective-permute-start(f32[32,512]{1,0:T(8,128)S(1)} %get-tuple-element.26), channel_id=1, source_target_pairs={{0,4},{1,5},{2,6},{3,7},{4,0},{5,1},{6,2},{7,3},{8,12},{9,13},{10,... | collective-permute-start | bytes 196616 | tf_op jit(solution)/shard_map/ppermute | solution.py:144
  11.5 7.1 %collective-permute-start.3 = (f32[32,512]{1,0:T(8,128)S(1)}, f32[32,512]{1,0:T(8,128)S(1)}, u32[]{:S(2)}, u32[]{:S(2)}) collective-permute-start(f32[32,512]{1,0:T(8,128)S(1)} %get-tuple-element.24), channel_id=1, source_target_pairs={{0,4},{1,5},{2,6},{3,7},{4,0},{5,1},{6,2},{7,3},{8,12},{9,13},{10,... | collective-permute-start | bytes 196616 | tf_op jit(solution)/shard_map/ppermute | solution.py:144
  12.8 6.4 %collective-permute-start.7 = (f32[32,512]{1,0:T(8,128)S(1)}, f32[32,512]{1,0:T(8,128)S(1)}, u32[]{:S(2)}, u32[]{:S(2)}) collective-permute-start(f32[32,512]{1,0:T(8,128)S(1)} %get-tuple-element.28), channel_id=1, source_target_pairs={{0,4},{1,5},{2,6},{3,7},{4,0},{5,1},{6,2},{7,3},{8,12},{9,13},{10,... | collective-permute-start | bytes 196616 | tf_op jit(solution)/shard_map/ppermute | solution.py:144
  14.4 9.6 %collective-permute-start.9 = (f32[32,512]{1,0:T(8,128)S(1)}, f32[32,512]{1,0:T(8,128)S(1)}, u32[]{:S(2)}, u32[]{:S(2)}) collective-permute-start(f32[32,512]{1,0:T(8,128)S(1)} %get-tuple-element.30), channel_id=1, source_target_pairs={{0,4},{1,5},{2,6},{3,7},{4,0},{5,1},{6,2},{7,3},{8,12},{9,13},{10,... | collective-permute-start | bytes 196616 | tf_op jit(solution)/shard_map/ppermute | solution.py:144
  14.9 6.2 %collective-permute-start.6 = (f32[32,512]{1,0:T(8,128)S(1)}, f32[32,512]{1,0:T(8,128)S(1)}, u32[]{:S(2)}, u32[]{:S(2)}) collective-permute-start(f32[32,512]{1,0:T(8,128)S(1)} %add.23), channel_id=1, source_target_pairs={{0,24},{1,25},{2,26},{3,27},{4,28},{5,29},{6,30},{7,31},{8,16},{9,... | collective-permute-start | bytes 196616 | tf_op jit(solution)/shard_map/ppermute | solution.py:144
  18.6 5.3 %collective-permute-start.4 = (f32[32,512]{1,0:T(8,128)S(1)}, f32[32,512]{1,0:T(8,128)S(1)}, u32[]{:S(2)}, u32[]{:S(2)}) collective-permute-start(f32[32,512]{1,0:T(8,128)S(1)} %add.22), channel_id=1, source_target_pairs={{0,16},{1,17},{2,18},{3,19},{4,20},{5,21},{6,22},{7,23},{8,24},{9,... | collective-permute-start | bytes 196616 | tf_op jit(solution)/shard_map/ppermute | solution.py:144
  19.2 5.0 %collective-permute-start.8 = (f32[32,512]{1,0:T(8,128)S(1)}, f32[32,512]{1,0:T(8,128)S(1)}, u32[]{:S(2)}, u32[]{:S(2)}) collective-permute-start(f32[32,512]{1,0:T(8,128)S(1)} %add.25), channel_id=1, source_target_pairs={{0,8},{1,9},{2,10},{3,11},{4,12},{5,13},{6,14},{7,15},{8,0},{9,1},... | collective-permute-start | bytes 196616 | tf_op jit(solution)/shard_map/ppermute | solution.py:144
  24.2 6.5 %collective-permute-start.11 = (f32[32,512]{1,0:T(8,128)S(1)}, f32[32,512]{1,0:T(8,128)S(1)}, u32[]{:S(2)}, u32[]{:S(2)}) collective-permute-start(f32[32,512]{1,0:T(8,128)S(1)} %add_add_fusion), channel_id=1, source_target_pairs={{0,24},{1,25},{2,26},{3,27},{4,28},{5,29},{6,30},{7,31},{8,16},{9,... | collective-permute-start | bytes 196616 | tf_op jit(solution)/shard_map/ppermute | solution.py:144
  26.5 6.0 %collective-permute-start.13 = (f32[32,512]{1,0:T(8,128)S(1)}, f32[32,512]{1,0:T(8,128)S(1)}, u32[]{:S(2)}, u32[]{:S(2)}) collective-permute-start(f32[32,512]{1,0:T(8,128)S(1)} %add_add_fusion), channel_id=1, source_target_pairs={{0,16},{1,17},{2,18},{3,19},{4,20},{5,21},{6,22},{7,23},{8,24},{9,... | collective-permute-start | bytes 196616 | tf_op jit(solution)/shard_map/ppermute | solution.py:144
  26.6 6.4 %collective-permute-start.15 = (f32[32,512]{1,0:T(8,128)S(1)}, f32[32,512]{1,0:T(8,128)S(1)}, u32[]{:S(2)}, u32[]{:S(2)}) collective-permute-start(f32[32,512]{1,0:T(8,128)S(1)} %add_add_fusion), channel_id=1, source_target_pairs={{0,8},{1,9},{2,10},{3,11},{4,12},{5,13},{6,14},{7,15},{8,0},{9,1},... | collective-permute-start | bytes 196616 | tf_op jit(solution)/shard_map/ppermute | solution.py:144
  28.7 4.4 %collective-permute-start.10 = (f32[32,512]{1,0:T(8,128)S(1)}, f32[32,512]{1,0:T(8,128)S(1)}, u32[]{:S(2)}, u32[]{:S(2)}) collective-permute-start(f32[32,512]{1,0:T(8,128)S(1)} %add_add_fusion), channel_id=1, source_target_pairs={{0,2},{1,0},{2,3},{3,1},{4,6},{5,4},{6,7},{7,5},{8,9},{9,11},{10,8... | collective-permute-start | bytes 196616 | tf_op jit(solution)/shard_map/ppermute | solution.py:239
  30.8 5.0 %collective-permute-start.17 = (f32[64,512]{1,0:T(8,128)S(1)}, f32[64,512]{1,0:T(8,128)S(1)}, u32[]{:S(2)}, u32[]{:S(2)}) collective-permute-start(f32[64,512]{1,0:T(8,128)S(1)} %pad_maximum_fusion.1.refs_4_), channel_id=1, source_target_pairs={{0,4},{1,5},{2,6},{3,7},{4,0},{5,1},{6,2},{7,3},{8,12},{9,13},{10,... | collective-permute-start | bytes 393224 | tf_op jit(solution)/shard_map/ppermute | solution.py:144
  31.6 3.1 %collective-permute-start.12 = (f32[32,512]{1,0:T(8,128)S(1)}, f32[32,512]{1,0:T(8,128)S(1)}, u32[]{:S(2)}, u32[]{:S(2)}) collective-permute-start(f32[32,512]{1,0:T(8,128)S(1)} %collective-permute-done.11), channel_id=1, source_target_pairs={{0,2},{1,0},{2,3},{3,1},{4,6},{5,4},{6,7},{7,5},{8,9},{9,11},{10,8... | collective-permute-start | bytes 196616 | tf_op jit(solution)/shard_map/ppermute | solution.py:239
  32.5 2.5 %collective-permute-start.14 = (f32[32,512]{1,0:T(8,128)S(1)}, f32[32,512]{1,0:T(8,128)S(1)}, u32[]{:S(2)}, u32[]{:S(2)}) collective-permute-start(f32[32,512]{1,0:T(8,128)S(1)} %collective-permute-done.13), channel_id=1, source_target_pairs={{0,2},{1,0},{2,3},{3,1},{4,6},{5,4},{6,7},{7,5},{8,9},{9,11},{10,8... | collective-permute-start | bytes 196616 | tf_op jit(solution)/shard_map/ppermute | solution.py:239
  33.0 2.7 %collective-permute-start.16 = (f32[32,512]{1,0:T(8,128)S(1)}, f32[32,512]{1,0:T(8,128)S(1)}, u32[]{:S(2)}, u32[]{:S(2)}) collective-permute-start(f32[32,512]{1,0:T(8,128)S(1)} %collective-permute-done.15), channel_id=1, source_target_pairs={{0,2},{1,0},{2,3},{3,1},{4,6},{5,4},{6,7},{7,5},{8,9},{9,11},{10,8... | collective-permute-start | bytes 196616 | tf_op jit(solution)/shard_map/ppermute | solution.py:239
  33.1 6.0 %collective-permute-start.22 = (f32[64,512]{1,0:T(8,128)S(1)}, f32[64,512]{1,0:T(8,128)S(1)}, u32[]{:S(2)}, u32[]{:S(2)}) collective-permute-start(f32[64,512]{1,0:T(8,128)S(1)} %constant_dynamic-update-slice_fusion.refs_5_), channel_id=1, source_target_pairs={{0,4},{1,5},{2,6},{3,7},{4,0},{5,1},{6,2},{7,3},{8,12},{9,13},{10,... | collective-permute-start | bytes 393224 | tf_op jit(solution)/shard_map/ppermute | solution.py:144
  35.9 1.4 %collective-permute-start.18 = (f32[32,512]{1,0:T(8,128)S(1)}, f32[32,512]{1,0:T(8,128)S(1)}, u32[]{:S(2)}, u32[]{:S(2)}) collective-permute-start(f32[32,512]{1,0:T(8,128)S(1)} %get-tuple-element.38), channel_id=1, source_target_pairs={{0,1},{1,0},{2,3},{3,2},{4,5},{5,4},{6,7},{7,6},{8,9},{9,8},{10,11... | collective-permute-start | bytes 196616 | tf_op jit(solution)/shard_map/ppermute | solution.py:144
  36.4 1.3 %collective-permute-start.19 = (f32[32,512]{1,0:T(8,128)S(1)}, f32[32,512]{1,0:T(8,128)S(1)}, u32[]{:S(2)}, u32[]{:S(2)}) collective-permute-start(f32[32,512]{1,0:T(8,128)S(1)} %get-tuple-element.37), channel_id=1, source_target_pairs={{0,1},{1,0},{2,3},{3,2},{4,5},{5,4},{6,7},{7,6},{8,9},{9,8},{10,11... | collective-permute-start | bytes 196616 | tf_op jit(solution)/shard_map/ppermute | solution.py:144
  36.5 1.3 %collective-permute-start.20 = (f32[32,512]{1,0:T(8,128)S(1)}, f32[32,512]{1,0:T(8,128)S(1)}, u32[]{:S(2)}, u32[]{:S(2)}) collective-permute-start(f32[32,512]{1,0:T(8,128)S(1)} %get-tuple-element.36), channel_id=1, source_target_pairs={{0,1},{1,0},{2,3},{3,2},{4,5},{5,4},{6,7},{7,6},{8,9},{9,8},{10,11... | collective-permute-start | bytes 196616 | tf_op jit(solution)/shard_map/ppermute | solution.py:144
  36.9 1.3 %collective-permute-start.21 = (f32[32,512]{1,0:T(8,128)S(1)}, f32[32,512]{1,0:T(8,128)S(1)}, u32[]{:S(2)}, u32[]{:S(2)}) collective-permute-start(f32[32,512]{1,0:T(8,128)S(1)} %get-tuple-element.35), channel_id=1, source_target_pairs={{0,1},{1,0},{2,3},{3,2},{4,5},{5,4},{6,7},{7,6},{8,9},{9,8},{10,11... | collective-permute-start | bytes 196616 | tf_op jit(solution)/shard_map/ppermute | solution.py:144

commit v6 on v5

--- a/solution.py
+++ b/solution.py
@@ -32,15 +32,23 @@
     return high, low
 
 
-def linear_kernel(held, coef, lin, out):
-    del out
+def linear_kernel(feats, coef, lin, held, weights, sems):
     rows, width = held.shape
-    weights = coef[...].reshape(1, width).astype(jnp.float32)
     step = min(512, rows)
+    fetch = pltpu.make_async_copy(coef, weights, sems.at[rows // step])
+    fetch.start()
+    copies = []
     for i in range(0, rows, step):
+        part = pl.ds(i, step)
+        copies.append(pltpu.make_async_copy(feats.at[part], held.at[part], sems.at[i // step]))
+        copies[-1].start()
+    fetch.wait()
+    scale = weights[...].reshape(1, width).astype(jnp.float32)
+    for i in range(0, rows, step):
+        copies[i // step].wait()
         total = jnp.zeros((step, 128), jnp.float32)
         for j in range(0, width, 128):
-            total = total + held[i : i + step, j : j + 128].astype(jnp.float32) * weights[:, j : j + 128]
+            total = total + held[i : i + step, j : j + 128].astype(jnp.float32) * scale[:, j : j + 128]
         lin[:, i : i + step] = jnp.sum(total.T, axis=0, keepdims=True)
 
 
@@ -169,11 +177,17 @@
         return call(*args)
 
     f32, bf16 = jnp.float32, jnp.bfloat16
-    lin, features = kernel(
+    pieces = rows // min(512, rows)
+    lin, features = pl.pallas_call(
         linear_kernel,
-        (jax.ShapeDtypeStruct((1, rows), f32), jax.ShapeDtypeStruct((rows, width), bf16)),
-        (features, coef), 0, "linear", 2 * rows * width, {0: 1},
-    )
+        out_shape=(jax.ShapeDtypeStruct((1, rows), f32), jax.ShapeDtypeStruct((rows, width), bf16)),
+        in_specs=[ANY, ANY],
+        out_specs=(VMEM, VMEM),
+        scratch_shapes=[pltpu.VMEM((width,), bf16), pltpu.SemaphoreType.DMA((pieces + 1,))],
+        compiler_params=pltpu.CompilerParams(vmem_limit_bytes=LIMIT),
+        cost_estimate=pl.CostEstimate(flops=2 * rows * width, bytes_accessed=2 * rows * width, transcendentals=0),
+        name="linear",
+    )(*(pltpu.with_memory_space_constraint(value, pltpu.HBM) for value in (features, coef)))
     linears = [lin] + [swap(lin, 0, k) for k in [*range(n_gr // 2, n_gr), *range(1, n_gr // 2)]]
 
     half = width // 2
@@ -209,7 +223,7 @@
     for k in [*range(n_gr // 2 + 2, n_gr), *range(1, n_gr // 2)]:
         owned = owned + arrived[k]
     owned = owned + parts[0]
-    gathered = [owned] + [swap(owned, k * fan, 0) for k in [3, 2, 1]]
+    gathered = [owned] + [swap(owned, k * fan, 0) for k in [3, 1, 2]]
     blocks = [jnp.concatenate(gathered[0:2], axis=0), jnp.concatenate(gathered[2:4], axis=0)]
     sides, others = [], []
     for side in blocks:

time: 40.7 us -> 39.8 us (0.978)
  local copies, waits for them, and re-layouts: 2.26 us -> 0.05 us
  Pallas kernels: 4.28 us -> 5.96 us
    pallas_call x0 -> x1, Pallas kernels: none -> 2.57 us  [per_device(): pl.pallas_call(linear_kernel, out_shape=(jax.ShapeDtypeStruct((1, rows),...]
    unnamed x14 -> x11, local copies, waits for them, and re-layouts: 2.23 us -> 0.02 us
    pallas_call x4 -> x3, Pallas kernels: 2.81 us -> 1.92 us  [kernel(): return call(*args)]
  transfers between devices with their start and end apart: 23 -> 23, of which waited for: 14 -> 13; matrix products, arithmetic and copies ran while one was open for 0% -> 0% of each run, Pallas kernels for 3% -> 3%
where the time goes in v6:
time: 39.8 us; the launch traced here: 39.6 us
  starting transfers between devices  22.9 us (58%)
  waiting for transfers between devices  10.4 us (26%)
  Pallas kernels  5.96 us (15%)
    ppermute x19, starting transfers between devices, exchange(): return lax.ppermute(value, AXES, pairs)  21.2 us
    ppermute x19, waiting for transfers between devices, exchange(): return lax.ppermute(value, AXES, pairs)  9.15 us
    pallas_call x1, Pallas kernels, per_device(): pl.pallas_call(linear_kernel, out_shape=(jax.ShapeDtypeStruct((1, rows),...  2.57 us
    pallas_call x3, Pallas kernels, kernel(): return call(*args)  1.92 us
    ppermute x4, starting transfers between devices, per_device(): lax.ppermute(have[i:i + clusters // 4], AXES, pairs)  1.77 us
    pallas_call x1, Pallas kernels, per_device(): pl.pallas_call(functools.partial(other_kernel, scale), out_shape=jax.Shap...  1.47 us
    ppermute x4, waiting for transfers between devices, per_device(): lax.ppermute(have[i:i + clusters // 4], AXES, pairs)  1.23 us
  transfers between devices with their start and end apart: 23, of which 13 were waited for; matrix products, arithmetic and copies ran while one was open for 0% of the time, Pallas kernels for 3%

profile of v6, /device:TPU:0, one launch (start us, length us, event | category | flops | bytes accessed | tf_op | source)
XLA Modules:
  0.0 39.6 jit_solution(7747963979621899038)
XLA Ops:
  0.0 0.0 copy-start
  0.0 0.0 copy-start.1
  0.0 0.0 copy-start.2
  0.0 0.0 copy-start.3
  0.0 0.0 copy-start.4
  0.0 2.6 %linear.1 = (f32[1,2048]{1,0:T(1,128)S(1)}, bf16[2048,1024]{1,0:T(8,128)(2,1)S(1)}) custom-call(bf16[2048,1024]{1,0:T(8,128)(2,1)} %feats.1, bf16[1024]{0:T(1024)(128)(2,1)} %coef.1), custom_call_target="tpu_custom_call" | custom-call | flops 4194304 | bytes 4194304 | tf_op jit(solution)/shard_map/linear/pallas_call | solution.py:181
  2.6 3.0 %collective-permute-start = (f32[1,2048]{1,0:T(1,128)S(1)}, f32[1,2048]{1,0:T(1,128)S(1)}, u32[]{:S(2)}, u32[]{:S(2)}) collective-permute-start(f32[1,2048]{1,0:T(1,128)S(1)} %get-tuple-element.20.refs_0_), channel_id=1, source_target_pairs={{0,2},{1,3},{2,0},{3,1},{4,6},{5,7},{6,4},{7,5},{8,10},{9,11},{10,... | collective-permute-start | bytes 24584 | tf_op jit(solution)/shard_map/ppermute | solution.py:152
  5.6 0.0 collective-permute-start.1
  5.6 0.2 collective-permute-start.2
  5.8 1.4 %collective-permute-done.refs_1_ = f32[1,2048]{1,0:T(1,128)S(1)} collective-permute-done((f32[1,2048]{1,0:T(1,128)S(1)}, f32[1,2048]{1,0:T(1,128)S(1)}, u32[]{:S(2)}, u32[]{:S(2)}) %collective-permute-start) | collective-permute-done | bytes 8224 | tf_op jit(solution)/shard_map/ppermute | solution.py:152
  7.2 1.4 %collective-permute-done.1.refs_2_ = f32[1,2048]{1,0:T(1,128)S(1)} collective-permute-done((f32[1,2048]{1,0:T(1,128)S(1)}, f32[1,2048]{1,0:T(1,128)S(1)}, u32[]{:S(2)}, u32[]{:S(2)}) %collective-permute-start.1) | collective-permute-done | bytes 8224 | tf_op jit(solution)/shard_map/ppermute | solution.py:152
  8.7 0.0 collective-permute-done.2.refs_3_
  8.7 0.0 copy-done
  8.7 0.0 copy-done.1
  8.7 0.0 copy-done.2
  8.7 0.0 copy-done.3
  8.7 0.0 copy-done.4
  8.7 0.6 %send_far.1 = (f32[32,512]{1,0:T(8,128)S(1)}, f32[32,512]{1,0:T(8,128)S(1)}, bf16[128,2048]{1,0:T(8,128)(2,1)S(1)}) custom-call(f32[16]{0:T(128)S(1)} %copy-done.4, f32[1,2048]{1,0:T(1,128)S(1)} %get-tuple-element.20.refs_0_, f32[1,2048]{1,0:T(1,128)S(1)} %collective-permute-done.refs_1_, f32[1,2048]{1,0:T(1,128)S(1)} %collective-permute-done.1.refs_2_, ...), custom_call_target="tpu_custom_call" | custom-call | flops 134217728 | bytes 524288 | tf_op jit(solution)/shard_map/send_far/pallas_call | solution.py:177
  9.3 1.6 %collective-permute-start.5 = (f32[32,512]{1,0:T(8,128)S(1)}, f32[32,512]{1,0:T(8,128)S(1)}, u32[]{:S(2)}, u32[]{:S(2)}) collective-permute-start(f32[32,512]{1,0:T(8,128)S(1)} %get-tuple-element.26), channel_id=1, source_target_pairs={{0,4},{1,5},{2,6},{3,7},{4,0},{5,1},{6,2},{7,3},{8,12},{9,13},{10,... | collective-permute-start | bytes 196616 | tf_op jit(solution)/shard_map/ppermute | solution.py:152
  10.9 0.5 %collective-permute-start.3 = (f32[32,512]{1,0:T(8,128)S(1)}, f32[32,512]{1,0:T(8,128)S(1)}, u32[]{:S(2)}, u32[]{:S(2)}) collective-permute-start(f32[32,512]{1,0:T(8,128)S(1)} %get-tuple-element.24), channel_id=1, source_target_pairs={{0,4},{1,5},{2,6},{3,7},{4,0},{5,1},{6,2},{7,3},{8,12},{9,13},{10,... | collective-permute-start | bytes 196616 | tf_op jit(solution)/shard_map/ppermute | solution.py:152
  11.4 0.8 %rest.1 = (f32[32,512]{1,0:T(8,128)S(1)}, f32[32,512]{1,0:T(8,128)S(1)}, f32[32,512]{1,0:T(8,128)S(1)}, f32[32,512]{1,0:T(8,128)S(1)}, f32[32,512]{1,0:T(8,128)S(1)}, /*index=5*/f32[32,512]{1,0:T(8,128)S(1)}) custom-call(bf16[128,2048]{1,0:T(8,128)(2,1)S(1)} %get-tuple-element.22.picks, bf16[2048,1024]{1,0:T(8,128)(2,1)S(1)} %get-tuple-element.21.refs_8_.held), custom_call_target="tpu_custom_call" | custom-call | flops 402653184 | bytes 1572864 | tf_op jit(solution)/shard_map/rest/pallas_call | solution.py:177
  12.3 1.6 %collective-permute-start.7 = (f32[32,512]{1,0:T(8,128)S(1)}, f32[32,512]{1,0:T(8,128)S(1)}, u32[]{:S(2)}, u32[]{:S(2)}) collective-permute-start(f32[32,512]{1,0:T(8,128)S(1)} %get-tuple-element.28), channel_id=1, source_target_pairs={{0,4},{1,5},{2,6},{3,7},{4,0},{5,1},{6,2},{7,3},{8,12},{9,13},{10,... | collective-permute-start | bytes 196616 | tf_op jit(solution)/shard_map/ppermute | solution.py:152
  13.8 0.5 %collective-permute-start.9 = (f32[32,512]{1,0:T(8,128)S(1)}, f32[32,512]{1,0:T(8,128)S(1)}, u32[]{:S(2)}, u32[]{:S(2)}) collective-permute-start(f32[32,512]{1,0:T(8,128)S(1)} %get-tuple-element.30), channel_id=1, source_target_pairs={{0,4},{1,5},{2,6},{3,7},{4,0},{5,1},{6,2},{7,3},{8,12},{9,13},{10,... | collective-permute-start | bytes 196616 | tf_op jit(solution)/shard_map/ppermute | solution.py:152
  14.3 0.0 collective-permute-done.5
  14.4 3.7 %collective-permute-start.6 = (f32[32,512]{1,0:T(8,128)S(1)}, f32[32,512]{1,0:T(8,128)S(1)}, u32[]{:S(2)}, u32[]{:S(2)}) collective-permute-start(f32[32,512]{1,0:T(8,128)S(1)} %add.23), channel_id=1, source_target_pairs={{0,24},{1,25},{2,26},{3,27},{4,28},{5,29},{6,30},{7,31},{8,16},{9,... | collective-permute-start | bytes 196616 | tf_op jit(solution)/shard_map/ppermute | solution.py:152
  18.0 0.0 collective-permute-done.3
  18.1 0.6 %collective-permute-start.4 = (f32[32,512]{1,0:T(8,128)S(1)}, f32[32,512]{1,0:T(8,128)S(1)}, u32[]{:S(2)}, u32[]{:S(2)}) collective-permute-start(f32[32,512]{1,0:T(8,128)S(1)} %add.22), channel_id=1, source_target_pairs={{0,16},{1,17},{2,18},{3,19},{4,20},{5,21},{6,22},{7,23},{8,24},{9,... | collective-permute-start | bytes 196616 | tf_op jit(solution)/shard_map/ppermute | solution.py:152
  18.7 0.0 collective-permute-done.7
  18.7 1.6 %collective-permute-start.8 = (f32[32,512]{1,0:T(8,128)S(1)}, f32[32,512]{1,0:T(8,128)S(1)}, u32[]{:S(2)}, u32[]{:S(2)}) collective-permute-start(f32[32,512]{1,0:T(8,128)S(1)} %add.25), channel_id=1, source_target_pairs={{0,8},{1,9},{2,10},{3,11},{4,12},{5,13},{6,14},{7,15},{8,0},{9,1},... | collective-permute-start | bytes 196616 | tf_op jit(solution)/shard_map/ppermute | solution.py:152
  20.3 0.3 collective-permute-done.6
  20.6 2.8 %collective-permute-done.4 = f32[32,512]{1,0:T(8,128)S(1)} collective-permute-done((f32[32,512]{1,0:T(8,128)S(1)}, f32[32,512]{1,0:T(8,128)S(1)}, u32[]{:S(2)}, u32[]{:S(2)}) %collective-permute-start.4) | collective-permute-done | bytes 65568 | tf_op jit(solution)/shard_map/ppermute | solution.py:152
  23.4 0.0 collective-permute-done.9
  23.4 0.3 collective-permute-done.8
  23.7 2.2 %collective-permute-start.11 = (f32[32,512]{1,0:T(8,128)S(1)}, f32[32,512]{1,0:T(8,128)S(1)}, u32[]{:S(2)}, u32[]{:S(2)}) collective-permute-start(f32[32,512]{1,0:T(8,128)S(1)} %add_add_fusion), channel_id=1, source_target_pairs={{0,24},{1,25},{2,26},{3,27},{4,28},{5,29},{6,30},{7,31},{8,16},{9,... | collective-permute-start | bytes 196616 | tf_op jit(solution)/shard_map/ppermute | solution.py:152
  25.9 0.1 collective-permute-start.13
  26.1 2.1 %collective-permute-start.15 = (f32[32,512]{1,0:T(8,128)S(1)}, f32[32,512]{1,0:T(8,128)S(1)}, u32[]{:S(2)}, u32[]{:S(2)}) collective-permute-start(f32[32,512]{1,0:T(8,128)S(1)} %add_add_fusion), channel_id=1, source_target_pairs={{0,16},{1,17},{2,18},{3,19},{4,20},{5,21},{6,22},{7,23},{8,24},{9,... | collective-permute-start | bytes 196616 | tf_op jit(solution)/shard_map/ppermute | solution.py:152
  28.2 0.5 %collective-permute-start.10 = (f32[32,512]{1,0:T(8,128)S(1)}, f32[32,512]{1,0:T(8,128)S(1)}, u32[]{:S(2)}, u32[]{:S(2)}) collective-permute-start(f32[32,512]{1,0:T(8,128)S(1)} %add_add_fusion), channel_id=1, source_target_pairs={{0,2},{1,0},{2,3},{3,1},{4,6},{5,4},{6,7},{7,5},{8,9},{9,11},{10,8... | collective-permute-start | bytes 196616 | tf_op jit(solution)/shard_map/ppermute | solution.py:253
  28.7 1.6 %collective-permute-done.11 = f32[32,512]{1,0:T(8,128)S(1)} collective-permute-done((f32[32,512]{1,0:T(8,128)S(1)}, f32[32,512]{1,0:T(8,128)S(1)}, u32[]{:S(2)}, u32[]{:S(2)}) %collective-permute-start.11) | collective-permute-done | bytes 65568 | tf_op jit(solution)/shard_map/ppermute | solution.py:152
  30.3 0.8 %collective-permute-start.17 = (f32[64,512]{1,0:T(8,128)S(1)}, f32[64,512]{1,0:T(8,128)S(1)}, u32[]{:S(2)}, u32[]{:S(2)}) collective-permute-start(f32[64,512]{1,0:T(8,128)S(1)} %pad_maximum_fusion.1.refs_4_), channel_id=1, source_target_pairs={{0,4},{1,5},{2,6},{3,7},{4,0},{5,1},{6,2},{7,3},{8,12},{9,13},{10,... | collective-permute-start | bytes 393224 | tf_op jit(solution)/shard_map/ppermute | solution.py:152
  31.1 0.9 %collective-permute-start.12 = (f32[32,512]{1,0:T(8,128)S(1)}, f32[32,512]{1,0:T(8,128)S(1)}, u32[]{:S(2)}, u32[]{:S(2)}) collective-permute-start(f32[32,512]{1,0:T(8,128)S(1)} %collective-permute-done.11), channel_id=1, source_target_pairs={{0,2},{1,0},{2,3},{3,1},{4,6},{5,4},{6,7},{7,5},{8,9},{9,11},{10,8... | collective-permute-start | bytes 196616 | tf_op jit(solution)/shard_map/ppermute | solution.py:253
  32.0 0.0 collective-permute-done.13
  32.0 0.0 collective-permute-start.14
  32.0 0.0 collective-permute-done.15
  32.0 0.3 collective-permute-start.16
  32.4 0.0 collective-permute-done.10
  32.4 1.6 %collective-permute-start.22 = (f32[64,512]{1,0:T(8,128)S(1)}, f32[64,512]{1,0:T(8,128)S(1)}, u32[]{:S(2)}, u32[]{:S(2)}) collective-permute-start(f32[64,512]{1,0:T(8,128)S(1)} %constant_dynamic-update-slice_fusion.refs_5_), channel_id=1, source_target_pairs={{0,4},{1,5},{2,6},{3,7},{4,0},{5,1},{6,2},{7,3},{8,12},{9,13},{10,... | collective-permute-start | bytes 393224 | tf_op jit(solution)/shard_map/ppermute | solution.py:152
  33.9 0.0 collective-permute-done.12
  34.0 0.6 %collective-permute-done.14 = f32[32,512]{1,0:T(8,128)S(1)} collective-permute-done((f32[32,512]{1,0:T(8,128)S(1)}, f32[32,512]{1,0:T(8,128)S(1)}, u32[]{:S(2)}, u32[]{:S(2)}) %collective-permute-start.14) | collective-permute-done | bytes 65568 | tf_op jit(solution)/shard_map/ppermute | solution.py:253
  34.5 0.7 %collective-permute-done.16 = f32[32,512]{1,0:T(8,128)S(1)} collective-permute-done((f32[32,512]{1,0:T(8,128)S(1)}, f32[32,512]{1,0:T(8,128)S(1)}, u32[]{:S(2)}, u32[]{:S(2)}) %collective-permute-start.16) | collective-permute-done | bytes 65568 | tf_op jit(solution)/shard_map/ppermute | solution.py:253
  35.2 0.1 collective-permute-done.17.refs_0_
  35.4 0.5 %collective-permute-start.18 = (f32[32,512]{1,0:T(8,128)S(1)}, f32[32,512]{1,0:T(8,128)S(1)}, u32[]{:S(2)}, u32[]{:S(2)}) collective-permute-start(f32[32,512]{1,0:T(8,128)S(1)} %get-tuple-element.38), channel_id=1, source_target_pairs={{0,1},{1,0},{2,3},{3,2},{4,5},{5,4},{6,7},{7,6},{8,9},{9,8},{10,11... | collective-permute-start | bytes 196616 | tf_op jit(solution)/shard_map/ppermute | solution.py:152
  35.9 0.1 collective-permute-start.19
  36.0 0.4 %collective-permute-start.20 = (f32[32,512]{1,0:T(8,128)S(1)}, f32[32,512]{1,0:T(8,128)S(1)}, u32[]{:S(2)}, u32[]{:S(2)}) collective-permute-start(f32[32,512]{1,0:T(8,128)S(1)} %get-tuple-element.36), channel_id=1, source_target_pairs={{0,1},{1,0},{2,3},{3,2},{4,5},{5,4},{6,7},{7,6},{8,9},{9,8},{10,11... | collective-permute-start | bytes 196616 | tf_op jit(solution)/shard_map/ppermute | solution.py:152
  36.4 0.1 collective-permute-start.21
  36.5 0.3 collective-permute-done.18.refs_0_
  36.8 0.4 collective-permute-done.19.refs_1_
  37.1 0.2 collective-permute-done.20.refs_2_
  37.3 0.4 collective-permute-done.21.refs_3_
  37.6 0.5 %meat_own.1 = (f32[2,512,256]{2,1,0:T(8,128)S(1)}, bf16[256,512]{1,0:T(8,128)(2,1)S(1)}) custom-call(f32[128,512]{1,0:T(8,128)S(1)} %maximum_select_fusion.have, f32[32,512]{1,0:T(8,128)S(1)} %collective-permute-done.18.refs_0_, f32[32,512]{1,0:T(8,128)S(1)} %collective-permute-done.19.refs_1_, f32[32,512]{1,0:T(8,128)S(1)} %collective-permute-done.20.refs_2_, ...), custom_call_target="tpu_custom_call" | custom-call | flops 201326592 | bytes 786432 | tf_op jit(solution)/shard_map/meat_own/pallas_call | solution.py:177
  38.1 0.0 collective-permute-done.22.refs_1_
  38.1 1.5 %meat_other.1 = f32[512,1024]{1,0:T(8,128)} custom-call(f32[2,512,256]{2,1,0:T(8,128)S(1)} %get-tuple-element.32.first, bf16[256,512]{1,0:T(8,128)(2,1)S(1)} %get-tuple-element.33.left, f32[64,512]{1,0:T(8,128)S(1)} %collective-permute-done.17.refs_0_, f32[64,512]{1,0:T(8,128)S(1)} %collective-permute-done.22.refs_1_), custom_call_target="tpu_custom_call" | custom-call | flops 201326592 | bytes 2097152 | tf_op jit(solution)/shard_map/meat_other/pallas_call | solution.py:268
  (11 shorter events, 0.2 us)
Async XLA Ops:
  0.0 8.7 %copy-start = (f32[2048]{0:T(1024)S(1)}, f32[2048]{0:T(1024)}, u32[]{:S(2)}) copy-start(f32[2048]{0:T(1024)} %param.9) | copy-start | bytes 24580
  0.0 8.7 %copy-start.1 = (f32[2048]{0:T(1024)S(1)}, f32[2048]{0:T(1024)}, u32[]{:S(2)}) copy-start(f32[2048]{0:T(1024)} %param.10) | copy-start | bytes 24580
  0.0 8.7 %copy-start.2 = (s32[2048]{0:T(1024)S(1)}, s32[2048]{0:T(1024)}, u32[]{:S(2)}) copy-start(s32[2048]{0:T(1024)} %param.11) | copy-start | bytes 24580
  0.0 8.7 %copy-start.3 = (s32[2048]{0:T(1024)S(1)}, s32[2048]{0:T(1024)}, u32[]{:S(2)}) copy-start(s32[2048]{0:T(1024)} %param.12) | copy-start | bytes 24580
  0.0 8.7 %copy-start.4 = (f32[16]{0:T(128)S(1)}, f32[16]{0:T(128)}, u32[]{:S(2)}) copy-start(f32[16]{0:T(128)} %effect.1) | copy-start | bytes 196
  2.6 4.6 %collective-permute-start = (f32[1,2048]{1,0:T(1,128)S(1)}, f32[1,2048]{1,0:T(1,128)S(1)}, u32[]{:S(2)}, u32[]{:S(2)}) collective-permute-start(f32[1,2048]{1,0:T(1,128)S(1)} %get-tuple-element.20.refs_0_), channel_id=1, source_target_pairs={{0,2},{1,3},{2,0},{3,1},{4,6},{5,7},{6,4},{7,5},{8,10},{9,11},{10,... | collective-permute-start | bytes 24584 | tf_op jit(solution)/shard_map/ppermute | solution.py:152
  5.6 3.1 %collective-permute-start.1 = (f32[1,2048]{1,0:T(1,128)S(1)}, f32[1,2048]{1,0:T(1,128)S(1)}, u32[]{:S(2)}, u32[]{:S(2)}) collective-permute-start(f32[1,2048]{1,0:T(1,128)S(1)} %get-tuple-element.20.refs_0_), channel_id=1, source_target_pairs={{0,3},{1,2},{2,1},{3,0},{4,7},{5,6},{6,5},{7,4},{8,11},{9,10},{10,... | collective-permute-start | bytes 24584 | tf_op jit(solution)/shard_map/ppermute | solution.py:152
  5.6 3.1 %collective-permute-start.2 = (f32[1,2048]{1,0:T(1,128)S(1)}, f32[1,2048]{1,0:T(1,128)S(1)}, u32[]{:S(2)}, u32[]{:S(2)}) collective-permute-start(f32[1,2048]{1,0:T(1,128)S(1)} %get-tuple-element.20.refs_0_), channel_id=1, source_target_pairs={{0,1},{1,0},{2,3},{3,2},{4,5},{5,4},{6,7},{7,6},{8,9},{9,8},{10,11... | collective-permute-start | bytes 24584 | tf_op jit(solution)/shard_map/ppermute | solution.py:152
  9.3 5.0 %collective-permute-start.5 = (f32[32,512]{1,0:T(8,128)S(1)}, f32[32,512]{1,0:T(8,128)S(1)}, u32[]{:S(2)}, u32[]{:S(2)}) collective-permute-start(f32[32,512]{1,0:T(8,128)S(1)} %get-tuple-element.26), channel_id=1, source_target_pairs={{0,4},{1,5},{2,6},{3,7},{4,0},{5,1},{6,2},{7,3},{8,12},{9,13},{10,... | collective-permute-start | bytes 196616 | tf_op jit(solution)/shard_map/ppermute | solution.py:152
  10.9 7.1 %collective-permute-start.3 = (f32[32,512]{1,0:T(8,128)S(1)}, f32[32,512]{1,0:T(8,128)S(1)}, u32[]{:S(2)}, u32[]{:S(2)}) collective-permute-start(f32[32,512]{1,0:T(8,128)S(1)} %get-tuple-element.24), channel_id=1, source_target_pairs={{0,4},{1,5},{2,6},{3,7},{4,0},{5,1},{6,2},{7,3},{8,12},{9,13},{10,... | collective-permute-start | bytes 196616 | tf_op jit(solution)/shard_map/ppermute | solution.py:152
  12.3 6.4 %collective-permute-start.7 = (f32[32,512]{1,0:T(8,128)S(1)}, f32[32,512]{1,0:T(8,128)S(1)}, u32[]{:S(2)}, u32[]{:S(2)}) collective-permute-start(f32[32,512]{1,0:T(8,128)S(1)} %get-tuple-element.28), channel_id=1, source_target_pairs={{0,4},{1,5},{2,6},{3,7},{4,0},{5,1},{6,2},{7,3},{8,12},{9,13},{10,... | collective-permute-start | bytes 196616 | tf_op jit(solution)/shard_map/ppermute | solution.py:152
  13.8 9.6 %collective-permute-start.9 = (f32[32,512]{1,0:T(8,128)S(1)}, f32[32,512]{1,0:T(8,128)S(1)}, u32[]{:S(2)}, u32[]{:S(2)}) collective-permute-start(f32[32,512]{1,0:T(8,128)S(1)} %get-tuple-element.30), channel_id=1, source_target_pairs={{0,4},{1,5},{2,6},{3,7},{4,0},{5,1},{6,2},{7,3},{8,12},{9,13},{10,... | collective-permute-start | bytes 196616 | tf_op jit(solution)/shard_map/ppermute | solution.py:152
  14.4 6.2 %collective-permute-start.6 = (f32[32,512]{1,0:T(8,128)S(1)}, f32[32,512]{1,0:T(8,128)S(1)}, u32[]{:S(2)}, u32[]{:S(2)}) collective-permute-start(f32[32,512]{1,0:T(8,128)S(1)} %add.23), channel_id=1, source_target_pairs={{0,24},{1,25},{2,26},{3,27},{4,28},{5,29},{6,30},{7,31},{8,16},{9,... | collective-permute-start | bytes 196616 | tf_op jit(solution)/shard_map/ppermute | solution.py:152
  18.1 5.3 %collective-permute-start.4 = (f32[32,512]{1,0:T(8,128)S(1)}, f32[32,512]{1,0:T(8,128)S(1)}, u32[]{:S(2)}, u32[]{:S(2)}) collective-permute-start(f32[32,512]{1,0:T(8,128)S(1)} %add.22), channel_id=1, source_target_pairs={{0,16},{1,17},{2,18},{3,19},{4,20},{5,21},{6,22},{7,23},{8,24},{9,... | collective-permute-start | bytes 196616 | tf_op jit(solution)/shard_map/ppermute | solution.py:152
  18.7 5.0 %collective-permute-start.8 = (f32[32,512]{1,0:T(8,128)S(1)}, f32[32,512]{1,0:T(8,128)S(1)}, u32[]{:S(2)}, u32[]{:S(2)}) collective-permute-start(f32[32,512]{1,0:T(8,128)S(1)} %add.25), channel_id=1, source_target_pairs={{0,8},{1,9},{2,10},{3,11},{4,12},{5,13},{6,14},{7,15},{8,0},{9,1},... | collective-permute-start | bytes 196616 | tf_op jit(solution)/shard_map/ppermute | solution.py:152
  23.7 6.6 %collective-permute-start.11 = (f32[32,512]{1,0:T(8,128)S(1)}, f32[32,512]{1,0:T(8,128)S(1)}, u32[]{:S(2)}, u32[]{:S(2)}) collective-permute-start(f32[32,512]{1,0:T(8,128)S(1)} %add_add_fusion), channel_id=1, source_target_pairs={{0,24},{1,25},{2,26},{3,27},{4,28},{5,29},{6,30},{7,31},{8,16},{9,... | collective-permute-start | bytes 196616 | tf_op jit(solution)/shard_map/ppermute | solution.py:152
  25.9 6.1 %collective-permute-start.13 = (f32[32,512]{1,0:T(8,128)S(1)}, f32[32,512]{1,0:T(8,128)S(1)}, u32[]{:S(2)}, u32[]{:S(2)}) collective-permute-start(f32[32,512]{1,0:T(8,128)S(1)} %add_add_fusion), channel_id=1, source_target_pairs={{0,8},{1,9},{2,10},{3,11},{4,12},{5,13},{6,14},{7,15},{8,0},{9,1},... | collective-permute-start | bytes 196616 | tf_op jit(solution)/shard_map/ppermute | solution.py:152
  26.1 6.0 %collective-permute-start.15 = (f32[32,512]{1,0:T(8,128)S(1)}, f32[32,512]{1,0:T(8,128)S(1)}, u32[]{:S(2)}, u32[]{:S(2)}) collective-permute-start(f32[32,512]{1,0:T(8,128)S(1)} %add_add_fusion), channel_id=1, source_target_pairs={{0,16},{1,17},{2,18},{3,19},{4,20},{5,21},{6,22},{7,23},{8,24},{9,... | collective-permute-start | bytes 196616 | tf_op jit(solution)/shard_map/ppermute | solution.py:152
  28.2 4.2 %collective-permute-start.10 = (f32[32,512]{1,0:T(8,128)S(1)}, f32[32,512]{1,0:T(8,128)S(1)}, u32[]{:S(2)}, u32[]{:S(2)}) collective-permute-start(f32[32,512]{1,0:T(8,128)S(1)} %add_add_fusion), channel_id=1, source_target_pairs={{0,2},{1,0},{2,3},{3,1},{4,6},{5,4},{6,7},{7,5},{8,9},{9,11},{10,8... | collective-permute-start | bytes 196616 | tf_op jit(solution)/shard_map/ppermute | solution.py:253
  30.3 5.0 %collective-permute-start.17 = (f32[64,512]{1,0:T(8,128)S(1)}, f32[64,512]{1,0:T(8,128)S(1)}, u32[]{:S(2)}, u32[]{:S(2)}) collective-permute-start(f32[64,512]{1,0:T(8,128)S(1)} %pad_maximum_fusion.1.refs_4_), channel_id=1, source_target_pairs={{0,4},{1,5},{2,6},{3,7},{4,0},{5,1},{6,2},{7,3},{8,12},{9,13},{10,... | collective-permute-start | bytes 393224 | tf_op jit(solution)/shard_map/ppermute | solution.py:152
  31.1 2.8 %collective-permute-start.12 = (f32[32,512]{1,0:T(8,128)S(1)}, f32[32,512]{1,0:T(8,128)S(1)}, u32[]{:S(2)}, u32[]{:S(2)}) collective-permute-start(f32[32,512]{1,0:T(8,128)S(1)} %collective-permute-done.11), channel_id=1, source_target_pairs={{0,2},{1,0},{2,3},{3,1},{4,6},{5,4},{6,7},{7,5},{8,9},{9,11},{10,8... | collective-permute-start | bytes 196616 | tf_op jit(solution)/shard_map/ppermute | solution.py:253
  32.0 2.5 %collective-permute-start.14 = (f32[32,512]{1,0:T(8,128)S(1)}, f32[32,512]{1,0:T(8,128)S(1)}, u32[]{:S(2)}, u32[]{:S(2)}) collective-permute-start(f32[32,512]{1,0:T(8,128)S(1)} %collective-permute-done.13), channel_id=1, source_target_pairs={{0,2},{1,0},{2,3},{3,1},{4,6},{5,4},{6,7},{7,5},{8,9},{9,11},{10,8... | collective-permute-start | bytes 196616 | tf_op jit(solution)/shard_map/ppermute | solution.py:253
  32.0 3.1 %collective-permute-start.16 = (f32[32,512]{1,0:T(8,128)S(1)}, f32[32,512]{1,0:T(8,128)S(1)}, u32[]{:S(2)}, u32[]{:S(2)}) collective-permute-start(f32[32,512]{1,0:T(8,128)S(1)} %collective-permute-done.15), channel_id=1, source_target_pairs={{0,2},{1,0},{2,3},{3,1},{4,6},{5,4},{6,7},{7,5},{8,9},{9,11},{10,8... | collective-permute-start | bytes 196616 | tf_op jit(solution)/shard_map/ppermute | solution.py:253
  32.4 5.8 %collective-permute-start.22 = (f32[64,512]{1,0:T(8,128)S(1)}, f32[64,512]{1,0:T(8,128)S(1)}, u32[]{:S(2)}, u32[]{:S(2)}) collective-permute-start(f32[64,512]{1,0:T(8,128)S(1)} %constant_dynamic-update-slice_fusion.refs_5_), channel_id=1, source_target_pairs={{0,4},{1,5},{2,6},{3,7},{4,0},{5,1},{6,2},{7,3},{8,12},{9,13},{10,... | collective-permute-start | bytes 393224 | tf_op jit(solution)/shard_map/ppermute | solution.py:152
  35.4 1.4 %collective-permute-start.18 = (f32[32,512]{1,0:T(8,128)S(1)}, f32[32,512]{1,0:T(8,128)S(1)}, u32[]{:S(2)}, u32[]{:S(2)}) collective-permute-start(f32[32,512]{1,0:T(8,128)S(1)} %get-tuple-element.38), channel_id=1, source_target_pairs={{0,1},{1,0},{2,3},{3,2},{4,5},{5,4},{6,7},{7,6},{8,9},{9,8},{10,11... | collective-permute-start | bytes 196616 | tf_op jit(solution)/shard_map/ppermute | solution.py:152
  35.9 1.3 %collective-permute-start.19 = (f32[32,512]{1,0:T(8,128)S(1)}, f32[32,512]{1,0:T(8,128)S(1)}, u32[]{:S(2)}, u32[]{:S(2)}) collective-permute-start(f32[32,512]{1,0:T(8,128)S(1)} %get-tuple-element.37), channel_id=1, source_target_pairs={{0,1},{1,0},{2,3},{3,2},{4,5},{5,4},{6,7},{7,6},{8,9},{9,8},{10,11... | collective-permute-start | bytes 196616 | tf_op jit(solution)/shard_map/ppermute | solution.py:152
  36.0 1.3 %collective-permute-start.20 = (f32[32,512]{1,0:T(8,128)S(1)}, f32[32,512]{1,0:T(8,128)S(1)}, u32[]{:S(2)}, u32[]{:S(2)}) collective-permute-start(f32[32,512]{1,0:T(8,128)S(1)} %get-tuple-element.36), channel_id=1, source_target_pairs={{0,1},{1,0},{2,3},{3,2},{4,5},{5,4},{6,7},{7,6},{8,9},{9,8},{10,11... | collective-permute-start | bytes 196616 | tf_op jit(solution)/shard_map/ppermute | solution.py:152
  36.4 1.3 %collective-permute-start.21 = (f32[32,512]{1,0:T(8,128)S(1)}, f32[32,512]{1,0:T(8,128)S(1)}, u32[]{:S(2)}, u32[]{:S(2)}) collective-permute-start(f32[32,512]{1,0:T(8,128)S(1)} %get-tuple-element.35), channel_id=1, source_target_pairs={{0,1},{1,0},{2,3},{3,2},{4,5},{5,4},{6,7},{7,6},{8,9},{9,8},{10,11... | collective-permute-start | bytes 196616 | tf_op jit(solution)/shard_map/ppermute | solution.py:152

commit v7 on v6

--- a/solution.py
+++ b/solution.py
@@ -223,7 +223,15 @@
     for k in [*range(n_gr // 2 + 2, n_gr), *range(1, n_gr // 2)]:
         owned = owned + arrived[k]
     owned = owned + parts[0]
-    gathered = [owned] + [swap(owned, k * fan, 0) for k in [3, 1, 2]]
+    def along(value, k):
+        table = [[2, 0, 3, 1], [1, 3, 0, 2], [3, 2, 1, 0]][k]
+        pairs = []
+        for c in range(n_cal):
+            there = (table[c // fan] if n_gr == 4 else (c // fan) ^ (k + 1)) * fan + c % fan
+            pairs += [(c * n_gr + g, there * n_gr + g) for g in range(n_gr)]
+        return lax.ppermute(value, AXES, pairs)
+
+    gathered = [owned] + [along(owned, k) for k in range(n_gr - 1)]
     blocks = [jnp.concatenate(gathered[0:2], axis=0), jnp.concatenate(gathered[2:4], axis=0)]
     sides, others = [], []
     for side in blocks:
@@ -262,7 +270,7 @@
     first, left = kernel(
         functools.partial(own_kernel, scale),
         (jax.ShapeDtypeStruct((parts, wide, block), f32), jax.ShapeDtypeStruct((2 * clusters, wide), bf16)),
-        (have, *got, *sides), 0, "meat_own", work,
+        (have, *got, *sides), 0, "meat_own",
     )
     args = (first, left, *others)
     return pl.pallas_call(

time: 39.8 us -> 39.6 us (level)
  waiting for transfers between devices: 10.4 us -> 9.19 us
  starting transfers between devices: 22.9 us -> 24 us
    ppermute x0 -> x3, starting transfers between devices: none -> 4.22 us  [along(): return lax.ppermute(value, AXES, pairs)]
    ppermute x19 -> x16, starting transfers between devices: 21.2 us -> 17.5 us  [exchange(): return lax.ppermute(value, AXES, pairs)]
    ppermute x19 -> x16, waiting for transfers between devices: 9.15 us -> 8.05 us  [exchange(): return lax.ppermute(value, AXES, pairs)]
    ppermute x4, waiting for transfers between devices: 1.23 us -> 0.42 us  [per_device(): lax.ppermute(have[i:i + clusters // 4], AXES, pairs)]
    ppermute x0 -> x3, waiting for transfers between devices: none -> 0.71 us  [along(): return lax.ppermute(value, AXES, pairs)]
    ppermute x4, starting transfers between devices: 1.77 us -> 2.27 us  [per_device(): lax.ppermute(have[i:i + clusters // 4], AXES, pairs)]
  transfers between devices with their start and end apart: 23 -> 23, of which waited for: 13 -> 12; matrix products, arithmetic and copies ran while one was open for 0% -> 0% of each run, Pallas kernels for 3% -> 3%
where the time goes in v7:
time: 39.6 us; the launch traced here: 39.4 us
  starting transfers between devices  24 us (61%)
  waiting for transfers between devices  9.19 us (23%)
  Pallas kernels  5.96 us (15%)
    ppermute x16, starting transfers between devices, exchange(): return lax.ppermute(value, AXES, pairs)  17.5 us
    ppermute x16, waiting for transfers between devices, exchange(): return lax.ppermute(value, AXES, pairs)  8.05 us
    ppermute x3, starting transfers between devices, along(): return lax.ppermute(value, AXES, pairs)  4.22 us
    pallas_call x1, Pallas kernels, per_device(): pl.pallas_call(linear_kernel, out_shape=(jax.ShapeDtypeStruct((1, rows),...  2.57 us
    ppermute x4, starting transfers between devices, per_device(): lax.ppermute(have[i:i + clusters // 4], AXES, pairs)  2.27 us
    pallas_call x3, Pallas kernels, kernel(): return call(*args)  1.92 us
    pallas_call x1, Pallas kernels, per_device(): pl.pallas_call(functools.partial(other_kernel, scale), out_shape=jax.Shap...  1.47 us
  transfers between devices with their start and end apart: 23, of which 12 were waited for; matrix products, arithmetic and copies ran while one was open for 0% of the time, Pallas kernels for 3%

profile of v7, /device:TPU:0, one launch (start us, length us, event | category | flops | bytes accessed | tf_op | source)
XLA Modules:
  0.0 39.4 jit_solution(3478480680612440323)
XLA Ops:
  0.0 0.0 copy-start
  0.0 0.0 copy-start.1
  0.0 0.0 copy-start.2
  0.0 0.0 copy-start.3
  0.0 0.0 copy-start.4
  0.0 2.6 %linear.1 = (f32[1,2048]{1,0:T(1,128)S(1)}, bf16[2048,1024]{1,0:T(8,128)(2,1)S(1)}) custom-call(bf16[2048,1024]{1,0:T(8,128)(2,1)} %feats.1, bf16[1024]{0:T(1024)(128)(2,1)} %coef.1), custom_call_target="tpu_custom_call" | custom-call | flops 4194304 | bytes 4194304 | tf_op jit(solution)/shard_map/linear/pallas_call | solution.py:181
  2.6 3.0 %collective-permute-start = (f32[1,2048]{1,0:T(1,128)S(1)}, f32[1,2048]{1,0:T(1,128)S(1)}, u32[]{:S(2)}, u32[]{:S(2)}) collective-permute-start(f32[1,2048]{1,0:T(1,128)S(1)} %get-tuple-element.20.refs_0_), channel_id=1, source_target_pairs={{0,2},{1,3},{2,0},{3,1},{4,6},{5,7},{6,4},{7,5},{8,10},{9,11},{10,... | collective-permute-start | bytes 24584 | tf_op jit(solution)/shard_map/ppermute | solution.py:152
  5.6 0.0 collective-permute-start.1
  5.6 0.2 collective-permute-start.2
  5.8 1.4 %collective-permute-done.refs_1_ = f32[1,2048]{1,0:T(1,128)S(1)} collective-permute-done((f32[1,2048]{1,0:T(1,128)S(1)}, f32[1,2048]{1,0:T(1,128)S(1)}, u32[]{:S(2)}, u32[]{:S(2)}) %collective-permute-start) | collective-permute-done | bytes 8224 | tf_op jit(solution)/shard_map/ppermute | solution.py:152
  7.2 1.4 %collective-permute-done.1.refs_2_ = f32[1,2048]{1,0:T(1,128)S(1)} collective-permute-done((f32[1,2048]{1,0:T(1,128)S(1)}, f32[1,2048]{1,0:T(1,128)S(1)}, u32[]{:S(2)}, u32[]{:S(2)}) %collective-permute-start.1) | collective-permute-done | bytes 8224 | tf_op jit(solution)/shard_map/ppermute | solution.py:152
  8.7 0.0 collective-permute-done.2.refs_3_
  8.7 0.0 copy-done
  8.7 0.0 copy-done.1
  8.7 0.0 copy-done.2
  8.7 0.0 copy-done.3
  8.7 0.0 copy-done.4
  8.7 0.6 %send_far.1 = (f32[32,512]{1,0:T(8,128)S(1)}, f32[32,512]{1,0:T(8,128)S(1)}, bf16[128,2048]{1,0:T(8,128)(2,1)S(1)}) custom-call(f32[16]{0:T(128)S(1)} %copy-done.4, f32[1,2048]{1,0:T(1,128)S(1)} %get-tuple-element.20.refs_0_, f32[1,2048]{1,0:T(1,128)S(1)} %collective-permute-done.refs_1_, f32[1,2048]{1,0:T(1,128)S(1)} %collective-permute-done.1.refs_2_, ...), custom_call_target="tpu_custom_call" | custom-call | flops 134217728 | bytes 524288 | tf_op jit(solution)/shard_map/send_far/pallas_call | solution.py:177
  9.3 1.6 %collective-permute-start.5 = (f32[32,512]{1,0:T(8,128)S(1)}, f32[32,512]{1,0:T(8,128)S(1)}, u32[]{:S(2)}, u32[]{:S(2)}) collective-permute-start(f32[32,512]{1,0:T(8,128)S(1)} %get-tuple-element.26), channel_id=1, source_target_pairs={{0,4},{1,5},{2,6},{3,7},{4,0},{5,1},{6,2},{7,3},{8,12},{9,13},{10,... | collective-permute-start | bytes 196616 | tf_op jit(solution)/shard_map/ppermute | solution.py:152
  10.9 0.5 %collective-permute-start.3 = (f32[32,512]{1,0:T(8,128)S(1)}, f32[32,512]{1,0:T(8,128)S(1)}, u32[]{:S(2)}, u32[]{:S(2)}) collective-permute-start(f32[32,512]{1,0:T(8,128)S(1)} %get-tuple-element.24), channel_id=1, source_target_pairs={{0,4},{1,5},{2,6},{3,7},{4,0},{5,1},{6,2},{7,3},{8,12},{9,13},{10,... | collective-permute-start | bytes 196616 | tf_op jit(solution)/shard_map/ppermute | solution.py:152
  11.4 0.8 %rest.1 = (f32[32,512]{1,0:T(8,128)S(1)}, f32[32,512]{1,0:T(8,128)S(1)}, f32[32,512]{1,0:T(8,128)S(1)}, f32[32,512]{1,0:T(8,128)S(1)}, f32[32,512]{1,0:T(8,128)S(1)}, /*index=5*/f32[32,512]{1,0:T(8,128)S(1)}) custom-call(bf16[128,2048]{1,0:T(8,128)(2,1)S(1)} %get-tuple-element.22.picks, bf16[2048,1024]{1,0:T(8,128)(2,1)S(1)} %get-tuple-element.21.refs_8_.held), custom_call_target="tpu_custom_call" | custom-call | flops 402653184 | bytes 1572864 | tf_op jit(solution)/shard_map/rest/pallas_call | solution.py:177
  12.3 1.6 %collective-permute-start.7 = (f32[32,512]{1,0:T(8,128)S(1)}, f32[32,512]{1,0:T(8,128)S(1)}, u32[]{:S(2)}, u32[]{:S(2)}) collective-permute-start(f32[32,512]{1,0:T(8,128)S(1)} %get-tuple-element.28), channel_id=1, source_target_pairs={{0,4},{1,5},{2,6},{3,7},{4,0},{5,1},{6,2},{7,3},{8,12},{9,13},{10,... | collective-permute-start | bytes 196616 | tf_op jit(solution)/shard_map/ppermute | solution.py:152
  13.8 0.5 %collective-permute-start.9 = (f32[32,512]{1,0:T(8,128)S(1)}, f32[32,512]{1,0:T(8,128)S(1)}, u32[]{:S(2)}, u32[]{:S(2)}) collective-permute-start(f32[32,512]{1,0:T(8,128)S(1)} %get-tuple-element.30), channel_id=1, source_target_pairs={{0,4},{1,5},{2,6},{3,7},{4,0},{5,1},{6,2},{7,3},{8,12},{9,13},{10,... | collective-permute-start | bytes 196616 | tf_op jit(solution)/shard_map/ppermute | solution.py:152
  14.3 0.0 collective-permute-done.5
  14.4 3.7 %collective-permute-start.6 = (f32[32,512]{1,0:T(8,128)S(1)}, f32[32,512]{1,0:T(8,128)S(1)}, u32[]{:S(2)}, u32[]{:S(2)}) collective-permute-start(f32[32,512]{1,0:T(8,128)S(1)} %add.23), channel_id=1, source_target_pairs={{0,24},{1,25},{2,26},{3,27},{4,28},{5,29},{6,30},{7,31},{8,16},{9,... | collective-permute-start | bytes 196616 | tf_op jit(solution)/shard_map/ppermute | solution.py:152
  18.0 0.0 collective-permute-done.3
  18.1 0.6 %collective-permute-start.4 = (f32[32,512]{1,0:T(8,128)S(1)}, f32[32,512]{1,0:T(8,128)S(1)}, u32[]{:S(2)}, u32[]{:S(2)}) collective-permute-start(f32[32,512]{1,0:T(8,128)S(1)} %add.22), channel_id=1, source_target_pairs={{0,16},{1,17},{2,18},{3,19},{4,20},{5,21},{6,22},{7,23},{8,24},{9,... | collective-permute-start | bytes 196616 | tf_op jit(solution)/shard_map/ppermute | solution.py:152
  18.7 0.0 collective-permute-done.7
  18.7 1.6 %collective-permute-start.8 = (f32[32,512]{1,0:T(8,128)S(1)}, f32[32,512]{1,0:T(8,128)S(1)}, u32[]{:S(2)}, u32[]{:S(2)}) collective-permute-start(f32[32,512]{1,0:T(8,128)S(1)} %add.25), channel_id=1, source_target_pairs={{0,8},{1,9},{2,10},{3,11},{4,12},{5,13},{6,14},{7,15},{8,0},{9,1},... | collective-permute-start | bytes 196616 | tf_op jit(solution)/shard_map/ppermute | solution.py:152
  20.3 0.3 collective-permute-done.6
  20.6 2.8 %collective-permute-done.4 = f32[32,512]{1,0:T(8,128)S(1)} collective-permute-done((f32[32,512]{1,0:T(8,128)S(1)}, f32[32,512]{1,0:T(8,128)S(1)}, u32[]{:S(2)}, u32[]{:S(2)}) %collective-permute-start.4) | collective-permute-done | bytes 65568 | tf_op jit(solution)/shard_map/ppermute | solution.py:152
  23.4 0.0 collective-permute-done.9
  23.4 0.3 collective-permute-done.8
  23.7 1.7 %collective-permute-start.11 = (f32[32,512]{1,0:T(8,128)S(1)}, f32[32,512]{1,0:T(8,128)S(1)}, u32[]{:S(2)}, u32[]{:S(2)}) collective-permute-start(f32[32,512]{1,0:T(8,128)S(1)} %add_add_fusion), channel_id=1, source_target_pairs={{0,16},{1,17},{2,18},{3,19},{4,20},{5,21},{6,22},{7,23},{8,0},{9,1... | collective-permute-start | bytes 196616 | tf_op jit(solution)/shard_map/ppermute | solution.py:232
  25.5 0.3 collective-permute-start.13
  25.8 2.1 %collective-permute-start.15 = (f32[32,512]{1,0:T(8,128)S(1)}, f32[32,512]{1,0:T(8,128)S(1)}, u32[]{:S(2)}, u32[]{:S(2)}) collective-permute-start(f32[32,512]{1,0:T(8,128)S(1)} %add_add_fusion), channel_id=1, source_target_pairs={{0,24},{1,25},{2,26},{3,27},{4,28},{5,29},{6,30},{7,31},{8,16},{9,... | collective-permute-start | bytes 196616 | tf_op jit(solution)/shard_map/ppermute | solution.py:232
  27.9 1.1 %collective-permute-start.10 = (f32[32,512]{1,0:T(8,128)S(1)}, f32[32,512]{1,0:T(8,128)S(1)}, u32[]{:S(2)}, u32[]{:S(2)}) collective-permute-start(f32[32,512]{1,0:T(8,128)S(1)} %add_add_fusion), channel_id=1, source_target_pairs={{0,2},{1,0},{2,3},{3,1},{4,6},{5,4},{6,7},{7,5},{8,9},{9,11},{10,8... | collective-permute-start | bytes 196616 | tf_op jit(solution)/shard_map/ppermute | solution.py:261
  29.1 0.0 collective-permute-done.11
  29.1 1.6 %collective-permute-start.17 = (f32[64,512]{1,0:T(8,128)S(1)}, f32[64,512]{1,0:T(8,128)S(1)}, u32[]{:S(2)}, u32[]{:S(2)}) collective-permute-start(f32[64,512]{1,0:T(8,128)S(1)} %pad_maximum_fusion.1.refs_4_), channel_id=1, source_target_pairs={{0,4},{1,5},{2,6},{3,7},{4,0},{5,1},{6,2},{7,3},{8,12},{9,13},{10,... | collective-permute-start | bytes 393224 | tf_op jit(solution)/shard_map/ppermute | solution.py:152
  30.6 0.0 collective-permute-start.12
  30.6 0.0 collective-permute-done.13
  30.7 0.6 %collective-permute-start.14 = (f32[32,512]{1,0:T(8,128)S(1)}, f32[32,512]{1,0:T(8,128)S(1)}, u32[]{:S(2)}, u32[]{:S(2)}) collective-permute-start(f32[32,512]{1,0:T(8,128)S(1)} %collective-permute-done.13), channel_id=1, source_target_pairs={{0,2},{1,0},{2,3},{3,1},{4,6},{5,4},{6,7},{7,5},{8,9},{9,11},{10,8... | collective-permute-start | bytes 196616 | tf_op jit(solution)/shard_map/ppermute | solution.py:261
  31.3 0.7 %collective-permute-done.15 = f32[32,512]{1,0:T(8,128)S(1)} collective-permute-done((f32[32,512]{1,0:T(8,128)S(1)}, f32[32,512]{1,0:T(8,128)S(1)}, u32[]{:S(2)}, u32[]{:S(2)}) %collective-permute-start.15) | collective-permute-done | bytes 65568 | tf_op jit(solution)/shard_map/ppermute | solution.py:232
  32.0 0.5 %collective-permute-start.16 = (f32[32,512]{1,0:T(8,128)S(1)}, f32[32,512]{1,0:T(8,128)S(1)}, u32[]{:S(2)}, u32[]{:S(2)}) collective-permute-start(f32[32,512]{1,0:T(8,128)S(1)} %collective-permute-done.15), channel_id=1, source_target_pairs={{0,2},{1,0},{2,3},{3,1},{4,6},{5,4},{6,7},{7,5},{8,9},{9,11},{10,8... | collective-permute-start | bytes 196616 | tf_op jit(solution)/shard_map/ppermute | solution.py:261
  32.5 0.0 collective-permute-done.10
  32.5 1.5 %collective-permute-start.22 = (f32[64,512]{1,0:T(8,128)S(1)}, f32[64,512]{1,0:T(8,128)S(1)}, u32[]{:S(2)}, u32[]{:S(2)}) collective-permute-start(f32[64,512]{1,0:T(8,128)S(1)} %constant_dynamic-update-slice_fusion.refs_5_), channel_id=1, source_target_pairs={{0,4},{1,5},{2,6},{3,7},{4,0},{5,1},{6,2},{7,3},{8,12},{9,13},{10,... | collective-permute-start | bytes 393224 | tf_op jit(solution)/shard_map/ppermute | solution.py:152
  34.0 0.0 collective-permute-done.12
  34.0 0.0 collective-permute-done.14
  34.0 0.4 %collective-permute-done.16 = f32[32,512]{1,0:T(8,128)S(1)} collective-permute-done((f32[32,512]{1,0:T(8,128)S(1)}, f32[32,512]{1,0:T(8,128)S(1)}, u32[]{:S(2)}, u32[]{:S(2)}) %collective-permute-start.16) | collective-permute-done | bytes 65568 | tf_op jit(solution)/shard_map/ppermute | solution.py:261
  34.5 0.0 collective-permute-done.17.refs_0_
  34.5 0.6 %collective-permute-start.18 = (f32[32,512]{1,0:T(8,128)S(1)}, f32[32,512]{1,0:T(8,128)S(1)}, u32[]{:S(2)}, u32[]{:S(2)}) collective-permute-start(f32[32,512]{1,0:T(8,128)S(1)} %get-tuple-element.38), channel_id=1, source_target_pairs={{0,1},{1,0},{2,3},{3,2},{4,5},{5,4},{6,7},{7,6},{8,9},{9,8},{10,11... | collective-permute-start | bytes 196616 | tf_op jit(solution)/shard_map/ppermute | solution.py:152
  35.2 0.1 collective-permute-start.19
  35.2 0.4 %collective-permute-start.20 = (f32[32,512]{1,0:T(8,128)S(1)}, f32[32,512]{1,0:T(8,128)S(1)}, u32[]{:S(2)}, u32[]{:S(2)}) collective-permute-start(f32[32,512]{1,0:T(8,128)S(1)} %get-tuple-element.36), channel_id=1, source_target_pairs={{0,1},{1,0},{2,3},{3,2},{4,5},{5,4},{6,7},{7,6},{8,9},{9,8},{10,11... | collective-permute-start | bytes 196616 | tf_op jit(solution)/shard_map/ppermute | solution.py:152
  35.7 0.1 collective-permute-start.21
  35.7 0.3 collective-permute-done.18.refs_0_
  36.1 0.4 collective-permute-done.19.refs_1_
  36.4 0.2 collective-permute-done.20.refs_2_
  36.6 0.4 collective-permute-done.21.refs_3_
  36.9 0.5 %meat_own.1 = (f32[2,512,256]{2,1,0:T(8,128)S(1)}, bf16[256,512]{1,0:T(8,128)(2,1)S(1)}) custom-call(f32[128,512]{1,0:T(8,128)S(1)} %maximum_select_fusion.have, f32[32,512]{1,0:T(8,128)S(1)} %collective-permute-done.18.refs_0_, f32[32,512]{1,0:T(8,128)S(1)} %collective-permute-done.19.refs_1_, f32[32,512]{1,0:T(8,128)S(1)} %collective-permute-done.20.refs_2_, ...), custom_call_target="tpu_custom_call" | custom-call | tf_op jit(solution)/shard_map/meat_own/pallas_call | solution.py:177
  37.4 0.6 %collective-permute-done.22.refs_1_ = f32[64,512]{1,0:T(8,128)S(1)} collective-permute-done((f32[64,512]{1,0:T(8,128)S(1)}, f32[64,512]{1,0:T(8,128)S(1)}, u32[]{:S(2)}, u32[]{:S(2)}) %collective-permute-start.22) | collective-permute-done | bytes 131104 | tf_op jit(solution)/shard_map/ppermute | solution.py:152
  38.0 1.5 %meat_other.1 = f32[512,1024]{1,0:T(8,128)} custom-call(f32[2,512,256]{2,1,0:T(8,128)S(1)} %get-tuple-element.32.first, bf16[256,512]{1,0:T(8,128)(2,1)S(1)} %get-tuple-element.33.left, f32[64,512]{1,0:T(8,128)S(1)} %collective-permute-done.17.refs_0_, f32[64,512]{1,0:T(8,128)S(1)} %collective-permute-done.22.refs_1_), custom_call_target="tpu_custom_call" | custom-call | flops 201326592 | bytes 2097152 | tf_op jit(solution)/shard_map/meat_other/pallas_call | solution.py:276
  (11 shorter events, 0.2 us)
Async XLA Ops:
  0.0 8.7 %copy-start = (f32[2048]{0:T(1024)S(1)}, f32[2048]{0:T(1024)}, u32[]{:S(2)}) copy-start(f32[2048]{0:T(1024)} %param.9) | copy-start | bytes 24580
  0.0 8.7 %copy-start.1 = (f32[2048]{0:T(1024)S(1)}, f32[2048]{0:T(1024)}, u32[]{:S(2)}) copy-start(f32[2048]{0:T(1024)} %param.10) | copy-start | bytes 24580
  0.0 8.7 %copy-start.2 = (s32[2048]{0:T(1024)S(1)}, s32[2048]{0:T(1024)}, u32[]{:S(2)}) copy-start(s32[2048]{0:T(1024)} %param.11) | copy-start | bytes 24580
  0.0 8.7 %copy-start.3 = (s32[2048]{0:T(1024)S(1)}, s32[2048]{0:T(1024)}, u32[]{:S(2)}) copy-start(s32[2048]{0:T(1024)} %param.12) | copy-start | bytes 24580
  0.0 8.7 %copy-start.4 = (f32[16]{0:T(128)S(1)}, f32[16]{0:T(128)}, u32[]{:S(2)}) copy-start(f32[16]{0:T(128)} %effect.1) | copy-start | bytes 196
  2.6 4.6 %collective-permute-start = (f32[1,2048]{1,0:T(1,128)S(1)}, f32[1,2048]{1,0:T(1,128)S(1)}, u32[]{:S(2)}, u32[]{:S(2)}) collective-permute-start(f32[1,2048]{1,0:T(1,128)S(1)} %get-tuple-element.20.refs_0_), channel_id=1, source_target_pairs={{0,2},{1,3},{2,0},{3,1},{4,6},{5,7},{6,4},{7,5},{8,10},{9,11},{10,... | collective-permute-start | bytes 24584 | tf_op jit(solution)/shard_map/ppermute | solution.py:152
  5.6 3.1 %collective-permute-start.1 = (f32[1,2048]{1,0:T(1,128)S(1)}, f32[1,2048]{1,0:T(1,128)S(1)}, u32[]{:S(2)}, u32[]{:S(2)}) collective-permute-start(f32[1,2048]{1,0:T(1,128)S(1)} %get-tuple-element.20.refs_0_), channel_id=1, source_target_pairs={{0,3},{1,2},{2,1},{3,0},{4,7},{5,6},{6,5},{7,4},{8,11},{9,10},{10,... | collective-permute-start | bytes 24584 | tf_op jit(solution)/shard_map/ppermute | solution.py:152
  5.6 3.1 %collective-permute-start.2 = (f32[1,2048]{1,0:T(1,128)S(1)}, f32[1,2048]{1,0:T(1,128)S(1)}, u32[]{:S(2)}, u32[]{:S(2)}) collective-permute-start(f32[1,2048]{1,0:T(1,128)S(1)} %get-tuple-element.20.refs_0_), channel_id=1, source_target_pairs={{0,1},{1,0},{2,3},{3,2},{4,5},{5,4},{6,7},{7,6},{8,9},{9,8},{10,11... | collective-permute-start | bytes 24584 | tf_op jit(solution)/shard_map/ppermute | solution.py:152
  9.3 5.0 %collective-permute-start.5 = (f32[32,512]{1,0:T(8,128)S(1)}, f32[32,512]{1,0:T(8,128)S(1)}, u32[]{:S(2)}, u32[]{:S(2)}) collective-permute-start(f32[32,512]{1,0:T(8,128)S(1)} %get-tuple-element.26), channel_id=1, source_target_pairs={{0,4},{1,5},{2,6},{3,7},{4,0},{5,1},{6,2},{7,3},{8,12},{9,13},{10,... | collective-permute-start | bytes 196616 | tf_op jit(solution)/shard_map/ppermute | solution.py:152
  10.9 7.1 %collective-permute-start.3 = (f32[32,512]{1,0:T(8,128)S(1)}, f32[32,512]{1,0:T(8,128)S(1)}, u32[]{:S(2)}, u32[]{:S(2)}) collective-permute-start(f32[32,512]{1,0:T(8,128)S(1)} %get-tuple-element.24), channel_id=1, source_target_pairs={{0,4},{1,5},{2,6},{3,7},{4,0},{5,1},{6,2},{7,3},{8,12},{9,13},{10,... | collective-permute-start | bytes 196616 | tf_op jit(solution)/shard_map/ppermute | solution.py:152
  12.3 6.4 %collective-permute-start.7 = (f32[32,512]{1,0:T(8,128)S(1)}, f32[32,512]{1,0:T(8,128)S(1)}, u32[]{:S(2)}, u32[]{:S(2)}) collective-permute-start(f32[32,512]{1,0:T(8,128)S(1)} %get-tuple-element.28), channel_id=1, source_target_pairs={{0,4},{1,5},{2,6},{3,7},{4,0},{5,1},{6,2},{7,3},{8,12},{9,13},{10,... | collective-permute-start | bytes 196616 | tf_op jit(solution)/shard_map/ppermute | solution.py:152
  13.8 9.6 %collective-permute-start.9 = (f32[32,512]{1,0:T(8,128)S(1)}, f32[32,512]{1,0:T(8,128)S(1)}, u32[]{:S(2)}, u32[]{:S(2)}) collective-permute-start(f32[32,512]{1,0:T(8,128)S(1)} %get-tuple-element.30), channel_id=1, source_target_pairs={{0,4},{1,5},{2,6},{3,7},{4,0},{5,1},{6,2},{7,3},{8,12},{9,13},{10,... | collective-permute-start | bytes 196616 | tf_op jit(solution)/shard_map/ppermute | solution.py:152
  14.4 6.2 %collective-permute-start.6 = (f32[32,512]{1,0:T(8,128)S(1)}, f32[32,512]{1,0:T(8,128)S(1)}, u32[]{:S(2)}, u32[]{:S(2)}) collective-permute-start(f32[32,512]{1,0:T(8,128)S(1)} %add.23), channel_id=1, source_target_pairs={{0,24},{1,25},{2,26},{3,27},{4,28},{5,29},{6,30},{7,31},{8,16},{9,... | collective-permute-start | bytes 196616 | tf_op jit(solution)/shard_map/ppermute | solution.py:152
  18.1 5.3 %collective-permute-start.4 = (f32[32,512]{1,0:T(8,128)S(1)}, f32[32,512]{1,0:T(8,128)S(1)}, u32[]{:S(2)}, u32[]{:S(2)}) collective-permute-start(f32[32,512]{1,0:T(8,128)S(1)} %add.22), channel_id=1, source_target_pairs={{0,16},{1,17},{2,18},{3,19},{4,20},{5,21},{6,22},{7,23},{8,24},{9,... | collective-permute-start | bytes 196616 | tf_op jit(solution)/shard_map/ppermute | solution.py:152
  18.7 5.0 %collective-permute-start.8 = (f32[32,512]{1,0:T(8,128)S(1)}, f32[32,512]{1,0:T(8,128)S(1)}, u32[]{:S(2)}, u32[]{:S(2)}) collective-permute-start(f32[32,512]{1,0:T(8,128)S(1)} %add.25), channel_id=1, source_target_pairs={{0,8},{1,9},{2,10},{3,11},{4,12},{5,13},{6,14},{7,15},{8,0},{9,1},... | collective-permute-start | bytes 196616 | tf_op jit(solution)/shard_map/ppermute | solution.py:152
  23.7 5.3 %collective-permute-start.11 = (f32[32,512]{1,0:T(8,128)S(1)}, f32[32,512]{1,0:T(8,128)S(1)}, u32[]{:S(2)}, u32[]{:S(2)}) collective-permute-start(f32[32,512]{1,0:T(8,128)S(1)} %add_add_fusion), channel_id=1, source_target_pairs={{0,16},{1,17},{2,18},{3,19},{4,20},{5,21},{6,22},{7,23},{8,0},{9,1... | collective-permute-start | bytes 196616 | tf_op jit(solution)/shard_map/ppermute | solution.py:232
  25.5 5.2 %collective-permute-start.13 = (f32[32,512]{1,0:T(8,128)S(1)}, f32[32,512]{1,0:T(8,128)S(1)}, u32[]{:S(2)}, u32[]{:S(2)}) collective-permute-start(f32[32,512]{1,0:T(8,128)S(1)} %add_add_fusion), channel_id=1, source_target_pairs={{0,8},{1,9},{2,10},{3,11},{4,12},{5,13},{6,14},{7,15},{8,24},{9,25... | collective-permute-start | bytes 196616 | tf_op jit(solution)/shard_map/ppermute | solution.py:232
  25.8 6.2 %collective-permute-start.15 = (f32[32,512]{1,0:T(8,128)S(1)}, f32[32,512]{1,0:T(8,128)S(1)}, u32[]{:S(2)}, u32[]{:S(2)}) collective-permute-start(f32[32,512]{1,0:T(8,128)S(1)} %add_add_fusion), channel_id=1, source_target_pairs={{0,24},{1,25},{2,26},{3,27},{4,28},{5,29},{6,30},{7,31},{8,16},{9,... | collective-permute-start | bytes 196616 | tf_op jit(solution)/shard_map/ppermute | solution.py:232
  27.9 4.6 %collective-permute-start.10 = (f32[32,512]{1,0:T(8,128)S(1)}, f32[32,512]{1,0:T(8,128)S(1)}, u32[]{:S(2)}, u32[]{:S(2)}) collective-permute-start(f32[32,512]{1,0:T(8,128)S(1)} %add_add_fusion), channel_id=1, source_target_pairs={{0,2},{1,0},{2,3},{3,1},{4,6},{5,4},{6,7},{7,5},{8,9},{9,11},{10,8... | collective-permute-start | bytes 196616 | tf_op jit(solution)/shard_map/ppermute | solution.py:261
  29.1 5.4 %collective-permute-start.17 = (f32[64,512]{1,0:T(8,128)S(1)}, f32[64,512]{1,0:T(8,128)S(1)}, u32[]{:S(2)}, u32[]{:S(2)}) collective-permute-start(f32[64,512]{1,0:T(8,128)S(1)} %pad_maximum_fusion.1.refs_4_), channel_id=1, source_target_pairs={{0,4},{1,5},{2,6},{3,7},{4,0},{5,1},{6,2},{7,3},{8,12},{9,13},{10,... | collective-permute-start | bytes 393224 | tf_op jit(solution)/shard_map/ppermute | solution.py:152
  30.6 3.4 %collective-permute-start.12 = (f32[32,512]{1,0:T(8,128)S(1)}, f32[32,512]{1,0:T(8,128)S(1)}, u32[]{:S(2)}, u32[]{:S(2)}) collective-permute-start(f32[32,512]{1,0:T(8,128)S(1)} %collective-permute-done.11), channel_id=1, source_target_pairs={{0,2},{1,0},{2,3},{3,1},{4,6},{5,4},{6,7},{7,5},{8,9},{9,11},{10,8... | collective-permute-start | bytes 196616 | tf_op jit(solution)/shard_map/ppermute | solution.py:261
  30.7 3.4 %collective-permute-start.14 = (f32[32,512]{1,0:T(8,128)S(1)}, f32[32,512]{1,0:T(8,128)S(1)}, u32[]{:S(2)}, u32[]{:S(2)}) collective-permute-start(f32[32,512]{1,0:T(8,128)S(1)} %collective-permute-done.13), channel_id=1, source_target_pairs={{0,2},{1,0},{2,3},{3,1},{4,6},{5,4},{6,7},{7,5},{8,9},{9,11},{10,8... | collective-permute-start | bytes 196616 | tf_op jit(solution)/shard_map/ppermute | solution.py:261
  32.0 2.4 %collective-permute-start.16 = (f32[32,512]{1,0:T(8,128)S(1)}, f32[32,512]{1,0:T(8,128)S(1)}, u32[]{:S(2)}, u32[]{:S(2)}) collective-permute-start(f32[32,512]{1,0:T(8,128)S(1)} %collective-permute-done.15), channel_id=1, source_target_pairs={{0,2},{1,0},{2,3},{3,1},{4,6},{5,4},{6,7},{7,5},{8,9},{9,11},{10,8... | collective-permute-start | bytes 196616 | tf_op jit(solution)/shard_map/ppermute | solution.py:261
  32.5 5.4 %collective-permute-start.22 = (f32[64,512]{1,0:T(8,128)S(1)}, f32[64,512]{1,0:T(8,128)S(1)}, u32[]{:S(2)}, u32[]{:S(2)}) collective-permute-start(f32[64,512]{1,0:T(8,128)S(1)} %constant_dynamic-update-slice_fusion.refs_5_), channel_id=1, source_target_pairs={{0,4},{1,5},{2,6},{3,7},{4,0},{5,1},{6,2},{7,3},{8,12},{9,13},{10,... | collective-permute-start | bytes 393224 | tf_op jit(solution)/shard_map/ppermute | solution.py:152
  34.5 1.5 %collective-permute-start.18 = (f32[32,512]{1,0:T(8,128)S(1)}, f32[32,512]{1,0:T(8,128)S(1)}, u32[]{:S(2)}, u32[]{:S(2)}) collective-permute-start(f32[32,512]{1,0:T(8,128)S(1)} %get-tuple-element.38), channel_id=1, source_target_pairs={{0,1},{1,0},{2,3},{3,2},{4,5},{5,4},{6,7},{7,6},{8,9},{9,8},{10,11... | collective-permute-start | bytes 196616 | tf_op jit(solution)/shard_map/ppermute | solution.py:152
  35.2 1.3 %collective-permute-start.19 = (f32[32,512]{1,0:T(8,128)S(1)}, f32[32,512]{1,0:T(8,128)S(1)}, u32[]{:S(2)}, u32[]{:S(2)}) collective-permute-start(f32[32,512]{1,0:T(8,128)S(1)} %get-tuple-element.37), channel_id=1, source_target_pairs={{0,1},{1,0},{2,3},{3,2},{4,5},{5,4},{6,7},{7,6},{8,9},{9,8},{10,11... | collective-permute-start | bytes 196616 | tf_op jit(solution)/shard_map/ppermute | solution.py:152
  35.2 1.3 %collective-permute-start.20 = (f32[32,512]{1,0:T(8,128)S(1)}, f32[32,512]{1,0:T(8,128)S(1)}, u32[]{:S(2)}, u32[]{:S(2)}) collective-permute-start(f32[32,512]{1,0:T(8,128)S(1)} %get-tuple-element.36), channel_id=1, source_target_pairs={{0,1},{1,0},{2,3},{3,2},{4,5},{5,4},{6,7},{7,6},{8,9},{9,8},{10,11... | collective-permute-start | bytes 196616 | tf_op jit(solution)/shard_map/ppermute | solution.py:152
  35.7 1.3 %collective-permute-start.21 = (f32[32,512]{1,0:T(8,128)S(1)}, f32[32,512]{1,0:T(8,128)S(1)}, u32[]{:S(2)}, u32[]{:S(2)}) collective-permute-start(f32[32,512]{1,0:T(8,128)S(1)} %get-tuple-element.35), channel_id=1, source_target_pairs={{0,1},{1,0},{2,3},{3,2},{4,5},{5,4},{6,7},{7,6},{8,9},{9,8},{10,11... | collective-permute-start | bytes 196616 | tf_op jit(solution)/shard_map/ppermute | solution.py:152

commit v8 on v7

--- a/solution.py
+++ b/solution.py
@@ -258,11 +258,13 @@
                 pairs.append((c * n_gr + g, c * n_gr + (g ^ flip)))
         if bits > 2:
             pairs = [(c * n_gr + g, c * n_gr + (g ^ bits)) for c in range(n_cal) for g in range(n_gr)]
-        got = jnp.concatenate([lax.ppermute(have[i : i + clusters // 4], AXES, pairs) for i in range(0, clusters, clusters // 4)], axis=0)
+        edges = [clusters * k // 16 for k in [0, 8, 12, 16]]
+        got = jnp.concatenate([lax.ppermute(have[i:j], AXES, pairs) for i, j in zip(edges, edges[1:])], axis=0)
         got, *others[:1] = lax.optimization_barrier((got, *others[:1]))
         have = jnp.where((turn & bits) != 0, got, have)
         bits //= 2
-    got = [swap(have[i : i + clusters // 4], 0, 1) for i in range(0, clusters, clusters // 4)]
+    edges = [clusters * k // 16 for k in [0, 6, 12, 16]]
+    got = [swap(have[i:j], 0, 1) for i, j in zip(edges, edges[1:])]
     scale = 1.0 / (rows * n_cal)
     wide, block = have.shape[1], min(256, half)
     parts = half // block

time: 39.6 us -> 39.5 us (level)
  starting transfers between devices: 24 us -> 23.2 us
  waiting for transfers between devices: 9.19 us -> 9.84 us
    ppermute x16 -> x15, starting transfers between devices: 17.5 us -> 16.8 us  [exchange(): return lax.ppermute(value, AXES, pairs)]
    ppermute x16 -> x15, waiting for transfers between devices: 8.05 us -> 8.52 us  [exchange(): return lax.ppermute(value, AXES, pairs)]
    ppermute x4 -> x3, starting transfers between devices: 2.27 us -> 2.22 us  [per_device(): lax.ppermute(have[i:j], AXES, pairs)]
  transfers between devices with their start and end apart: 23 -> 21, of which waited for: 12 -> 10; matrix products, arithmetic and copies ran while one was open for 0% -> 0% of each run, Pallas kernels for 3% -> 3%
where the time goes in v8:
time: 39.5 us; the launch traced here: 39.4 us
  starting transfers between devices  23.2 us (59%)
  waiting for transfers between devices  9.84 us (25%)
  Pallas kernels  5.96 us (15%)
    ppermute x15, starting transfers between devices, exchange(): return lax.ppermute(value, AXES, pairs)  16.8 us
    ppermute x15, waiting for transfers between devices, exchange(): return lax.ppermute(value, AXES, pairs)  8.52 us
    ppermute x3, starting transfers between devices, along(): return lax.ppermute(value, AXES, pairs)  4.22 us
    pallas_call x1, Pallas kernels, per_device(): pl.pallas_call(linear_kernel, out_shape=(jax.ShapeDtypeStruct((1, rows),...  2.57 us
    ppermute x3, starting transfers between devices, per_device(): lax.ppermute(have[i:j], AXES, pairs)  2.22 us
    pallas_call x3, Pallas kernels, kernel(): return call(*args)  1.92 us
    pallas_call x1, Pallas kernels, per_device(): pl.pallas_call(functools.partial(other_kernel, scale), out_shape=jax.Shap...  1.47 us
    ppermute x3, waiting for transfers between devices, along(): return lax.ppermute(value, AXES, pairs)  0.82 us
  transfers between devices with their start and end apart: 21, of which 10 were waited for; matrix products, arithmetic and copies ran while one was open for 0% of the time, Pallas kernels for 3%

profile of v8, /device:TPU:0, one launch (start us, length us, event | category | flops | bytes accessed | tf_op | source)
XLA Modules:
  0.0 39.4 jit_solution(12003223046078445232)
XLA Ops:
  0.0 0.0 copy-start
  0.0 0.0 copy-start.1
  0.0 0.0 copy-start.2
  0.0 0.0 copy-start.3
  0.0 0.0 copy-start.4
  0.0 2.6 %linear.1 = (f32[1,2048]{1,0:T(1,128)S(1)}, bf16[2048,1024]{1,0:T(8,128)(2,1)S(1)}) custom-call(bf16[2048,1024]{1,0:T(8,128)(2,1)} %feats.1, bf16[1024]{0:T(1024)(128)(2,1)} %coef.1), custom_call_target="tpu_custom_call" | custom-call | flops 4194304 | bytes 4194304 | tf_op jit(solution)/shard_map/linear/pallas_call | solution.py:181
  2.6 3.0 %collective-permute-start = (f32[1,2048]{1,0:T(1,128)S(1)}, f32[1,2048]{1,0:T(1,128)S(1)}, u32[]{:S(2)}, u32[]{:S(2)}) collective-permute-start(f32[1,2048]{1,0:T(1,128)S(1)} %get-tuple-element.20.refs_0_), channel_id=1, source_target_pairs={{0,2},{1,3},{2,0},{3,1},{4,6},{5,7},{6,4},{7,5},{8,10},{9,11},{10,... | collective-permute-start | bytes 24584 | tf_op jit(solution)/shard_map/ppermute | solution.py:152
  5.6 0.0 collective-permute-start.1
  5.6 0.2 collective-permute-start.2
  5.8 1.4 %collective-permute-done.refs_1_ = f32[1,2048]{1,0:T(1,128)S(1)} collective-permute-done((f32[1,2048]{1,0:T(1,128)S(1)}, f32[1,2048]{1,0:T(1,128)S(1)}, u32[]{:S(2)}, u32[]{:S(2)}) %collective-permute-start) | collective-permute-done | bytes 8224 | tf_op jit(solution)/shard_map/ppermute | solution.py:152
  7.2 1.4 %collective-permute-done.1.refs_2_ = f32[1,2048]{1,0:T(1,128)S(1)} collective-permute-done((f32[1,2048]{1,0:T(1,128)S(1)}, f32[1,2048]{1,0:T(1,128)S(1)}, u32[]{:S(2)}, u32[]{:S(2)}) %collective-permute-start.1) | collective-permute-done | bytes 8224 | tf_op jit(solution)/shard_map/ppermute | solution.py:152
  8.7 0.0 collective-permute-done.2.refs_3_
  8.7 0.0 copy-done
  8.7 0.0 copy-done.1
  8.7 0.0 copy-done.2
  8.7 0.0 copy-done.3
  8.7 0.0 copy-done.4
  8.7 0.6 %send_far.1 = (f32[32,512]{1,0:T(8,128)S(1)}, f32[32,512]{1,0:T(8,128)S(1)}, bf16[128,2048]{1,0:T(8,128)(2,1)S(1)}) custom-call(f32[16]{0:T(128)S(1)} %copy-done.4, f32[1,2048]{1,0:T(1,128)S(1)} %get-tuple-element.20.refs_0_, f32[1,2048]{1,0:T(1,128)S(1)} %collective-permute-done.refs_1_, f32[1,2048]{1,0:T(1,128)S(1)} %collective-permute-done.1.refs_2_, ...), custom_call_target="tpu_custom_call" | custom-call | flops 134217728 | bytes 524288 | tf_op jit(solution)/shard_map/send_far/pallas_call | solution.py:177
  9.3 1.6 %collective-permute-start.5 = (f32[32,512]{1,0:T(8,128)S(1)}, f32[32,512]{1,0:T(8,128)S(1)}, u32[]{:S(2)}, u32[]{:S(2)}) collective-permute-start(f32[32,512]{1,0:T(8,128)S(1)} %get-tuple-element.26), channel_id=1, source_target_pairs={{0,4},{1,5},{2,6},{3,7},{4,0},{5,1},{6,2},{7,3},{8,12},{9,13},{10,... | collective-permute-start | bytes 196616 | tf_op jit(solution)/shard_map/ppermute | solution.py:152
  10.9 0.5 %collective-permute-start.3 = (f32[32,512]{1,0:T(8,128)S(1)}, f32[32,512]{1,0:T(8,128)S(1)}, u32[]{:S(2)}, u32[]{:S(2)}) collective-permute-start(f32[32,512]{1,0:T(8,128)S(1)} %get-tuple-element.24), channel_id=1, source_target_pairs={{0,4},{1,5},{2,6},{3,7},{4,0},{5,1},{6,2},{7,3},{8,12},{9,13},{10,... | collective-permute-start | bytes 196616 | tf_op jit(solution)/shard_map/ppermute | solution.py:152
  11.4 0.8 %rest.1 = (f32[32,512]{1,0:T(8,128)S(1)}, f32[32,512]{1,0:T(8,128)S(1)}, f32[32,512]{1,0:T(8,128)S(1)}, f32[32,512]{1,0:T(8,128)S(1)}, f32[32,512]{1,0:T(8,128)S(1)}, /*index=5*/f32[32,512]{1,0:T(8,128)S(1)}) custom-call(bf16[128,2048]{1,0:T(8,128)(2,1)S(1)} %get-tuple-element.22.picks, bf16[2048,1024]{1,0:T(8,128)(2,1)S(1)} %get-tuple-element.21.refs_8_.held), custom_call_target="tpu_custom_call" | custom-call | flops 402653184 | bytes 1572864 | tf_op jit(solution)/shard_map/rest/pallas_call | solution.py:177
  12.3 1.6 %collective-permute-start.7 = (f32[32,512]{1,0:T(8,128)S(1)}, f32[32,512]{1,0:T(8,128)S(1)}, u32[]{:S(2)}, u32[]{:S(2)}) collective-permute-start(f32[32,512]{1,0:T(8,128)S(1)} %get-tuple-element.28), channel_id=1, source_target_pairs={{0,4},{1,5},{2,6},{3,7},{4,0},{5,1},{6,2},{7,3},{8,12},{9,13},{10,... | collective-permute-start | bytes 196616 | tf_op jit(solution)/shard_map/ppermute | solution.py:152
  13.8 0.5 %collective-permute-start.9 = (f32[32,512]{1,0:T(8,128)S(1)}, f32[32,512]{1,0:T(8,128)S(1)}, u32[]{:S(2)}, u32[]{:S(2)}) collective-permute-start(f32[32,512]{1,0:T(8,128)S(1)} %get-tuple-element.30), channel_id=1, source_target_pairs={{0,4},{1,5},{2,6},{3,7},{4,0},{5,1},{6,2},{7,3},{8,12},{9,13},{10,... | collective-permute-start | bytes 196616 | tf_op jit(solution)/shard_map/ppermute | solution.py:152
  14.3 0.0 collective-permute-done.5
  14.4 3.7 %collective-permute-start.6 = (f32[32,512]{1,0:T(8,128)S(1)}, f32[32,512]{1,0:T(8,128)S(1)}, u32[]{:S(2)}, u32[]{:S(2)}) collective-permute-start(f32[32,512]{1,0:T(8,128)S(1)} %add.23), channel_id=1, source_target_pairs={{0,24},{1,25},{2,26},{3,27},{4,28},{5,29},{6,30},{7,31},{8,16},{9,... | collective-permute-start | bytes 196616 | tf_op jit(solution)/shard_map/ppermute | solution.py:152
  18.0 0.0 collective-permute-done.3
  18.1 0.6 %collective-permute-start.4 = (f32[32,512]{1,0:T(8,128)S(1)}, f32[32,512]{1,0:T(8,128)S(1)}, u32[]{:S(2)}, u32[]{:S(2)}) collective-permute-start(f32[32,512]{1,0:T(8,128)S(1)} %add.22), channel_id=1, source_target_pairs={{0,16},{1,17},{2,18},{3,19},{4,20},{5,21},{6,22},{7,23},{8,24},{9,... | collective-permute-start | bytes 196616 | tf_op jit(solution)/shard_map/ppermute | solution.py:152
  18.7 0.0 collective-permute-done.7
  18.7 1.6 %collective-permute-start.8 = (f32[32,512]{1,0:T(8,128)S(1)}, f32[32,512]{1,0:T(8,128)S(1)}, u32[]{:S(2)}, u32[]{:S(2)}) collective-permute-start(f32[32,512]{1,0:T(8,128)S(1)} %add.25), channel_id=1, source_target_pairs={{0,8},{1,9},{2,10},{3,11},{4,12},{5,13},{6,14},{7,15},{8,0},{9,1},... | collective-permute-start | bytes 196616 | tf_op jit(solution)/shard_map/ppermute | solution.py:152
  20.3 0.3 collective-permute-done.6
  20.6 2.8 %collective-permute-done.4 = f32[32,512]{1,0:T(8,128)S(1)} collective-permute-done((f32[32,512]{1,0:T(8,128)S(1)}, f32[32,512]{1,0:T(8,128)S(1)}, u32[]{:S(2)}, u32[]{:S(2)}) %collective-permute-start.4) | collective-permute-done | bytes 65568 | tf_op jit(solution)/shard_map/ppermute | solution.py:152
  23.4 0.0 collective-permute-done.9
  23.4 0.3 collective-permute-done.8
  23.7 1.7 %collective-permute-start.10 = (f32[32,512]{1,0:T(8,128)S(1)}, f32[32,512]{1,0:T(8,128)S(1)}, u32[]{:S(2)}, u32[]{:S(2)}) collective-permute-start(f32[32,512]{1,0:T(8,128)S(1)} %add_add_fusion), channel_id=1, source_target_pairs={{0,16},{1,17},{2,18},{3,19},{4,20},{5,21},{6,22},{7,23},{8,0},{9,1... | collective-permute-start | bytes 196616 | tf_op jit(solution)/shard_map/ppermute | solution.py:232
  25.5 0.3 collective-permute-start.12
  25.8 2.1 %collective-permute-start.14 = (f32[32,512]{1,0:T(8,128)S(1)}, f32[32,512]{1,0:T(8,128)S(1)}, u32[]{:S(2)}, u32[]{:S(2)}) collective-permute-start(f32[32,512]{1,0:T(8,128)S(1)} %add_add_fusion), channel_id=1, source_target_pairs={{0,24},{1,25},{2,26},{3,27},{4,28},{5,29},{6,30},{7,31},{8,16},{9,... | collective-permute-start | bytes 196616 | tf_op jit(solution)/shard_map/ppermute | solution.py:232
  27.9 0.1 collective-permute-done.10
  28.1 1.1 %collective-permute-start.11 = (f32[64,512]{1,0:T(8,128)S(1)}, f32[64,512]{1,0:T(8,128)S(1)}, u32[]{:S(2)}, u32[]{:S(2)}) collective-permute-start(f32[64,512]{1,0:T(8,128)S(1)} %pad_maximum_fusion.1.refs_3_), channel_id=1, source_target_pairs={{0,2},{1,0},{2,3},{3,1},{4,6},{5,4},{6,7},{7,5},{8,9},{9,11},{10,8... | collective-permute-start | bytes 393224 | tf_op jit(solution)/shard_map/ppermute | solution.py:262
  29.1 1.5 %collective-permute-start.16 = (f32[64,512]{1,0:T(8,128)S(1)}, f32[64,512]{1,0:T(8,128)S(1)}, u32[]{:S(2)}, u32[]{:S(2)}) collective-permute-start(f32[64,512]{1,0:T(8,128)S(1)} %pad_maximum_fusion.1.refs_3_), channel_id=1, source_target_pairs={{0,4},{1,5},{2,6},{3,7},{4,0},{5,1},{6,2},{7,3},{8,12},{9,13},{10,... | collective-permute-start | bytes 393224 | tf_op jit(solution)/shard_map/ppermute | solution.py:152
  30.6 0.0 collective-permute-done.12
  30.7 0.6 %collective-permute-start.13 = (f32[32,512]{1,0:T(8,128)S(1)}, f32[32,512]{1,0:T(8,128)S(1)}, u32[]{:S(2)}, u32[]{:S(2)}) collective-permute-start(f32[32,512]{1,0:T(8,128)S(1)} %collective-permute-done.12), channel_id=1, source_target_pairs={{0,2},{1,0},{2,3},{3,1},{4,6},{5,4},{6,7},{7,5},{8,9},{9,11},{10,8... | collective-permute-start | bytes 196616 | tf_op jit(solution)/shard_map/ppermute | solution.py:262
  31.3 0.7 %collective-permute-done.14 = f32[32,512]{1,0:T(8,128)S(1)} collective-permute-done((f32[32,512]{1,0:T(8,128)S(1)}, f32[32,512]{1,0:T(8,128)S(1)}, u32[]{:S(2)}, u32[]{:S(2)}) %collective-permute-start.14) | collective-permute-done | bytes 65568 | tf_op jit(solution)/shard_map/ppermute | solution.py:232
  32.0 0.5 %collective-permute-start.15 = (f32[32,512]{1,0:T(8,128)S(1)}, f32[32,512]{1,0:T(8,128)S(1)}, u32[]{:S(2)}, u32[]{:S(2)}) collective-permute-start(f32[32,512]{1,0:T(8,128)S(1)} %collective-permute-done.14), channel_id=1, source_target_pairs={{0,2},{1,0},{2,3},{3,1},{4,6},{5,4},{6,7},{7,5},{8,9},{9,11},{10,8... | collective-permute-start | bytes 196616 | tf_op jit(solution)/shard_map/ppermute | solution.py:262
  32.5 1.4 %collective-permute-start.20 = (f32[64,512]{1,0:T(8,128)S(1)}, f32[64,512]{1,0:T(8,128)S(1)}, u32[]{:S(2)}, u32[]{:S(2)}) collective-permute-start(f32[64,512]{1,0:T(8,128)S(1)} %constant_dynamic-update-slice_fusion.refs_4_), channel_id=1, source_target_pairs={{0,4},{1,5},{2,6},{3,7},{4,0},{5,1},{6,2},{7,3},{8,12},{9,13},{10,... | collective-permute-start | bytes 393224 | tf_op jit(solution)/shard_map/ppermute | solution.py:152
  33.9 0.0 collective-permute-done.13
  33.9 0.5 %collective-permute-done.15 = f32[32,512]{1,0:T(8,128)S(1)} collective-permute-done((f32[32,512]{1,0:T(8,128)S(1)}, f32[32,512]{1,0:T(8,128)S(1)}, u32[]{:S(2)}, u32[]{:S(2)}) %collective-permute-start.15) | collective-permute-done | bytes 65568 | tf_op jit(solution)/shard_map/ppermute | solution.py:262
  34.4 0.0 collective-permute-done.11
  34.5 0.0 collective-permute-done.16.refs_0_
  34.5 0.1 collective-permute-start.17
  34.6 0.5 %collective-permute-start.18 = (f32[48,512]{1,0:T(8,128)S(1)}, f32[48,512]{1,0:T(8,128)S(1)}, u32[]{:S(2)}, u32[]{:S(2)}) collective-permute-start(f32[48,512]{1,0:T(8,128)S(1)} %get-tuple-element.35), channel_id=1, source_target_pairs={{0,1},{1,0},{2,3},{3,2},{4,5},{5,4},{6,7},{7,6},{8,9},{9,8},{10,11... | collective-permute-start | bytes 294920 | tf_op jit(solution)/shard_map/ppermute | solution.py:152
  35.1 0.1 collective-permute-start.19
  35.2 1.2 %collective-permute-done.19.refs_2_ = f32[32,512]{1,0:T(8,128)S(1)} collective-permute-done((f32[32,512]{1,0:T(8,128)S(1)}, f32[32,512]{1,0:T(8,128)S(1)}, u32[]{:S(2)}, u32[]{:S(2)}) %collective-permute-start.19) | collective-permute-done | bytes 65568 | tf_op jit(solution)/shard_map/ppermute | solution.py:152
  36.4 0.0 collective-permute-done.17.refs_0_
  36.4 0.0 collective-permute-done.18.refs_1_
  36.4 0.5 %meat_own.1 = (f32[2,512,256]{2,1,0:T(8,128)S(1)}, bf16[256,512]{1,0:T(8,128)(2,1)S(1)}) custom-call(f32[128,512]{1,0:T(8,128)S(1)} %maximum_select_fusion.have, f32[48,512]{1,0:T(8,128)S(1)} %collective-permute-done.17.refs_0_, f32[48,512]{1,0:T(8,128)S(1)} %collective-permute-done.18.refs_1_, f32[32,512]{1,0:T(8,128)S(1)} %collective-permute-done.19.refs_2_, ...), custom_call_target="tpu_custom_call" | custom-call | tf_op jit(solution)/shard_map/meat_own/pallas_call | solution.py:177
  36.9 1.0 %collective-permute-done.20.refs_1_ = f32[64,512]{1,0:T(8,128)S(1)} collective-permute-done((f32[64,512]{1,0:T(8,128)S(1)}, f32[64,512]{1,0:T(8,128)S(1)}, u32[]{:S(2)}, u32[]{:S(2)}) %collective-permute-start.20) | collective-permute-done | bytes 131104 | tf_op jit(solution)/shard_map/ppermute | solution.py:152
  37.9 1.5 %meat_other.1 = f32[512,1024]{1,0:T(8,128)} custom-call(f32[2,512,256]{2,1,0:T(8,128)S(1)} %get-tuple-element.32.first, bf16[256,512]{1,0:T(8,128)(2,1)S(1)} %get-tuple-element.33.left, f32[64,512]{1,0:T(8,128)S(1)} %collective-permute-done.16.refs_0_, f32[64,512]{1,0:T(8,128)S(1)} %collective-permute-done.20.refs_1_), custom_call_target="tpu_custom_call" | custom-call | flops 201326592 | bytes 2097152 | tf_op jit(solution)/shard_map/meat_other/pallas_call | solution.py:278
  (12 shorter events, 0.2 us)
Async XLA Ops:
  0.0 8.7 %copy-start = (f32[2048]{0:T(1024)S(1)}, f32[2048]{0:T(1024)}, u32[]{:S(2)}) copy-start(f32[2048]{0:T(1024)} %param.9) | copy-start | bytes 24580
  0.0 8.7 %copy-start.1 = (f32[2048]{0:T(1024)S(1)}, f32[2048]{0:T(1024)}, u32[]{:S(2)}) copy-start(f32[2048]{0:T(1024)} %param.10) | copy-start | bytes 24580
  0.0 8.7 %copy-start.2 = (s32[2048]{0:T(1024)S(1)}, s32[2048]{0:T(1024)}, u32[]{:S(2)}) copy-start(s32[2048]{0:T(1024)} %param.11) | copy-start | bytes 24580
  0.0 8.7 %copy-start.3 = (s32[2048]{0:T(1024)S(1)}, s32[2048]{0:T(1024)}, u32[]{:S(2)}) copy-start(s32[2048]{0:T(1024)} %param.12) | copy-start | bytes 24580
  0.0 8.7 %copy-start.4 = (f32[16]{0:T(128)S(1)}, f32[16]{0:T(128)}, u32[]{:S(2)}) copy-start(f32[16]{0:T(128)} %effect.1) | copy-start | bytes 196
  2.6 4.6 %collective-permute-start = (f32[1,2048]{1,0:T(1,128)S(1)}, f32[1,2048]{1,0:T(1,128)S(1)}, u32[]{:S(2)}, u32[]{:S(2)}) collective-permute-start(f32[1,2048]{1,0:T(1,128)S(1)} %get-tuple-element.20.refs_0_), channel_id=1, source_target_pairs={{0,2},{1,3},{2,0},{3,1},{4,6},{5,7},{6,4},{7,5},{8,10},{9,11},{10,... | collective-permute-start | bytes 24584 | tf_op jit(solution)/shard_map/ppermute | solution.py:152
  5.6 3.1 %collective-permute-start.1 = (f32[1,2048]{1,0:T(1,128)S(1)}, f32[1,2048]{1,0:T(1,128)S(1)}, u32[]{:S(2)}, u32[]{:S(2)}) collective-permute-start(f32[1,2048]{1,0:T(1,128)S(1)} %get-tuple-element.20.refs_0_), channel_id=1, source_target_pairs={{0,3},{1,2},{2,1},{3,0},{4,7},{5,6},{6,5},{7,4},{8,11},{9,10},{10,... | collective-permute-start | bytes 24584 | tf_op jit(solution)/shard_map/ppermute | solution.py:152
  5.6 3.1 %collective-permute-start.2 = (f32[1,2048]{1,0:T(1,128)S(1)}, f32[1,2048]{1,0:T(1,128)S(1)}, u32[]{:S(2)}, u32[]{:S(2)}) collective-permute-start(f32[1,2048]{1,0:T(1,128)S(1)} %get-tuple-element.20.refs_0_), channel_id=1, source_target_pairs={{0,1},{1,0},{2,3},{3,2},{4,5},{5,4},{6,7},{7,6},{8,9},{9,8},{10,11... | collective-permute-start | bytes 24584 | tf_op jit(solution)/shard_map/ppermute | solution.py:152
  9.3 5.0 %collective-permute-start.5 = (f32[32,512]{1,0:T(8,128)S(1)}, f32[32,512]{1,0:T(8,128)S(1)}, u32[]{:S(2)}, u32[]{:S(2)}) collective-permute-start(f32[32,512]{1,0:T(8,128)S(1)} %get-tuple-element.26), channel_id=1, source_target_pairs={{0,4},{1,5},{2,6},{3,7},{4,0},{5,1},{6,2},{7,3},{8,12},{9,13},{10,... | collective-permute-start | bytes 196616 | tf_op jit(solution)/shard_map/ppermute | solution.py:152
  10.9 7.1 %collective-permute-start.3 = (f32[32,512]{1,0:T(8,128)S(1)}, f32[32,512]{1,0:T(8,128)S(1)}, u32[]{:S(2)}, u32[]{:S(2)}) collective-permute-start(f32[32,512]{1,0:T(8,128)S(1)} %get-tuple-element.24), channel_id=1, source_target_pairs={{0,4},{1,5},{2,6},{3,7},{4,0},{5,1},{6,2},{7,3},{8,12},{9,13},{10,... | collective-permute-start | bytes 196616 | tf_op jit(solution)/shard_map/ppermute | solution.py:152
  12.3 6.4 %collective-permute-start.7 = (f32[32,512]{1,0:T(8,128)S(1)}, f32[32,512]{1,0:T(8,128)S(1)}, u32[]{:S(2)}, u32[]{:S(2)}) collective-permute-start(f32[32,512]{1,0:T(8,128)S(1)} %get-tuple-element.28), channel_id=1, source_target_pairs={{0,4},{1,5},{2,6},{3,7},{4,0},{5,1},{6,2},{7,3},{8,12},{9,13},{10,... | collective-permute-start | bytes 196616 | tf_op jit(solution)/shard_map/ppermute | solution.py:152
  13.8 9.6 %collective-permute-start.9 = (f32[32,512]{1,0:T(8,128)S(1)}, f32[32,512]{1,0:T(8,128)S(1)}, u32[]{:S(2)}, u32[]{:S(2)}) collective-permute-start(f32[32,512]{1,0:T(8,128)S(1)} %get-tuple-element.30), channel_id=1, source_target_pairs={{0,4},{1,5},{2,6},{3,7},{4,0},{5,1},{6,2},{7,3},{8,12},{9,13},{10,... | collective-permute-start | bytes 196616 | tf_op jit(solution)/shard_map/ppermute | solution.py:152
  14.4 6.2 %collective-permute-start.6 = (f32[32,512]{1,0:T(8,128)S(1)}, f32[32,512]{1,0:T(8,128)S(1)}, u32[]{:S(2)}, u32[]{:S(2)}) collective-permute-start(f32[32,512]{1,0:T(8,128)S(1)} %add.23), channel_id=1, source_target_pairs={{0,24},{1,25},{2,26},{3,27},{4,28},{5,29},{6,30},{7,31},{8,16},{9,... | collective-permute-start | bytes 196616 | tf_op jit(solution)/shard_map/ppermute | solution.py:152
  18.1 5.3 %collective-permute-start.4 = (f32[32,512]{1,0:T(8,128)S(1)}, f32[32,512]{1,0:T(8,128)S(1)}, u32[]{:S(2)}, u32[]{:S(2)}) collective-permute-start(f32[32,512]{1,0:T(8,128)S(1)} %add.22), channel_id=1, source_target_pairs={{0,16},{1,17},{2,18},{3,19},{4,20},{5,21},{6,22},{7,23},{8,24},{9,... | collective-permute-start | bytes 196616 | tf_op jit(solution)/shard_map/ppermute | solution.py:152
  18.7 5.0 %collective-permute-start.8 = (f32[32,512]{1,0:T(8,128)S(1)}, f32[32,512]{1,0:T(8,128)S(1)}, u32[]{:S(2)}, u32[]{:S(2)}) collective-permute-start(f32[32,512]{1,0:T(8,128)S(1)} %add.25), channel_id=1, source_target_pairs={{0,8},{1,9},{2,10},{3,11},{4,12},{5,13},{6,14},{7,15},{8,0},{9,1},... | collective-permute-start | bytes 196616 | tf_op jit(solution)/shard_map/ppermute | solution.py:152
  23.7 4.3 %collective-permute-start.10 = (f32[32,512]{1,0:T(8,128)S(1)}, f32[32,512]{1,0:T(8,128)S(1)}, u32[]{:S(2)}, u32[]{:S(2)}) collective-permute-start(f32[32,512]{1,0:T(8,128)S(1)} %add_add_fusion), channel_id=1, source_target_pairs={{0,16},{1,17},{2,18},{3,19},{4,20},{5,21},{6,22},{7,23},{8,0},{9,1... | collective-permute-start | bytes 196616 | tf_op jit(solution)/shard_map/ppermute | solution.py:232
  25.5 5.2 %collective-permute-start.12 = (f32[32,512]{1,0:T(8,128)S(1)}, f32[32,512]{1,0:T(8,128)S(1)}, u32[]{:S(2)}, u32[]{:S(2)}) collective-permute-start(f32[32,512]{1,0:T(8,128)S(1)} %add_add_fusion), channel_id=1, source_target_pairs={{0,8},{1,9},{2,10},{3,11},{4,12},{5,13},{6,14},{7,15},{8,24},{9,25... | collective-permute-start | bytes 196616 | tf_op jit(solution)/shard_map/ppermute | solution.py:232
  25.8 6.2 %collective-permute-start.14 = (f32[32,512]{1,0:T(8,128)S(1)}, f32[32,512]{1,0:T(8,128)S(1)}, u32[]{:S(2)}, u32[]{:S(2)}) collective-permute-start(f32[32,512]{1,0:T(8,128)S(1)} %add_add_fusion), channel_id=1, source_target_pairs={{0,24},{1,25},{2,26},{3,27},{4,28},{5,29},{6,30},{7,31},{8,16},{9,... | collective-permute-start | bytes 196616 | tf_op jit(solution)/shard_map/ppermute | solution.py:232
  28.1 6.4 %collective-permute-start.11 = (f32[64,512]{1,0:T(8,128)S(1)}, f32[64,512]{1,0:T(8,128)S(1)}, u32[]{:S(2)}, u32[]{:S(2)}) collective-permute-start(f32[64,512]{1,0:T(8,128)S(1)} %pad_maximum_fusion.1.refs_3_), channel_id=1, source_target_pairs={{0,2},{1,0},{2,3},{3,1},{4,6},{5,4},{6,7},{7,5},{8,9},{9,11},{10,8... | collective-permute-start | bytes 393224 | tf_op jit(solution)/shard_map/ppermute | solution.py:262
  29.1 5.3 %collective-permute-start.16 = (f32[64,512]{1,0:T(8,128)S(1)}, f32[64,512]{1,0:T(8,128)S(1)}, u32[]{:S(2)}, u32[]{:S(2)}) collective-permute-start(f32[64,512]{1,0:T(8,128)S(1)} %pad_maximum_fusion.1.refs_3_), channel_id=1, source_target_pairs={{0,4},{1,5},{2,6},{3,7},{4,0},{5,1},{6,2},{7,3},{8,12},{9,13},{10,... | collective-permute-start | bytes 393224 | tf_op jit(solution)/shard_map/ppermute | solution.py:152
  30.7 3.3 %collective-permute-start.13 = (f32[32,512]{1,0:T(8,128)S(1)}, f32[32,512]{1,0:T(8,128)S(1)}, u32[]{:S(2)}, u32[]{:S(2)}) collective-permute-start(f32[32,512]{1,0:T(8,128)S(1)} %collective-permute-done.12), channel_id=1, source_target_pairs={{0,2},{1,0},{2,3},{3,1},{4,6},{5,4},{6,7},{7,5},{8,9},{9,11},{10,8... | collective-permute-start | bytes 196616 | tf_op jit(solution)/shard_map/ppermute | solution.py:262
  32.0 2.4 %collective-permute-start.15 = (f32[32,512]{1,0:T(8,128)S(1)}, f32[32,512]{1,0:T(8,128)S(1)}, u32[]{:S(2)}, u32[]{:S(2)}) collective-permute-start(f32[32,512]{1,0:T(8,128)S(1)} %collective-permute-done.14), channel_id=1, source_target_pairs={{0,2},{1,0},{2,3},{3,1},{4,6},{5,4},{6,7},{7,5},{8,9},{9,11},{10,8... | collective-permute-start | bytes 196616 | tf_op jit(solution)/shard_map/ppermute | solution.py:262
  32.5 5.4 %collective-permute-start.20 = (f32[64,512]{1,0:T(8,128)S(1)}, f32[64,512]{1,0:T(8,128)S(1)}, u32[]{:S(2)}, u32[]{:S(2)}) collective-permute-start(f32[64,512]{1,0:T(8,128)S(1)} %constant_dynamic-update-slice_fusion.refs_4_), channel_id=1, source_target_pairs={{0,4},{1,5},{2,6},{3,7},{4,0},{5,1},{6,2},{7,3},{8,12},{9,13},{10,... | collective-permute-start | bytes 393224 | tf_op jit(solution)/shard_map/ppermute | solution.py:152
  34.5 1.8 %collective-permute-start.17 = (f32[48,512]{1,0:T(8,128)S(1)}, f32[48,512]{1,0:T(8,128)S(1)}, u32[]{:S(2)}, u32[]{:S(2)}) collective-permute-start(f32[48,512]{1,0:T(8,128)S(1)} %get-tuple-element.36), channel_id=1, source_target_pairs={{0,1},{1,0},{2,3},{3,2},{4,5},{5,4},{6,7},{7,6},{8,9},{9,8},{10,11... | collective-permute-start | bytes 294920 | tf_op jit(solution)/shard_map/ppermute | solution.py:152
  34.6 1.8 %collective-permute-start.18 = (f32[48,512]{1,0:T(8,128)S(1)}, f32[48,512]{1,0:T(8,128)S(1)}, u32[]{:S(2)}, u32[]{:S(2)}) collective-permute-start(f32[48,512]{1,0:T(8,128)S(1)} %get-tuple-element.35), channel_id=1, source_target_pairs={{0,1},{1,0},{2,3},{3,2},{4,5},{5,4},{6,7},{7,6},{8,9},{9,8},{10,11... | collective-permute-start | bytes 294920 | tf_op jit(solution)/shard_map/ppermute | solution.py:152
  35.1 1.3 %collective-permute-start.19 = (f32[32,512]{1,0:T(8,128)S(1)}, f32[32,512]{1,0:T(8,128)S(1)}, u32[]{:S(2)}, u32[]{:S(2)}) collective-permute-start(f32[32,512]{1,0:T(8,128)S(1)} %slice.16), channel_id=1, source_target_pairs={{0,1},{1,0},{2,3},{3,2},{4,5},{5,4},{6,7},{7,6},{8,9},{9,8},{10,11... | collective-permute-start | bytes 196616 | tf_op jit(solution)/shard_map/ppermute | solution.py:152

commit v9 on v8

--- a/solution.py
+++ b/solution.py
@@ -99,7 +99,7 @@
     left_high = left[: left.shape[0] // 2]
     dims = (((0,), (0,)), ((), ()))
     half = high.shape[1]
-    block = min(256, half)
+    block = min(512, half)
     for n in range(half // block):
         part = slice(n * block, (n + 1) * block)
         total = lax.dot_general(
@@ -266,7 +266,7 @@
     edges = [clusters * k // 16 for k in [0, 6, 12, 16]]
     got = [swap(have[i:j], 0, 1) for i, j in zip(edges, edges[1:])]
     scale = 1.0 / (rows * n_cal)
-    wide, block = have.shape[1], min(256, half)
+    wide, block = have.shape[1], min(512, half)
     parts = half // block
     work = 6 * clusters * half * wide
     first, left = kernel(

time: 39.5 us -> 39.5 us (level)
  no operation moved by 1% of the time
where the time goes in v9:
time: 39.5 us; the launch traced here: 39.4 us
  starting transfers between devices  23.2 us (59%)
  waiting for transfers between devices  9.84 us (25%)
  Pallas kernels  5.95 us (15%)
    ppermute x15, starting transfers between devices, exchange(): return lax.ppermute(value, AXES, pairs)  16.8 us
    ppermute x15, waiting for transfers between devices, exchange(): return lax.ppermute(value, AXES, pairs)  8.52 us
    ppermute x3, starting transfers between devices, along(): return lax.ppermute(value, AXES, pairs)  4.22 us
    pallas_call x1, Pallas kernels, per_device(): pl.pallas_call(linear_kernel, out_shape=(jax.ShapeDtypeStruct((1, rows),...  2.57 us
    ppermute x3, starting transfers between devices, per_device(): lax.ppermute(have[i:j], AXES, pairs)  2.22 us
    pallas_call x3, Pallas kernels, kernel(): return call(*args)  1.92 us
    pallas_call x1, Pallas kernels, per_device(): pl.pallas_call(functools.partial(other_kernel, scale), out_shape=jax.Shap...  1.45 us
    ppermute x3, waiting for transfers between devices, along(): return lax.ppermute(value, AXES, pairs)  0.82 us
  transfers between devices with their start and end apart: 21, of which 10 were waited for; matrix products, arithmetic and copies ran while one was open for 0% of the time, Pallas kernels for 3%

profile of v9, /device:TPU:0, one launch (start us, length us, event | category | flops | bytes accessed | tf_op | source)
XLA Modules:
  0.0 39.4 jit_solution(17576664521619266878)
XLA Ops:
  0.0 0.0 copy-start
  0.0 0.0 copy-start.1
  0.0 0.0 copy-start.2
  0.0 0.0 copy-start.3
  0.0 0.0 copy-start.4
  0.0 2.6 %linear.1 = (f32[1,2048]{1,0:T(1,128)S(1)}, bf16[2048,1024]{1,0:T(8,128)(2,1)S(1)}) custom-call(bf16[2048,1024]{1,0:T(8,128)(2,1)} %feats.1, bf16[1024]{0:T(1024)(128)(2,1)} %coef.1), custom_call_target="tpu_custom_call" | custom-call | flops 4194304 | bytes 4194304 | tf_op jit(solution)/shard_map/linear/pallas_call | solution.py:181
  2.6 3.0 %collective-permute-start = (f32[1,2048]{1,0:T(1,128)S(1)}, f32[1,2048]{1,0:T(1,128)S(1)}, u32[]{:S(2)}, u32[]{:S(2)}) collective-permute-start(f32[1,2048]{1,0:T(1,128)S(1)} %get-tuple-element.20.refs_0_), channel_id=1, source_target_pairs={{0,2},{1,3},{2,0},{3,1},{4,6},{5,7},{6,4},{7,5},{8,10},{9,11},{10,... | collective-permute-start | bytes 24584 | tf_op jit(solution)/shard_map/ppermute | solution.py:152
  5.6 0.0 collective-permute-start.1
  5.6 0.2 collective-permute-start.2
  5.8 1.4 %collective-permute-done.refs_1_ = f32[1,2048]{1,0:T(1,128)S(1)} collective-permute-done((f32[1,2048]{1,0:T(1,128)S(1)}, f32[1,2048]{1,0:T(1,128)S(1)}, u32[]{:S(2)}, u32[]{:S(2)}) %collective-permute-start) | collective-permute-done | bytes 8224 | tf_op jit(solution)/shard_map/ppermute | solution.py:152
  7.2 1.4 %collective-permute-done.1.refs_2_ = f32[1,2048]{1,0:T(1,128)S(1)} collective-permute-done((f32[1,2048]{1,0:T(1,128)S(1)}, f32[1,2048]{1,0:T(1,128)S(1)}, u32[]{:S(2)}, u32[]{:S(2)}) %collective-permute-start.1) | collective-permute-done | bytes 8224 | tf_op jit(solution)/shard_map/ppermute | solution.py:152
  8.7 0.0 collective-permute-done.2.refs_3_
  8.7 0.0 copy-done
  8.7 0.0 copy-done.1
  8.7 0.0 copy-done.2
  8.7 0.0 copy-done.3
  8.7 0.0 copy-done.4
  8.7 0.6 %send_far.1 = (f32[32,512]{1,0:T(8,128)S(1)}, f32[32,512]{1,0:T(8,128)S(1)}, bf16[128,2048]{1,0:T(8,128)(2,1)S(1)}) custom-call(f32[16]{0:T(128)S(1)} %copy-done.4, f32[1,2048]{1,0:T(1,128)S(1)} %get-tuple-element.20.refs_0_, f32[1,2048]{1,0:T(1,128)S(1)} %collective-permute-done.refs_1_, f32[1,2048]{1,0:T(1,128)S(1)} %collective-permute-done.1.refs_2_, ...), custom_call_target="tpu_custom_call" | custom-call | flops 134217728 | bytes 524288 | tf_op jit(solution)/shard_map/send_far/pallas_call | solution.py:177
  9.3 1.6 %collective-permute-start.5 = (f32[32,512]{1,0:T(8,128)S(1)}, f32[32,512]{1,0:T(8,128)S(1)}, u32[]{:S(2)}, u32[]{:S(2)}) collective-permute-start(f32[32,512]{1,0:T(8,128)S(1)} %get-tuple-element.26), channel_id=1, source_target_pairs={{0,4},{1,5},{2,6},{3,7},{4,0},{5,1},{6,2},{7,3},{8,12},{9,13},{10,... | collective-permute-start | bytes 196616 | tf_op jit(solution)/shard_map/ppermute | solution.py:152
  10.9 0.5 %collective-permute-start.3 = (f32[32,512]{1,0:T(8,128)S(1)}, f32[32,512]{1,0:T(8,128)S(1)}, u32[]{:S(2)}, u32[]{:S(2)}) collective-permute-start(f32[32,512]{1,0:T(8,128)S(1)} %get-tuple-element.24), channel_id=1, source_target_pairs={{0,4},{1,5},{2,6},{3,7},{4,0},{5,1},{6,2},{7,3},{8,12},{9,13},{10,... | collective-permute-start | bytes 196616 | tf_op jit(solution)/shard_map/ppermute | solution.py:152
  11.4 0.8 %rest.1 = (f32[32,512]{1,0:T(8,128)S(1)}, f32[32,512]{1,0:T(8,128)S(1)}, f32[32,512]{1,0:T(8,128)S(1)}, f32[32,512]{1,0:T(8,128)S(1)}, f32[32,512]{1,0:T(8,128)S(1)}, /*index=5*/f32[32,512]{1,0:T(8,128)S(1)}) custom-call(bf16[128,2048]{1,0:T(8,128)(2,1)S(1)} %get-tuple-element.22.picks, bf16[2048,1024]{1,0:T(8,128)(2,1)S(1)} %get-tuple-element.21.refs_8_.held), custom_call_target="tpu_custom_call" | custom-call | flops 402653184 | bytes 1572864 | tf_op jit(solution)/shard_map/rest/pallas_call | solution.py:177
  12.3 1.6 %collective-permute-start.7 = (f32[32,512]{1,0:T(8,128)S(1)}, f32[32,512]{1,0:T(8,128)S(1)}, u32[]{:S(2)}, u32[]{:S(2)}) collective-permute-start(f32[32,512]{1,0:T(8,128)S(1)} %get-tuple-element.28), channel_id=1, source_target_pairs={{0,4},{1,5},{2,6},{3,7},{4,0},{5,1},{6,2},{7,3},{8,12},{9,13},{10,... | collective-permute-start | bytes 196616 | tf_op jit(solution)/shard_map/ppermute | solution.py:152
  13.8 0.5 %collective-permute-start.9 = (f32[32,512]{1,0:T(8,128)S(1)}, f32[32,512]{1,0:T(8,128)S(1)}, u32[]{:S(2)}, u32[]{:S(2)}) collective-permute-start(f32[32,512]{1,0:T(8,128)S(1)} %get-tuple-element.30), channel_id=1, source_target_pairs={{0,4},{1,5},{2,6},{3,7},{4,0},{5,1},{6,2},{7,3},{8,12},{9,13},{10,... | collective-permute-start | bytes 196616 | tf_op jit(solution)/shard_map/ppermute | solution.py:152
  14.3 0.0 collective-permute-done.5
  14.4 3.7 %collective-permute-start.6 = (f32[32,512]{1,0:T(8,128)S(1)}, f32[32,512]{1,0:T(8,128)S(1)}, u32[]{:S(2)}, u32[]{:S(2)}) collective-permute-start(f32[32,512]{1,0:T(8,128)S(1)} %add.23), channel_id=1, source_target_pairs={{0,24},{1,25},{2,26},{3,27},{4,28},{5,29},{6,30},{7,31},{8,16},{9,... | collective-permute-start | bytes 196616 | tf_op jit(solution)/shard_map/ppermute | solution.py:152
  18.0 0.0 collective-permute-done.3
  18.1 0.6 %collective-permute-start.4 = (f32[32,512]{1,0:T(8,128)S(1)}, f32[32,512]{1,0:T(8,128)S(1)}, u32[]{:S(2)}, u32[]{:S(2)}) collective-permute-start(f32[32,512]{1,0:T(8,128)S(1)} %add.22), channel_id=1, source_target_pairs={{0,16},{1,17},{2,18},{3,19},{4,20},{5,21},{6,22},{7,23},{8,24},{9,... | collective-permute-start | bytes 196616 | tf_op jit(solution)/shard_map/ppermute | solution.py:152
  18.7 0.0 collective-permute-done.7
  18.7 1.6 %collective-permute-start.8 = (f32[32,512]{1,0:T(8,128)S(1)}, f32[32,512]{1,0:T(8,128)S(1)}, u32[]{:S(2)}, u32[]{:S(2)}) collective-permute-start(f32[32,512]{1,0:T(8,128)S(1)} %add.25), channel_id=1, source_target_pairs={{0,8},{1,9},{2,10},{3,11},{4,12},{5,13},{6,14},{7,15},{8,0},{9,1},... | collective-permute-start | bytes 196616 | tf_op jit(solution)/shard_map/ppermute | solution.py:152
  20.3 0.3 collective-permute-done.6
  20.6 2.8 %collective-permute-done.4 = f32[32,512]{1,0:T(8,128)S(1)} collective-permute-done((f32[32,512]{1,0:T(8,128)S(1)}, f32[32,512]{1,0:T(8,128)S(1)}, u32[]{:S(2)}, u32[]{:S(2)}) %collective-permute-start.4) | collective-permute-done | bytes 65568 | tf_op jit(solution)/shard_map/ppermute | solution.py:152
  23.4 0.0 collective-permute-done.9
  23.4 0.3 collective-permute-done.8
  23.7 1.7 %collective-permute-start.10 = (f32[32,512]{1,0:T(8,128)S(1)}, f32[32,512]{1,0:T(8,128)S(1)}, u32[]{:S(2)}, u32[]{:S(2)}) collective-permute-start(f32[32,512]{1,0:T(8,128)S(1)} %add_add_fusion), channel_id=1, source_target_pairs={{0,16},{1,17},{2,18},{3,19},{4,20},{5,21},{6,22},{7,23},{8,0},{9,1... | collective-permute-start | bytes 196616 | tf_op jit(solution)/shard_map/ppermute | solution.py:232
  25.5 0.3 collective-permute-start.12
  25.8 2.1 %collective-permute-start.14 = (f32[32,512]{1,0:T(8,128)S(1)}, f32[32,512]{1,0:T(8,128)S(1)}, u32[]{:S(2)}, u32[]{:S(2)}) collective-permute-start(f32[32,512]{1,0:T(8,128)S(1)} %add_add_fusion), channel_id=1, source_target_pairs={{0,24},{1,25},{2,26},{3,27},{4,28},{5,29},{6,30},{7,31},{8,16},{9,... | collective-permute-start | bytes 196616 | tf_op jit(solution)/shard_map/ppermute | solution.py:232
  27.9 0.1 collective-permute-done.10
  28.1 1.1 %collective-permute-start.11 = (f32[64,512]{1,0:T(8,128)S(1)}, f32[64,512]{1,0:T(8,128)S(1)}, u32[]{:S(2)}, u32[]{:S(2)}) collective-permute-start(f32[64,512]{1,0:T(8,128)S(1)} %pad_maximum_fusion.1.refs_3_), channel_id=1, source_target_pairs={{0,2},{1,0},{2,3},{3,1},{4,6},{5,4},{6,7},{7,5},{8,9},{9,11},{10,8... | collective-permute-start | bytes 393224 | tf_op jit(solution)/shard_map/ppermute | solution.py:262
  29.1 1.5 %collective-permute-start.16 = (f32[64,512]{1,0:T(8,128)S(1)}, f32[64,512]{1,0:T(8,128)S(1)}, u32[]{:S(2)}, u32[]{:S(2)}) collective-permute-start(f32[64,512]{1,0:T(8,128)S(1)} %pad_maximum_fusion.1.refs_3_), channel_id=1, source_target_pairs={{0,4},{1,5},{2,6},{3,7},{4,0},{5,1},{6,2},{7,3},{8,12},{9,13},{10,... | collective-permute-start | bytes 393224 | tf_op jit(solution)/shard_map/ppermute | solution.py:152
  30.6 0.0 collective-permute-done.12
  30.7 0.6 %collective-permute-start.13 = (f32[32,512]{1,0:T(8,128)S(1)}, f32[32,512]{1,0:T(8,128)S(1)}, u32[]{:S(2)}, u32[]{:S(2)}) collective-permute-start(f32[32,512]{1,0:T(8,128)S(1)} %collective-permute-done.12), channel_id=1, source_target_pairs={{0,2},{1,0},{2,3},{3,1},{4,6},{5,4},{6,7},{7,5},{8,9},{9,11},{10,8... | collective-permute-start | bytes 196616 | tf_op jit(solution)/shard_map/ppermute | solution.py:262
  31.3 0.7 %collective-permute-done.14 = f32[32,512]{1,0:T(8,128)S(1)} collective-permute-done((f32[32,512]{1,0:T(8,128)S(1)}, f32[32,512]{1,0:T(8,128)S(1)}, u32[]{:S(2)}, u32[]{:S(2)}) %collective-permute-start.14) | collective-permute-done | bytes 65568 | tf_op jit(solution)/shard_map/ppermute | solution.py:232
  32.0 0.5 %collective-permute-start.15 = (f32[32,512]{1,0:T(8,128)S(1)}, f32[32,512]{1,0:T(8,128)S(1)}, u32[]{:S(2)}, u32[]{:S(2)}) collective-permute-start(f32[32,512]{1,0:T(8,128)S(1)} %collective-permute-done.14), channel_id=1, source_target_pairs={{0,2},{1,0},{2,3},{3,1},{4,6},{5,4},{6,7},{7,5},{8,9},{9,11},{10,8... | collective-permute-start | bytes 196616 | tf_op jit(solution)/shard_map/ppermute | solution.py:262
  32.5 1.4 %collective-permute-start.20 = (f32[64,512]{1,0:T(8,128)S(1)}, f32[64,512]{1,0:T(8,128)S(1)}, u32[]{:S(2)}, u32[]{:S(2)}) collective-permute-start(f32[64,512]{1,0:T(8,128)S(1)} %constant_dynamic-update-slice_fusion.refs_4_), channel_id=1, source_target_pairs={{0,4},{1,5},{2,6},{3,7},{4,0},{5,1},{6,2},{7,3},{8,12},{9,13},{10,... | collective-permute-start | bytes 393224 | tf_op jit(solution)/shard_map/ppermute | solution.py:152
  33.9 0.0 collective-permute-done.13
  33.9 0.5 %collective-permute-done.15 = f32[32,512]{1,0:T(8,128)S(1)} collective-permute-done((f32[32,512]{1,0:T(8,128)S(1)}, f32[32,512]{1,0:T(8,128)S(1)}, u32[]{:S(2)}, u32[]{:S(2)}) %collective-permute-start.15) | collective-permute-done | bytes 65568 | tf_op jit(solution)/shard_map/ppermute | solution.py:262
  34.4 0.0 collective-permute-done.11
  34.5 0.0 collective-permute-done.16.refs_0_
  34.5 0.1 collective-permute-start.17
  34.6 0.5 %collective-permute-start.18 = (f32[48,512]{1,0:T(8,128)S(1)}, f32[48,512]{1,0:T(8,128)S(1)}, u32[]{:S(2)}, u32[]{:S(2)}) collective-permute-start(f32[48,512]{1,0:T(8,128)S(1)} %get-tuple-element.35), channel_id=1, source_target_pairs={{0,1},{1,0},{2,3},{3,2},{4,5},{5,4},{6,7},{7,6},{8,9},{9,8},{10,11... | collective-permute-start | bytes 294920 | tf_op jit(solution)/shard_map/ppermute | solution.py:152
  35.1 0.1 collective-permute-start.19
  35.2 1.2 %collective-permute-done.19.refs_2_ = f32[32,512]{1,0:T(8,128)S(1)} collective-permute-done((f32[32,512]{1,0:T(8,128)S(1)}, f32[32,512]{1,0:T(8,128)S(1)}, u32[]{:S(2)}, u32[]{:S(2)}) %collective-permute-start.19) | collective-permute-done | bytes 65568 | tf_op jit(solution)/shard_map/ppermute | solution.py:152
  36.4 0.0 collective-permute-done.17.refs_0_
  36.4 0.0 collective-permute-done.18.refs_1_
  36.4 0.5 %meat_own.1 = (f32[1,512,512]{2,1,0:T(8,128)S(1)}, bf16[256,512]{1,0:T(8,128)(2,1)S(1)}) custom-call(f32[128,512]{1,0:T(8,128)S(1)} %maximum_select_fusion.have, f32[48,512]{1,0:T(8,128)S(1)} %collective-permute-done.17.refs_0_, f32[48,512]{1,0:T(8,128)S(1)} %collective-permute-done.18.refs_1_, f32[32,512]{1,0:T(8,128)S(1)} %collective-permute-done.19.refs_2_, ...), custom_call_target="tpu_custom_call" | custom-call | tf_op jit(solution)/shard_map/meat_own/pallas_call | solution.py:177
  36.9 1.0 %collective-permute-done.20.refs_1_ = f32[64,512]{1,0:T(8,128)S(1)} collective-permute-done((f32[64,512]{1,0:T(8,128)S(1)}, f32[64,512]{1,0:T(8,128)S(1)}, u32[]{:S(2)}, u32[]{:S(2)}) %collective-permute-start.20) | collective-permute-done | bytes 131104 | tf_op jit(solution)/shard_map/ppermute | solution.py:152
  37.9 1.5 %meat_other.1 = f32[512,1024]{1,0:T(8,128)} custom-call(f32[1,512,512]{2,1,0:T(8,128)S(1)} %get-tuple-element.32.first, bf16[256,512]{1,0:T(8,128)(2,1)S(1)} %get-tuple-element.33.left, f32[64,512]{1,0:T(8,128)S(1)} %collective-permute-done.16.refs_0_, f32[64,512]{1,0:T(8,128)S(1)} %collective-permute-done.20.refs_1_), custom_call_target="tpu_custom_call" | custom-call | flops 201326592 | bytes 2097152 | tf_op jit(solution)/shard_map/meat_other/pallas_call | solution.py:278
  (12 shorter events, 0.2 us)
Async XLA Ops:
  0.0 8.7 %copy-start = (f32[2048]{0:T(1024)S(1)}, f32[2048]{0:T(1024)}, u32[]{:S(2)}) copy-start(f32[2048]{0:T(1024)} %param.9) | copy-start | bytes 24580
  0.0 8.7 %copy-start.1 = (f32[2048]{0:T(1024)S(1)}, f32[2048]{0:T(1024)}, u32[]{:S(2)}) copy-start(f32[2048]{0:T(1024)} %param.10) | copy-start | bytes 24580
  0.0 8.7 %copy-start.2 = (s32[2048]{0:T(1024)S(1)}, s32[2048]{0:T(1024)}, u32[]{:S(2)}) copy-start(s32[2048]{0:T(1024)} %param.11) | copy-start | bytes 24580
  0.0 8.7 %copy-start.3 = (s32[2048]{0:T(1024)S(1)}, s32[2048]{0:T(1024)}, u32[]{:S(2)}) copy-start(s32[2048]{0:T(1024)} %param.12) | copy-start | bytes 24580
  0.0 8.7 %copy-start.4 = (f32[16]{0:T(128)S(1)}, f32[16]{0:T(128)}, u32[]{:S(2)}) copy-start(f32[16]{0:T(128)} %effect.1) | copy-start | bytes 196
  2.6 4.6 %collective-permute-start = (f32[1,2048]{1,0:T(1,128)S(1)}, f32[1,2048]{1,0:T(1,128)S(1)}, u32[]{:S(2)}, u32[]{:S(2)}) collective-permute-start(f32[1,2048]{1,0:T(1,128)S(1)} %get-tuple-element.20.refs_0_), channel_id=1, source_target_pairs={{0,2},{1,3},{2,0},{3,1},{4,6},{5,7},{6,4},{7,5},{8,10},{9,11},{10,... | collective-permute-start | bytes 24584 | tf_op jit(solution)/shard_map/ppermute | solution.py:152
  5.6 3.1 %collective-permute-start.1 = (f32[1,2048]{1,0:T(1,128)S(1)}, f32[1,2048]{1,0:T(1,128)S(1)}, u32[]{:S(2)}, u32[]{:S(2)}) collective-permute-start(f32[1,2048]{1,0:T(1,128)S(1)} %get-tuple-element.20.refs_0_), channel_id=1, source_target_pairs={{0,3},{1,2},{2,1},{3,0},{4,7},{5,6},{6,5},{7,4},{8,11},{9,10},{10,... | collective-permute-start | bytes 24584 | tf_op jit(solution)/shard_map/ppermute | solution.py:152
  5.6 3.1 %collective-permute-start.2 = (f32[1,2048]{1,0:T(1,128)S(1)}, f32[1,2048]{1,0:T(1,128)S(1)}, u32[]{:S(2)}, u32[]{:S(2)}) collective-permute-start(f32[1,2048]{1,0:T(1,128)S(1)} %get-tuple-element.20.refs_0_), channel_id=1, source_target_pairs={{0,1},{1,0},{2,3},{3,2},{4,5},{5,4},{6,7},{7,6},{8,9},{9,8},{10,11... | collective-permute-start | bytes 24584 | tf_op jit(solution)/shard_map/ppermute | solution.py:152
  9.3 5.0 %collective-permute-start.5 = (f32[32,512]{1,0:T(8,128)S(1)}, f32[32,512]{1,0:T(8,128)S(1)}, u32[]{:S(2)}, u32[]{:S(2)}) collective-permute-start(f32[32,512]{1,0:T(8,128)S(1)} %get-tuple-element.26), channel_id=1, source_target_pairs={{0,4},{1,5},{2,6},{3,7},{4,0},{5,1},{6,2},{7,3},{8,12},{9,13},{10,... | collective-permute-start | bytes 196616 | tf_op jit(solution)/shard_map/ppermute | solution.py:152
  10.9 7.1 %collective-permute-start.3 = (f32[32,512]{1,0:T(8,128)S(1)}, f32[32,512]{1,0:T(8,128)S(1)}, u32[]{:S(2)}, u32[]{:S(2)}) collective-permute-start(f32[32,512]{1,0:T(8,128)S(1)} %get-tuple-element.24), channel_id=1, source_target_pairs={{0,4},{1,5},{2,6},{3,7},{4,0},{5,1},{6,2},{7,3},{8,12},{9,13},{10,... | collective-permute-start | bytes 196616 | tf_op jit(solution)/shard_map/ppermute | solution.py:152
  12.3 6.4 %collective-permute-start.7 = (f32[32,512]{1,0:T(8,128)S(1)}, f32[32,512]{1,0:T(8,128)S(1)}, u32[]{:S(2)}, u32[]{:S(2)}) collective-permute-start(f32[32,512]{1,0:T(8,128)S(1)} %get-tuple-element.28), channel_id=1, source_target_pairs={{0,4},{1,5},{2,6},{3,7},{4,0},{5,1},{6,2},{7,3},{8,12},{9,13},{10,... | collective-permute-start | bytes 196616 | tf_op jit(solution)/shard_map/ppermute | solution.py:152
  13.8 9.6 %collective-permute-start.9 = (f32[32,512]{1,0:T(8,128)S(1)}, f32[32,512]{1,0:T(8,128)S(1)}, u32[]{:S(2)}, u32[]{:S(2)}) collective-permute-start(f32[32,512]{1,0:T(8,128)S(1)} %get-tuple-element.30), channel_id=1, source_target_pairs={{0,4},{1,5},{2,6},{3,7},{4,0},{5,1},{6,2},{7,3},{8,12},{9,13},{10,... | collective-permute-start | bytes 196616 | tf_op jit(solution)/shard_map/ppermute | solution.py:152
  14.4 6.2 %collective-permute-start.6 = (f32[32,512]{1,0:T(8,128)S(1)}, f32[32,512]{1,0:T(8,128)S(1)}, u32[]{:S(2)}, u32[]{:S(2)}) collective-permute-start(f32[32,512]{1,0:T(8,128)S(1)} %add.23), channel_id=1, source_target_pairs={{0,24},{1,25},{2,26},{3,27},{4,28},{5,29},{6,30},{7,31},{8,16},{9,... | collective-permute-start | bytes 196616 | tf_op jit(solution)/shard_map/ppermute | solution.py:152
  18.1 5.3 %collective-permute-start.4 = (f32[32,512]{1,0:T(8,128)S(1)}, f32[32,512]{1,0:T(8,128)S(1)}, u32[]{:S(2)}, u32[]{:S(2)}) collective-permute-start(f32[32,512]{1,0:T(8,128)S(1)} %add.22), channel_id=1, source_target_pairs={{0,16},{1,17},{2,18},{3,19},{4,20},{5,21},{6,22},{7,23},{8,24},{9,... | collective-permute-start | bytes 196616 | tf_op jit(solution)/shard_map/ppermute | solution.py:152
  18.7 5.0 %collective-permute-start.8 = (f32[32,512]{1,0:T(8,128)S(1)}, f32[32,512]{1,0:T(8,128)S(1)}, u32[]{:S(2)}, u32[]{:S(2)}) collective-permute-start(f32[32,512]{1,0:T(8,128)S(1)} %add.25), channel_id=1, source_target_pairs={{0,8},{1,9},{2,10},{3,11},{4,12},{5,13},{6,14},{7,15},{8,0},{9,1},... | collective-permute-start | bytes 196616 | tf_op jit(solution)/shard_map/ppermute | solution.py:152
  23.7 4.3 %collective-permute-start.10 = (f32[32,512]{1,0:T(8,128)S(1)}, f32[32,512]{1,0:T(8,128)S(1)}, u32[]{:S(2)}, u32[]{:S(2)}) collective-permute-start(f32[32,512]{1,0:T(8,128)S(1)} %add_add_fusion), channel_id=1, source_target_pairs={{0,16},{1,17},{2,18},{3,19},{4,20},{5,21},{6,22},{7,23},{8,0},{9,1... | collective-permute-start | bytes 196616 | tf_op jit(solution)/shard_map/ppermute | solution.py:232
  25.5 5.2 %collective-permute-start.12 = (f32[32,512]{1,0:T(8,128)S(1)}, f32[32,512]{1,0:T(8,128)S(1)}, u32[]{:S(2)}, u32[]{:S(2)}) collective-permute-start(f32[32,512]{1,0:T(8,128)S(1)} %add_add_fusion), channel_id=1, source_target_pairs={{0,8},{1,9},{2,10},{3,11},{4,12},{5,13},{6,14},{7,15},{8,24},{9,25... | collective-permute-start | bytes 196616 | tf_op jit(solution)/shard_map/ppermute | solution.py:232
  25.8 6.2 %collective-permute-start.14 = (f32[32,512]{1,0:T(8,128)S(1)}, f32[32,512]{1,0:T(8,128)S(1)}, u32[]{:S(2)}, u32[]{:S(2)}) collective-permute-start(f32[32,512]{1,0:T(8,128)S(1)} %add_add_fusion), channel_id=1, source_target_pairs={{0,24},{1,25},{2,26},{3,27},{4,28},{5,29},{6,30},{7,31},{8,16},{9,... | collective-permute-start | bytes 196616 | tf_op jit(solution)/shard_map/ppermute | solution.py:232
  28.1 6.4 %collective-permute-start.11 = (f32[64,512]{1,0:T(8,128)S(1)}, f32[64,512]{1,0:T(8,128)S(1)}, u32[]{:S(2)}, u32[]{:S(2)}) collective-permute-start(f32[64,512]{1,0:T(8,128)S(1)} %pad_maximum_fusion.1.refs_3_), channel_id=1, source_target_pairs={{0,2},{1,0},{2,3},{3,1},{4,6},{5,4},{6,7},{7,5},{8,9},{9,11},{10,8... | collective-permute-start | bytes 393224 | tf_op jit(solution)/shard_map/ppermute | solution.py:262
  29.1 5.3 %collective-permute-start.16 = (f32[64,512]{1,0:T(8,128)S(1)}, f32[64,512]{1,0:T(8,128)S(1)}, u32[]{:S(2)}, u32[]{:S(2)}) collective-permute-start(f32[64,512]{1,0:T(8,128)S(1)} %pad_maximum_fusion.1.refs_3_), channel_id=1, source_target_pairs={{0,4},{1,5},{2,6},{3,7},{4,0},{5,1},{6,2},{7,3},{8,12},{9,13},{10,... | collective-permute-start | bytes 393224 | tf_op jit(solution)/shard_map/ppermute | solution.py:152
  30.7 3.3 %collective-permute-start.13 = (f32[32,512]{1,0:T(8,128)S(1)}, f32[32,512]{1,0:T(8,128)S(1)}, u32[]{:S(2)}, u32[]{:S(2)}) collective-permute-start(f32[32,512]{1,0:T(8,128)S(1)} %collective-permute-done.12), channel_id=1, source_target_pairs={{0,2},{1,0},{2,3},{3,1},{4,6},{5,4},{6,7},{7,5},{8,9},{9,11},{10,8... | collective-permute-start | bytes 196616 | tf_op jit(solution)/shard_map/ppermute | solution.py:262
  32.0 2.4 %collective-permute-start.15 = (f32[32,512]{1,0:T(8,128)S(1)}, f32[32,512]{1,0:T(8,128)S(1)}, u32[]{:S(2)}, u32[]{:S(2)}) collective-permute-start(f32[32,512]{1,0:T(8,128)S(1)} %collective-permute-done.14), channel_id=1, source_target_pairs={{0,2},{1,0},{2,3},{3,1},{4,6},{5,4},{6,7},{7,5},{8,9},{9,11},{10,8... | collective-permute-start | bytes 196616 | tf_op jit(solution)/shard_map/ppermute | solution.py:262
  32.5 5.4 %collective-permute-start.20 = (f32[64,512]{1,0:T(8,128)S(1)}, f32[64,512]{1,0:T(8,128)S(1)}, u32[]{:S(2)}, u32[]{:S(2)}) collective-permute-start(f32[64,512]{1,0:T(8,128)S(1)} %constant_dynamic-update-slice_fusion.refs_4_), channel_id=1, source_target_pairs={{0,4},{1,5},{2,6},{3,7},{4,0},{5,1},{6,2},{7,3},{8,12},{9,13},{10,... | collective-permute-start | bytes 393224 | tf_op jit(solution)/shard_map/ppermute | solution.py:152
  34.5 1.8 %collective-permute-start.17 = (f32[48,512]{1,0:T(8,128)S(1)}, f32[48,512]{1,0:T(8,128)S(1)}, u32[]{:S(2)}, u32[]{:S(2)}) collective-permute-start(f32[48,512]{1,0:T(8,128)S(1)} %get-tuple-element.36), channel_id=1, source_target_pairs={{0,1},{1,0},{2,3},{3,2},{4,5},{5,4},{6,7},{7,6},{8,9},{9,8},{10,11... | collective-permute-start | bytes 294920 | tf_op jit(solution)/shard_map/ppermute | solution.py:152
  34.6 1.8 %collective-permute-start.18 = (f32[48,512]{1,0:T(8,128)S(1)}, f32[48,512]{1,0:T(8,128)S(1)}, u32[]{:S(2)}, u32[]{:S(2)}) collective-permute-start(f32[48,512]{1,0:T(8,128)S(1)} %get-tuple-element.35), channel_id=1, source_target_pairs={{0,1},{1,0},{2,3},{3,2},{4,5},{5,4},{6,7},{7,6},{8,9},{9,8},{10,11... | collective-permute-start | bytes 294920 | tf_op jit(solution)/shard_map/ppermute | solution.py:152
  35.1 1.3 %collective-permute-start.19 = (f32[32,512]{1,0:T(8,128)S(1)}, f32[32,512]{1,0:T(8,128)S(1)}, u32[]{:S(2)}, u32[]{:S(2)}) collective-permute-start(f32[32,512]{1,0:T(8,128)S(1)} %slice.16), channel_id=1, source_target_pairs={{0,1},{1,0},{2,3},{3,2},{4,5},{5,4},{6,7},{7,6},{8,9},{9,8},{10,11... | collective-permute-start | bytes 196616 | tf_op jit(solution)/shard_map/ppermute | solution.py:152
